TPU v7x, 32 devices: a whole 2x2x4 slice. The times are simulated.
32 devices in a mesh: gx: 16 (over z, x, core), gy: 2 (over y).
Axes of the slice: x: 2, y: 2, z: 4, core: 2. Of those that a mesh axis runs over, the one named last changes fastest.
Arguments:
- part_cell: int32 [557056], P(('gx', 'gy')), may hold values from 0 to 16383
- part_offset: float32 [3, 557056], P(None, ('gx', 'gy')), may hold values from 0 to 1
- part_vort: float32 [3, 557056], P(None, ('gx', 'gy')), may hold values from -6 to 6
- moving: int32 [32, 3], P(('gx', 'gy')), may hold values from 0 to 17408, as said below
Outputs:
- velocity: float32 [3, 64, 64, 128], P(None, 'gx', 'gy')
- stretching: float32 [3, 64, 64, 128], P(None, 'gx', 'gy')
Inputs may be any that keep to these rules, and one draw needn't show every extreme that they name: Row r of moving belongs to the device at position r along gx+gy, with index a along gx. Its entries are p, the particles of that device's list bound for slab a - 1, q, those bound for slab a + 1, and l, the live length. The list holds the p particles for a - 1 in slots 0 to p - 1, then the q for a + 1, then the particles that stay, then unused slots from l on. p and q are at most 1024; some device has p = q = 1024 and l = 17408, and some device receives 1024 particles from each of its two neighbouring slabs.
All inputs are finite; a program needn't handle non-finite values.
Results may differ from a plain program's by a relative error of at most 0.0053.
Values sent between devices are 32-bit elements; how exact they have to be, the bound alone decides.
No kernel may reach another device: no remote copies, remote signals or barrier semaphores. Data moves between devices by JAX's collectives and lax.ppermute only.
A program may use at most 64 MiB of HBM per device.

v0:
```python
import jax
import jax.numpy as jnp
from jax import lax
from jax.sharding import PartitionSpec as P

CX = 4
CY = 32
NZ = 128
OUTER = 4
SWEEPS = 3


def padded(value, sides, width):
    for axis, dim in sides:
        devices, length = (lax.axis_size(axis), value.shape[dim])
        up = [(i, (i + 1) % devices) for i in range(devices)]
        down = [(j, i) for i, j in up]
        last = lax.slice_in_dim(value, length - width, length, axis=dim)
        leading = lax.slice_in_dim(value, 0, width, axis=dim)
        before = lax.ppermute(last, axis, up)
        after = lax.ppermute(leading, axis, down)
        value = jnp.concatenate([before, value, after], axis=dim)
    return value


def passed_along(block, axis, distance):
    devices = range(lax.axis_size(axis))
    route = [((i - distance) % len(devices), i) for i in devices]
    return lax.ppermute(block, axis, route)


def m4_weights(offset):
    remain = 1.0 - offset
    return (
        -0.5 * offset * remain * remain,
        1.0 - 2.5 * offset * offset + 1.5 * offset * offset * offset,
        1.0 - 2.5 * remain * remain + 1.5 * remain * remain * remain,
        -0.5 * offset * offset * remain,
    )


def jacobi_sweep(field, source):
    centre = field[..., 1:-1, 1:-1, :]
    summed = (
        field[..., :-2, 1:-1, :]
        + field[..., 2:, 1:-1, :]
        + field[..., 1:-1, :-2, :]
        + field[..., 1:-1, 2:, :]
    )
    summed = summed + jnp.roll(centre, 1, -1) + jnp.roll(centre, -1, -1) + source
    return field.at[..., 1:-1, 1:-1, :].set(summed / 6.0)


def slope_x(field):
    return (field[2:, 1:-1] - field[:-2, 1:-1]) * 0.5


def slope_y(field):
    return (field[1:-1, 2:] - field[1:-1, :-2]) * 0.5


def slope_z(field):
    centre = field[1:-1, 1:-1]
    return (jnp.roll(centre, -1, -1) - jnp.roll(centre, 1, -1)) * 0.5


def curl_of(potential):
    return jnp.stack(
        [
            slope_y(potential[2]) - slope_z(potential[1]),
            slope_z(potential[0]) - slope_x(potential[2]),
            slope_x(potential[1]) - slope_y(potential[0]),
        ]
    )


def stretch(omega, edged_velocity):
    return jnp.stack(
        [
            omega[0] * slope_x(edged_velocity[comp])
            + omega[1] * slope_y(edged_velocity[comp])
            + omega[2] * slope_z(edged_velocity[comp])
            for comp in range(3)
        ]
    )


def silence(listed, keep):
    return jnp.concatenate(
        [listed[:3], jnp.where(keep[None], listed[3:6], 0.0), listed[6:]], axis=0
    )


def fold_ghosts(extended, axis_dim, extent):
    centre = lax.slice_in_dim(extended, 4, extent + 4, axis=axis_dim)
    low_rim = lax.slice_in_dim(extended, 0, 2, axis=axis_dim)
    high_rim = lax.slice_in_dim(extended, extent + 6, extent + 8, axis=axis_dim)
    pad_low = [(0, 0)] * extended.ndim
    pad_high = [(0, 0)] * extended.ndim
    pad_low[axis_dim] = (0, extent - 2)
    pad_high[axis_dim] = (extent - 2, 0)
    return centre + jnp.pad(low_rim, pad_low) + jnp.pad(high_rim, pad_high)


def remesh(particles, block_rows):
    rounds = particles.shape[1] // block_rows
    stacked = particles.reshape(7, rounds, block_rows).transpose(1, 0, 2)
    span_x = jnp.arange(CX + 4, dtype=jnp.int32)
    span_y = jnp.arange(CY + 4, dtype=jnp.int32)
    span_z = jnp.arange(NZ, dtype=jnp.int32)

    def one_block(running, batch):
        cell_ids = batch[6].astype(jnp.int32)
        cell_x = cell_ids // (CY * NZ)
        cell_y = cell_ids // NZ % CY
        cell_z = cell_ids % NZ
        weight_x = m4_weights(batch[0])
        weight_y = m4_weights(batch[1])
        weight_z = m4_weights(batch[2])
        along_x = jnp.zeros((block_rows, CX + 4), jnp.float32)
        along_y = jnp.zeros((block_rows, CY + 4), jnp.float32)
        along_z = jnp.zeros((block_rows, NZ), jnp.float32)
        for tap in range(4):
            along_x = along_x + jnp.where(
                span_x[None] == (cell_x + 1 + tap)[:, None], weight_x[tap][:, None], 0.0
            )
            along_y = along_y + jnp.where(
                span_y[None] == (cell_y + 1 + tap)[:, None], weight_y[tap][:, None], 0.0
            )
            along_z = along_z + jnp.where(
                span_z[None] == ((cell_z + tap - 1) % NZ)[:, None], weight_z[tap][:, None], 0.0
            )
        plane_weight = (
            (along_x[:, :, None] * along_y[:, None, :])
            .reshape(block_rows, (CX + 4) * (CY + 4))
            .astype(jnp.bfloat16)
        )
        line_weight = (batch[3:6][:, :, None] * along_z[None]).astype(jnp.bfloat16)
        running = running + jnp.einsum(
            "pq,cpz->cqz", plane_weight, line_weight, preferred_element_type=jnp.float32
        )
        return (running, None)

    start_value = jnp.zeros((3, (CX + 4) * (CY + 4), NZ), jnp.float32)
    deposits = lax.scan(one_block, start_value, stacked)[0]
    return deposits.reshape(3, CX + 4, CY + 4, NZ)


def widen(field):
    return padded(field, (("gx", 1), ("gy", 2)), 2)


def per_device(part_cell, part_offset, part_vort, moving):
    slots = part_cell.shape[0]
    capacity = slots // 17
    to_prev = moving[0, 0]
    to_next = moving[0, 1]
    live_len = moving[0, 2]
    packed = jnp.concatenate([part_offset, part_vort, part_cell.astype(jnp.float32)[None]], axis=0)
    slot_ids = jnp.arange(slots, dtype=jnp.int32)
    room_ids = jnp.arange(capacity, dtype=jnp.int32)
    prev_list = silence(packed[:, :capacity], room_ids < to_prev)
    next_list = silence(lax.dynamic_slice_in_dim(packed, to_prev, capacity, 1), room_ids < to_next)
    staying = silence(packed, (slot_ids >= to_prev + to_next) & (slot_ids < live_len))
    from_prev = passed_along(next_list, "gx", 1)
    from_next = passed_along(prev_list, "gx", -1)
    particles = jnp.concatenate([staying, from_prev, from_next], axis=1)
    deposits = remesh(particles, min(capacity, 1024))
    extended = padded(deposits, (("gx", 1), ("gy", 2)), 2)
    omega = fold_ghosts(fold_ghosts(extended, 1, CX), 2, CY)
    source = widen(omega)[:, 1:-1, 1:-1]
    potential = jnp.zeros_like(omega)
    for outer_step in range(OUTER):
        if outer_step == 0:
            field = jnp.zeros((3, CX + 4, CY + 4, NZ), jnp.float32)
        else:
            field = widen(potential)
        for repeat in range(SWEEPS):
            field = jacobi_sweep(field, source)
        potential = field[:, 2:-2, 2:-2]
    edged = padded(potential, (("gx", 1), ("gy", 2)), 1)
    velocity = curl_of(edged)
    edged_velocity = padded(velocity, (("gx", 1), ("gy", 2)), 1)
    stretching = stretch(omega, edged_velocity)
    return (velocity, stretching)


def solution(mesh):
    return jax.shard_map(
        per_device,
        mesh=mesh,
        in_specs=(
            P(("gx", "gy")),
            P(None, ("gx", "gy")),
            P(None, ("gx", "gy")),
            P(("gx", "gy"), None),
        ),
        out_specs=(P(None, "gx", "gy", None), P(None, "gx", "gy", None)),
        check_vma=False,
    )
```

profile of v0, /device:TPU:0, one launch (start us, length us, event | category | flops | bytes accessed | tf_op | source)
XLA Modules:
  0.0 158.2 jit_solution(1691041750964243513)
XLA Ops:
  0.7 1.4 fusion.168
  7.7 5.0 %collective-permute-start.1 = (f32[7,1024]{1,0:T(8,128)S(1)}, f32[7,1024]{1,0:T(8,128)S(1)}, u32[]{:S(2)}, u32[]{:S(2)}) collective-permute-start(f32[7,1024]{1,0:T(8,128)S(1)} %pad_maximum_fusion.32), channel_id=1, source_target_pairs={{2,0},{4,2},{6,4},{8,6},{10,8},{12,10},{14,12},{16,14},{18,16},{20... | collective-permute-start | bytes 86024 | tf_op jit(solution)/shard_map/ppermute | solution.py:29
  15.0 47.3 %while.29 = (s32[]{:T(128)}, f32[3,288,128]{2,1,0:T(8,128)S(1)}, f32[19,7,1024]{2,1,0:T(8,128)S(1)}, s32[]{:T(128)}, s32[]{:T(128)}, /*index=5*/s32[]{}, s32[]{}, s32[]{}, s32[]{}) while((s32[]{:T(128)}, f32[3,288,128]{2,1,0:T(8,128)S(1)}, f32[19,7,1024]{2,1,0:T(8,128)S(1)}, s32[]{:T(128)}, s32[]{:T(128)}, ...), condition=%wide.region_1.2_spmd.clone.clone, body=%wide.region_0.1_spmd.clone.clone.sunk | while | flops 230187008 | bytes 4944055 | solution.py:145
  15.5 1.1 select_add_fusion.8
  18.0 1.1 select_add_fusion.8
  27.9 1.1 select_add_fusion.8
  30.4 1.1 select_add_fusion.8
  32.9 1.1 select_add_fusion.8
  35.4 1.1 select_add_fusion.8
  37.9 1.1 select_add_fusion.8
  40.4 1.1 select_add_fusion.8
  50.3 1.1 select_add_fusion.8
  52.8 1.1 select_add_fusion.8
  55.3 1.1 select_add_fusion.8
  57.8 1.1 select_add_fusion.8
  60.3 1.1 select_add_fusion.8
  62.4 4.4 %collective-permute-start.3 = (f32[3,2,36,128]{3,2,1,0:T(8,128)S(1)}, f32[3,2,36,128]{3,2,1,0:T(8,128)S(1)}, u32[]{:S(2)}, u32[]{:S(2)}) collective-permute-start(f32[3,2,36,128]{3,2,1,0:T(8,128)S(1)} %get-tuple-element.455), channel_id=1, source_target_pairs={{2,0},{4,2},{6,4},{8,6},{10,8},{12,10},{14,12},{16,14},{18,16},{20... | collective-permute-start | bytes 331784 | tf_op jit(solution)/shard_map/ppermute | solution.py:21
  66.9 2.6 %collective-permute-done.2 = f32[3,2,36,128]{3,2,1,0:T(8,128)S(1)} collective-permute-done((f32[3,2,36,128]{3,2,1,0:T(8,128)S(1)}, f32[3,2,36,128]{3,2,1,0:T(8,128)S(1)}, u32[]{:S(2)}, u32[]{:S(2)}) %collective-permute-start.2) | collective-permute-done | bytes 110624 | tf_op jit(solution)/shard_map/ppermute | solution.py:20
  69.6 2.0 %collective-permute-start.4 = (f32[3,12,2,128]{3,2,1,0:T(2,128)S(1)}, f32[3,12,2,128]{3,2,1,0:T(2,128)S(1)}, u32[]{:S(2)}, u32[]{:S(2)}) collective-permute-start(f32[3,12,2,128]{3,2,1,0:T(2,128)S(1)} %get-tuple-element.441), channel_id=1, source_target_pairs={{0,1},{1,0},{2,3},{3,2},{4,5},{5,4},{6,7},{7,6},{8,9},{9,8},{10,11... | collective-permute-start | bytes 110600 | tf_op jit(solution)/shard_map/ppermute | solution.py:20
  71.7 1.9 %collective-permute-done.4 = f32[3,12,2,128]{3,2,1,0:T(2,128)S(1)} collective-permute-done((f32[3,12,2,128]{3,2,1,0:T(2,128)S(1)}, f32[3,12,2,128]{3,2,1,0:T(2,128)S(1)}, u32[]{:S(2)}, u32[]{:S(2)}) %collective-permute-start.4) | collective-permute-done | bytes 36896 | tf_op jit(solution)/shard_map/ppermute | solution.py:20
  73.6 2.0 %collective-permute-done.5 = f32[3,12,2,128]{3,2,1,0:T(2,128)S(1)} collective-permute-done((f32[3,12,2,128]{3,2,1,0:T(2,128)S(1)}, f32[3,12,2,128]{3,2,1,0:T(2,128)S(1)}, u32[]{:S(2)}, u32[]{:S(2)}) %collective-permute-start.5) | collective-permute-done | bytes 36896 | tf_op jit(solution)/shard_map/ppermute | solution.py:21
  76.5 4.4 %collective-permute-start.7 = (f32[3,2,32,128]{3,2,1,0:T(8,128)S(1)}, f32[3,2,32,128]{3,2,1,0:T(8,128)S(1)}, u32[]{:S(2)}, u32[]{:S(2)}) collective-permute-start(f32[3,2,32,128]{3,2,1,0:T(8,128)S(1)} %get-tuple-element.518), channel_id=1, source_target_pairs={{2,0},{4,2},{6,4},{8,6},{10,8},{12,10},{14,12},{16,14},{18,16},{20... | collective-permute-start | bytes 294920 | tf_op jit(solution)/shard_map/ppermute | solution.py:21
  80.9 2.3 %collective-permute-done.6 = f32[3,2,32,128]{3,2,1,0:T(8,128)S(1)} collective-permute-done((f32[3,2,32,128]{3,2,1,0:T(8,128)S(1)}, f32[3,2,32,128]{3,2,1,0:T(8,128)S(1)}, u32[]{:S(2)}, u32[]{:S(2)}) %collective-permute-start.6) | collective-permute-done | bytes 98336 | tf_op jit(solution)/shard_map/ppermute | solution.py:20
  83.7 1.6 %collective-permute-start.9 = (f32[3,8,2,128]{3,2,1,0:T(2,128)S(1)}, f32[3,8,2,128]{3,2,1,0:T(2,128)S(1)}, u32[]{:S(2)}, u32[]{:S(2)}) collective-permute-start(f32[3,8,2,128]{3,2,1,0:T(2,128)S(1)} %get-tuple-element.464), channel_id=1, source_target_pairs={{1,0},{0,1},{3,2},{2,3},{5,4},{4,5},{7,6},{6,7},{9,8},{8,9},{11,10... | collective-permute-start | bytes 73736 | tf_op jit(solution)/shard_map/ppermute | solution.py:21
  85.4 1.8 %collective-permute-done.8 = f32[3,8,2,128]{3,2,1,0:T(2,128)S(1)} collective-permute-done((f32[3,8,2,128]{3,2,1,0:T(2,128)S(1)}, f32[3,8,2,128]{3,2,1,0:T(2,128)S(1)}, u32[]{:S(2)}, u32[]{:S(2)}) %collective-permute-start.8) | collective-permute-done | bytes 24608 | tf_op jit(solution)/shard_map/ppermute | solution.py:20
  89.4 4.4 %collective-permute-start.11 = (f32[3,2,32,128]{3,2,1,0:T(8,128)S(1)}, f32[3,2,32,128]{3,2,1,0:T(8,128)S(1)}, u32[]{:S(2)}, u32[]{:S(2)}) collective-permute-start(f32[3,2,32,128]{3,2,1,0:T(8,128)S(1)} %get-tuple-element.502), channel_id=1, source_target_pairs={{2,0},{4,2},{6,4},{8,6},{10,8},{12,10},{14,12},{16,14},{18,16},{20... | collective-permute-start | bytes 294920 | tf_op jit(solution)/shard_map/ppermute | solution.py:21
  93.9 2.3 %collective-permute-done.10 = f32[3,2,32,128]{3,2,1,0:T(8,128)S(1)} collective-permute-done((f32[3,2,32,128]{3,2,1,0:T(8,128)S(1)}, f32[3,2,32,128]{3,2,1,0:T(8,128)S(1)}, u32[]{:S(2)}, u32[]{:S(2)}) %collective-permute-start.10) | collective-permute-done | bytes 98336 | tf_op jit(solution)/shard_map/ppermute | solution.py:20
  96.2 1.7 %collective-permute-start.12 = (f32[3,8,2,128]{3,2,1,0:T(2,128)S(1)}, f32[3,8,2,128]{3,2,1,0:T(2,128)S(1)}, u32[]{:S(2)}, u32[]{:S(2)}) collective-permute-start(f32[3,8,2,128]{3,2,1,0:T(2,128)S(1)} %get-tuple-element.461), channel_id=1, source_target_pairs={{0,1},{1,0},{2,3},{3,2},{4,5},{5,4},{6,7},{7,6},{8,9},{9,8},{10,11... | collective-permute-start | bytes 73736 | tf_op jit(solution)/shard_map/ppermute | solution.py:20
  98.3 1.8 %collective-permute-done.12 = f32[3,8,2,128]{3,2,1,0:T(2,128)S(1)} collective-permute-done((f32[3,8,2,128]{3,2,1,0:T(2,128)S(1)}, f32[3,8,2,128]{3,2,1,0:T(2,128)S(1)}, u32[]{:S(2)}, u32[]{:S(2)}) %collective-permute-start.12) | collective-permute-done | bytes 24608 | tf_op jit(solution)/shard_map/ppermute | solution.py:20
  100.1 1.6 %collective-permute-done.13 = f32[3,8,2,128]{3,2,1,0:T(2,128)S(1)} collective-permute-done((f32[3,8,2,128]{3,2,1,0:T(2,128)S(1)}, f32[3,8,2,128]{3,2,1,0:T(2,128)S(1)}, u32[]{:S(2)}, u32[]{:S(2)}) %collective-permute-start.13) | collective-permute-done | bytes 24608 | tf_op jit(solution)/shard_map/ppermute | solution.py:21
  104.7 4.4 %collective-permute-start.15 = (f32[3,2,32,128]{3,2,1,0:T(8,128)S(1)}, f32[3,2,32,128]{3,2,1,0:T(8,128)S(1)}, u32[]{:S(2)}, u32[]{:S(2)}) collective-permute-start(f32[3,2,32,128]{3,2,1,0:T(8,128)S(1)} %get-tuple-element.492), channel_id=1, source_target_pairs={{2,0},{4,2},{6,4},{8,6},{10,8},{12,10},{14,12},{16,14},{18,16},{20... | collective-permute-start | bytes 294920 | tf_op jit(solution)/shard_map/ppermute | solution.py:21
  109.1 2.3 %collective-permute-done.14 = f32[3,2,32,128]{3,2,1,0:T(8,128)S(1)} collective-permute-done((f32[3,2,32,128]{3,2,1,0:T(8,128)S(1)}, f32[3,2,32,128]{3,2,1,0:T(8,128)S(1)}, u32[]{:S(2)}, u32[]{:S(2)}) %collective-permute-start.14) | collective-permute-done | bytes 98336 | tf_op jit(solution)/shard_map/ppermute | solution.py:20
  111.9 1.6 %collective-permute-start.17 = (f32[3,8,2,128]{3,2,1,0:T(2,128)S(1)}, f32[3,8,2,128]{3,2,1,0:T(2,128)S(1)}, u32[]{:S(2)}, u32[]{:S(2)}) collective-permute-start(f32[3,8,2,128]{3,2,1,0:T(2,128)S(1)} %get-tuple-element.460), channel_id=1, source_target_pairs={{1,0},{0,1},{3,2},{2,3},{5,4},{4,5},{7,6},{6,7},{9,8},{8,9},{11,10... | collective-permute-start | bytes 73736 | tf_op jit(solution)/shard_map/ppermute | solution.py:21
  113.5 1.8 %collective-permute-done.16 = f32[3,8,2,128]{3,2,1,0:T(2,128)S(1)} collective-permute-done((f32[3,8,2,128]{3,2,1,0:T(2,128)S(1)}, f32[3,8,2,128]{3,2,1,0:T(2,128)S(1)}, u32[]{:S(2)}, u32[]{:S(2)}) %collective-permute-start.16) | collective-permute-done | bytes 24608 | tf_op jit(solution)/shard_map/ppermute | solution.py:20
  118.7 4.4 %collective-permute-start.19 = (f32[3,2,32,128]{3,2,1,0:T(8,128)S(1)}, f32[3,2,32,128]{3,2,1,0:T(8,128)S(1)}, u32[]{:S(2)}, u32[]{:S(2)}) collective-permute-start(f32[3,2,32,128]{3,2,1,0:T(8,128)S(1)} %get-tuple-element.482), channel_id=1, source_target_pairs={{2,0},{4,2},{6,4},{8,6},{10,8},{12,10},{14,12},{16,14},{18,16},{20... | collective-permute-start | bytes 294920 | tf_op jit(solution)/shard_map/ppermute | solution.py:21
  123.1 2.3 %collective-permute-done.18 = f32[3,2,32,128]{3,2,1,0:T(8,128)S(1)} collective-permute-done((f32[3,2,32,128]{3,2,1,0:T(8,128)S(1)}, f32[3,2,32,128]{3,2,1,0:T(8,128)S(1)}, u32[]{:S(2)}, u32[]{:S(2)}) %collective-permute-start.18) | collective-permute-done | bytes 98336 | tf_op jit(solution)/shard_map/ppermute | solution.py:20
  125.4 1.7 %collective-permute-start.20 = (f32[3,8,2,128]{3,2,1,0:T(2,128)S(1)}, f32[3,8,2,128]{3,2,1,0:T(2,128)S(1)}, u32[]{:S(2)}, u32[]{:S(2)}) collective-permute-start(f32[3,8,2,128]{3,2,1,0:T(2,128)S(1)} %get-tuple-element.457), channel_id=1, source_target_pairs={{0,1},{1,0},{2,3},{3,2},{4,5},{5,4},{6,7},{7,6},{8,9},{9,8},{10,11... | collective-permute-start | bytes 73736 | tf_op jit(solution)/shard_map/ppermute | solution.py:20
  127.5 1.8 %collective-permute-done.20 = f32[3,8,2,128]{3,2,1,0:T(2,128)S(1)} collective-permute-done((f32[3,8,2,128]{3,2,1,0:T(2,128)S(1)}, f32[3,8,2,128]{3,2,1,0:T(2,128)S(1)}, u32[]{:S(2)}, u32[]{:S(2)}) %collective-permute-start.20) | collective-permute-done | bytes 24608 | tf_op jit(solution)/shard_map/ppermute | solution.py:20
  129.3 1.6 %collective-permute-done.21 = f32[3,8,2,128]{3,2,1,0:T(2,128)S(1)} collective-permute-done((f32[3,8,2,128]{3,2,1,0:T(2,128)S(1)}, f32[3,8,2,128]{3,2,1,0:T(2,128)S(1)}, u32[]{:S(2)}, u32[]{:S(2)}) %collective-permute-start.21) | collective-permute-done | bytes 24608 | tf_op jit(solution)/shard_map/ppermute | solution.py:21
  133.9 4.4 %collective-permute-start.23 = (f32[3,1,32,128]{3,2,1,0:T(8,128)S(1)}, f32[3,1,32,128]{3,2,1,0:T(8,128)S(1)}, u32[]{:S(2)}, u32[]{:S(2)}) collective-permute-start(f32[3,1,32,128]{3,2,1,0:T(8,128)S(1)} %get-tuple-element.472), channel_id=1, source_target_pairs={{2,0},{4,2},{6,4},{8,6},{10,8},{12,10},{14,12},{16,14},{18,16},{20... | collective-permute-start | bytes 147464 | tf_op jit(solution)/shard_map/ppermute | solution.py:21
  138.4 1.7 %collective-permute-done.22 = f32[3,1,32,128]{3,2,1,0:T(8,128)S(1)} collective-permute-done((f32[3,1,32,128]{3,2,1,0:T(8,128)S(1)}, f32[3,1,32,128]{3,2,1,0:T(8,128)S(1)}, u32[]{:S(2)}, u32[]{:S(2)}) %collective-permute-start.22) | collective-permute-done | bytes 49184 | tf_op jit(solution)/shard_map/ppermute | solution.py:20
  140.6 1.6 %collective-permute-start.25 = (f32[3,6,1,128]{3,2,1,0:T(1,128)S(1)}, f32[3,6,1,128]{3,2,1,0:T(1,128)S(1)}, u32[]{:S(2)}, u32[]{:S(2)}) collective-permute-start(f32[3,6,1,128]{3,2,1,0:T(1,128)S(1)} %get-tuple-element.514), channel_id=1, source_target_pairs={{1,0},{0,1},{3,2},{2,3},{5,4},{4,5},{7,6},{6,7},{9,8},{8,9},{11,10... | collective-permute-start | bytes 27656 | tf_op jit(solution)/shard_map/ppermute | solution.py:21
  142.2 1.6 %collective-permute-done.24 = f32[3,6,1,128]{3,2,1,0:T(1,128)S(1)} collective-permute-done((f32[3,6,1,128]{3,2,1,0:T(1,128)S(1)}, f32[3,6,1,128]{3,2,1,0:T(1,128)S(1)}, u32[]{:S(2)}, u32[]{:S(2)}) %collective-permute-start.24) | collective-permute-done | bytes 9248 | tf_op jit(solution)/shard_map/ppermute | solution.py:20
  145.0 4.4 %collective-permute-start.27 = (f32[3,1,32,128]{3,2,1,0:T(8,128)S(1)}, f32[3,1,32,128]{3,2,1,0:T(8,128)S(1)}, u32[]{:S(2)}, u32[]{:S(2)}) collective-permute-start(f32[3,1,32,128]{3,2,1,0:T(8,128)S(1)} %get-tuple-element.516), channel_id=1, source_target_pairs={{2,0},{4,2},{6,4},{8,6},{10,8},{12,10},{14,12},{16,14},{18,16},{20... | collective-permute-start | bytes 147464 | tf_op jit(solution)/shard_map/ppermute | solution.py:21
  149.4 1.8 %collective-permute-done.26 = f32[3,1,32,128]{3,2,1,0:T(8,128)S(1)} collective-permute-done((f32[3,1,32,128]{3,2,1,0:T(8,128)S(1)}, f32[3,1,32,128]{3,2,1,0:T(8,128)S(1)}, u32[]{:S(2)}, u32[]{:S(2)}) %collective-permute-start.26) | collective-permute-done | bytes 49184 | tf_op jit(solution)/shard_map/ppermute | solution.py:20
  151.2 1.7 %collective-permute-start.28 = (f32[3,6,1,128]{3,2,1,0:T(1,128)S(1)}, f32[3,6,1,128]{3,2,1,0:T(1,128)S(1)}, u32[]{:S(2)}, u32[]{:S(2)}) collective-permute-start(f32[3,6,1,128]{3,2,1,0:T(1,128)S(1)} %get-tuple-element.511), channel_id=1, source_target_pairs={{0,1},{1,0},{2,3},{3,2},{4,5},{5,4},{6,7},{7,6},{8,9},{9,8},{10,11... | collective-permute-start | bytes 27656 | tf_op jit(solution)/shard_map/ppermute | solution.py:20
  153.3 1.6 %collective-permute-done.28 = f32[3,6,1,128]{3,2,1,0:T(1,128)S(1)} collective-permute-done((f32[3,6,1,128]{3,2,1,0:T(1,128)S(1)}, f32[3,6,1,128]{3,2,1,0:T(1,128)S(1)}, u32[]{:S(2)}, u32[]{:S(2)}) %collective-permute-start.28) | collective-permute-done | bytes 9248 | tf_op jit(solution)/shard_map/ppermute | solution.py:20
  154.9 1.6 %collective-permute-done.29 = f32[3,6,1,128]{3,2,1,0:T(1,128)S(1)} collective-permute-done((f32[3,6,1,128]{3,2,1,0:T(1,128)S(1)}, f32[3,6,1,128]{3,2,1,0:T(1,128)S(1)}, u32[]{:S(2)}, u32[]{:S(2)}) %collective-permute-start.29) | collective-permute-done | bytes 9248 | tf_op jit(solution)/shard_map/ppermute | solution.py:21
  (380 shorter events, 52.8 us)
Async XLA Ops:
  0.6 7.0 %copy-start.1 = (f32[3,17408]{1,0:T(4,128)S(1)}, f32[3,17408]{1,0:T(4,128)}, u32[]{:S(2)}) copy-start(f32[3,17408]{1,0:T(4,128)} %param.32) | copy-start | bytes 626692
  0.6 7.0 %slice-start = ((f32[3,17408]{1,0:T(4,128)}), f32[3,1024]{1,0:T(4,128)S(1)}, s32[]{:S(2)}) async-start(f32[3,17408]{1,0:T(4,128)} %param.31), calls=%async_computation | async-start | bytes 32768 | tf_op jit(solution)/shard_map/slice | solution.py:90
  5.5 9.3 %copy-start = (f32[3,17408]{1,0:T(4,128)S(1)}, f32[3,17408]{1,0:T(4,128)}, u32[]{:S(2)}) copy-start(f32[3,17408]{1,0:T(4,128)} %param.31) | copy-start | bytes 626692
  6.5 8.3 %collective-permute-start = (f32[7,1024]{1,0:T(8,128)S(1)}, f32[7,1024]{1,0:T(8,128)S(1)}, u32[]{:S(2)}, u32[]{:S(2)}) collective-permute-start(f32[7,1024]{1,0:T(8,128)S(1)} %pad_maximum_fusion.31), channel_id=1, source_target_pairs={{30,0},{0,2},{2,4},{4,6},{6,8},{8,10},{10,12},{12,14},{14,16},{16,... | collective-permute-start | bytes 86024 | tf_op jit(solution)/shard_map/ppermute | solution.py:29
  7.7 7.1 %collective-permute-start.1 = (f32[7,1024]{1,0:T(8,128)S(1)}, f32[7,1024]{1,0:T(8,128)S(1)}, u32[]{:S(2)}, u32[]{:S(2)}) collective-permute-start(f32[7,1024]{1,0:T(8,128)S(1)} %pad_maximum_fusion.32), channel_id=1, source_target_pairs={{2,0},{4,2},{6,4},{8,6},{10,8},{12,10},{14,12},{16,14},{18,16},{20... | collective-permute-start | bytes 86024 | tf_op jit(solution)/shard_map/ppermute | solution.py:29
  62.4 7.1 %collective-permute-start.2 = (f32[3,2,36,128]{3,2,1,0:T(8,128)S(1)}, f32[3,2,36,128]{3,2,1,0:T(8,128)S(1)}, u32[]{:S(2)}, u32[]{:S(2)}) collective-permute-start(f32[3,2,36,128]{3,2,1,0:T(8,128)S(1)} %get-tuple-element.456), channel_id=1, source_target_pairs={{0,2},{2,4},{4,6},{6,8},{8,10},{10,12},{12,14},{14,16},{16,18},{18... | collective-permute-start | bytes 331784 | tf_op jit(solution)/shard_map/ppermute | solution.py:20
  62.4 7.0 %collective-permute-start.3 = (f32[3,2,36,128]{3,2,1,0:T(8,128)S(1)}, f32[3,2,36,128]{3,2,1,0:T(8,128)S(1)}, u32[]{:S(2)}, u32[]{:S(2)}) collective-permute-start(f32[3,2,36,128]{3,2,1,0:T(8,128)S(1)} %get-tuple-element.455), channel_id=1, source_target_pairs={{2,0},{4,2},{6,4},{8,6},{10,8},{12,10},{14,12},{16,14},{18,16},{20... | collective-permute-start | bytes 331784 | tf_op jit(solution)/shard_map/ppermute | solution.py:21
  69.6 4.0 %collective-permute-start.4 = (f32[3,12,2,128]{3,2,1,0:T(2,128)S(1)}, f32[3,12,2,128]{3,2,1,0:T(2,128)S(1)}, u32[]{:S(2)}, u32[]{:S(2)}) collective-permute-start(f32[3,12,2,128]{3,2,1,0:T(2,128)S(1)} %get-tuple-element.441), channel_id=1, source_target_pairs={{0,1},{1,0},{2,3},{3,2},{4,5},{5,4},{6,7},{7,6},{8,9},{9,8},{10,11... | collective-permute-start | bytes 110600 | tf_op jit(solution)/shard_map/ppermute | solution.py:20
  71.6 4.1 %copy-start.3 = (pred[4]{0:T(512)(128)(4,1)S(1)}, pred[4]{0:T(512)(128)(4,1)}, u32[]{:S(2)}) copy-start(pred[4]{0:T(512)(128)(4,1)} %constant.533.clone.1) | copy-start | bytes 16
  71.6 4.0 %collective-permute-start.5 = (f32[3,12,2,128]{3,2,1,0:T(2,128)S(1)}, f32[3,12,2,128]{3,2,1,0:T(2,128)S(1)}, u32[]{:S(2)}, u32[]{:S(2)}) collective-permute-start(f32[3,12,2,128]{3,2,1,0:T(2,128)S(1)} %get-tuple-element.442), channel_id=1, source_target_pairs={{1,0},{0,1},{3,2},{2,3},{5,4},{4,5},{7,6},{6,7},{9,8},{8,9},{11,10... | collective-permute-start | bytes 110600 | tf_op jit(solution)/shard_map/ppermute | solution.py:21
  75.7 0.7 copy-start.4
  76.4 6.8 %collective-permute-start.6 = (f32[3,2,32,128]{3,2,1,0:T(8,128)S(1)}, f32[3,2,32,128]{3,2,1,0:T(8,128)S(1)}, u32[]{:S(2)}, u32[]{:S(2)}) collective-permute-start(f32[3,2,32,128]{3,2,1,0:T(8,128)S(1)} %get-tuple-element.517), channel_id=1, source_target_pairs={{0,2},{2,4},{4,6},{6,8},{8,10},{10,12},{12,14},{14,16},{16,18},{18... | collective-permute-start | bytes 294920 | tf_op jit(solution)/shard_map/ppermute | solution.py:20
  76.5 6.7 %collective-permute-start.7 = (f32[3,2,32,128]{3,2,1,0:T(8,128)S(1)}, f32[3,2,32,128]{3,2,1,0:T(8,128)S(1)}, u32[]{:S(2)}, u32[]{:S(2)}) collective-permute-start(f32[3,2,32,128]{3,2,1,0:T(8,128)S(1)} %get-tuple-element.518), channel_id=1, source_target_pairs={{2,0},{4,2},{6,4},{8,6},{10,8},{12,10},{14,12},{16,14},{18,16},{20... | collective-permute-start | bytes 294920 | tf_op jit(solution)/shard_map/ppermute | solution.py:21
  83.3 3.9 %collective-permute-start.8 = (f32[3,8,2,128]{3,2,1,0:T(2,128)S(1)}, f32[3,8,2,128]{3,2,1,0:T(2,128)S(1)}, u32[]{:S(2)}, u32[]{:S(2)}) collective-permute-start(f32[3,8,2,128]{3,2,1,0:T(2,128)S(1)} %get-tuple-element.463), channel_id=1, source_target_pairs={{0,1},{1,0},{2,3},{3,2},{4,5},{5,4},{6,7},{7,6},{8,9},{9,8},{10,11... | collective-permute-start | bytes 73736 | tf_op jit(solution)/shard_map/ppermute | solution.py:20
  83.7 3.8 %collective-permute-start.9 = (f32[3,8,2,128]{3,2,1,0:T(2,128)S(1)}, f32[3,8,2,128]{3,2,1,0:T(2,128)S(1)}, u32[]{:S(2)}, u32[]{:S(2)}) collective-permute-start(f32[3,8,2,128]{3,2,1,0:T(2,128)S(1)} %get-tuple-element.464), channel_id=1, source_target_pairs={{1,0},{0,1},{3,2},{2,3},{5,4},{4,5},{7,6},{6,7},{9,8},{8,9},{11,10... | collective-permute-start | bytes 73736 | tf_op jit(solution)/shard_map/ppermute | solution.py:21
  89.4 6.8 %collective-permute-start.10 = (f32[3,2,32,128]{3,2,1,0:T(8,128)S(1)}, f32[3,2,32,128]{3,2,1,0:T(8,128)S(1)}, u32[]{:S(2)}, u32[]{:S(2)}) collective-permute-start(f32[3,2,32,128]{3,2,1,0:T(8,128)S(1)} %get-tuple-element.501), channel_id=1, source_target_pairs={{0,2},{2,4},{4,6},{6,8},{8,10},{10,12},{12,14},{14,16},{16,18},{18... | collective-permute-start | bytes 294920 | tf_op jit(solution)/shard_map/ppermute | solution.py:20
  89.4 6.7 %collective-permute-start.11 = (f32[3,2,32,128]{3,2,1,0:T(8,128)S(1)}, f32[3,2,32,128]{3,2,1,0:T(8,128)S(1)}, u32[]{:S(2)}, u32[]{:S(2)}) collective-permute-start(f32[3,2,32,128]{3,2,1,0:T(8,128)S(1)} %get-tuple-element.502), channel_id=1, source_target_pairs={{2,0},{4,2},{6,4},{8,6},{10,8},{12,10},{14,12},{16,14},{18,16},{20... | collective-permute-start | bytes 294920 | tf_op jit(solution)/shard_map/ppermute | solution.py:21
  96.2 3.9 %collective-permute-start.12 = (f32[3,8,2,128]{3,2,1,0:T(2,128)S(1)}, f32[3,8,2,128]{3,2,1,0:T(2,128)S(1)}, u32[]{:S(2)}, u32[]{:S(2)}) collective-permute-start(f32[3,8,2,128]{3,2,1,0:T(2,128)S(1)} %get-tuple-element.461), channel_id=1, source_target_pairs={{0,1},{1,0},{2,3},{3,2},{4,5},{5,4},{6,7},{7,6},{8,9},{9,8},{10,11... | collective-permute-start | bytes 73736 | tf_op jit(solution)/shard_map/ppermute | solution.py:20
  97.9 3.8 %collective-permute-start.13 = (f32[3,8,2,128]{3,2,1,0:T(2,128)S(1)}, f32[3,8,2,128]{3,2,1,0:T(2,128)S(1)}, u32[]{:S(2)}, u32[]{:S(2)}) collective-permute-start(f32[3,8,2,128]{3,2,1,0:T(2,128)S(1)} %get-tuple-element.462), channel_id=1, source_target_pairs={{1,0},{0,1},{3,2},{2,3},{5,4},{4,5},{7,6},{6,7},{9,8},{8,9},{11,10... | collective-permute-start | bytes 73736 | tf_op jit(solution)/shard_map/ppermute | solution.py:21
  104.6 6.8 %collective-permute-start.14 = (f32[3,2,32,128]{3,2,1,0:T(8,128)S(1)}, f32[3,2,32,128]{3,2,1,0:T(8,128)S(1)}, u32[]{:S(2)}, u32[]{:S(2)}) collective-permute-start(f32[3,2,32,128]{3,2,1,0:T(8,128)S(1)} %get-tuple-element.491), channel_id=1, source_target_pairs={{0,2},{2,4},{4,6},{6,8},{8,10},{10,12},{12,14},{14,16},{16,18},{18... | collective-permute-start | bytes 294920 | tf_op jit(solution)/shard_map/ppermute | solution.py:20
  104.7 6.7 %collective-permute-start.15 = (f32[3,2,32,128]{3,2,1,0:T(8,128)S(1)}, f32[3,2,32,128]{3,2,1,0:T(8,128)S(1)}, u32[]{:S(2)}, u32[]{:S(2)}) collective-permute-start(f32[3,2,32,128]{3,2,1,0:T(8,128)S(1)} %get-tuple-element.492), channel_id=1, source_target_pairs={{2,0},{4,2},{6,4},{8,6},{10,8},{12,10},{14,12},{16,14},{18,16},{20... | collective-permute-start | bytes 294920 | tf_op jit(solution)/shard_map/ppermute | solution.py:21
  111.4 3.9 %collective-permute-start.16 = (f32[3,8,2,128]{3,2,1,0:T(2,128)S(1)}, f32[3,8,2,128]{3,2,1,0:T(2,128)S(1)}, u32[]{:S(2)}, u32[]{:S(2)}) collective-permute-start(f32[3,8,2,128]{3,2,1,0:T(2,128)S(1)} %get-tuple-element.459), channel_id=1, source_target_pairs={{0,1},{1,0},{2,3},{3,2},{4,5},{5,4},{6,7},{7,6},{8,9},{9,8},{10,11... | collective-permute-start | bytes 73736 | tf_op jit(solution)/shard_map/ppermute | solution.py:20
  111.9 3.8 %collective-permute-start.17 = (f32[3,8,2,128]{3,2,1,0:T(2,128)S(1)}, f32[3,8,2,128]{3,2,1,0:T(2,128)S(1)}, u32[]{:S(2)}, u32[]{:S(2)}) collective-permute-start(f32[3,8,2,128]{3,2,1,0:T(2,128)S(1)} %get-tuple-element.460), channel_id=1, source_target_pairs={{1,0},{0,1},{3,2},{2,3},{5,4},{4,5},{7,6},{6,7},{9,8},{8,9},{11,10... | collective-permute-start | bytes 73736 | tf_op jit(solution)/shard_map/ppermute | solution.py:21
  118.6 6.8 %collective-permute-start.18 = (f32[3,2,32,128]{3,2,1,0:T(8,128)S(1)}, f32[3,2,32,128]{3,2,1,0:T(8,128)S(1)}, u32[]{:S(2)}, u32[]{:S(2)}) collective-permute-start(f32[3,2,32,128]{3,2,1,0:T(8,128)S(1)} %get-tuple-element.481), channel_id=1, source_target_pairs={{0,2},{2,4},{4,6},{6,8},{8,10},{10,12},{12,14},{14,16},{16,18},{18... | collective-permute-start | bytes 294920 | tf_op jit(solution)/shard_map/ppermute | solution.py:20
  118.7 6.7 %collective-permute-start.19 = (f32[3,2,32,128]{3,2,1,0:T(8,128)S(1)}, f32[3,2,32,128]{3,2,1,0:T(8,128)S(1)}, u32[]{:S(2)}, u32[]{:S(2)}) collective-permute-start(f32[3,2,32,128]{3,2,1,0:T(8,128)S(1)} %get-tuple-element.482), channel_id=1, source_target_pairs={{2,0},{4,2},{6,4},{8,6},{10,8},{12,10},{14,12},{16,14},{18,16},{20... | collective-permute-start | bytes 294920 | tf_op jit(solution)/shard_map/ppermute | solution.py:21
  125.4 3.9 %collective-permute-start.20 = (f32[3,8,2,128]{3,2,1,0:T(2,128)S(1)}, f32[3,8,2,128]{3,2,1,0:T(2,128)S(1)}, u32[]{:S(2)}, u32[]{:S(2)}) collective-permute-start(f32[3,8,2,128]{3,2,1,0:T(2,128)S(1)} %get-tuple-element.457), channel_id=1, source_target_pairs={{0,1},{1,0},{2,3},{3,2},{4,5},{5,4},{6,7},{7,6},{8,9},{9,8},{10,11... | collective-permute-start | bytes 73736 | tf_op jit(solution)/shard_map/ppermute | solution.py:20
  127.1 3.8 %collective-permute-start.21 = (f32[3,8,2,128]{3,2,1,0:T(2,128)S(1)}, f32[3,8,2,128]{3,2,1,0:T(2,128)S(1)}, u32[]{:S(2)}, u32[]{:S(2)}) collective-permute-start(f32[3,8,2,128]{3,2,1,0:T(2,128)S(1)} %get-tuple-element.458), channel_id=1, source_target_pairs={{1,0},{0,1},{3,2},{2,3},{5,4},{4,5},{7,6},{6,7},{9,8},{8,9},{11,10... | collective-permute-start | bytes 73736 | tf_op jit(solution)/shard_map/ppermute | solution.py:21
  133.9 6.3 %collective-permute-start.22 = (f32[3,1,32,128]{3,2,1,0:T(8,128)S(1)}, f32[3,1,32,128]{3,2,1,0:T(8,128)S(1)}, u32[]{:S(2)}, u32[]{:S(2)}) collective-permute-start(f32[3,1,32,128]{3,2,1,0:T(8,128)S(1)} %get-tuple-element.471), channel_id=1, source_target_pairs={{0,2},{2,4},{4,6},{6,8},{8,10},{10,12},{12,14},{14,16},{16,18},{18... | collective-permute-start | bytes 147464 | tf_op jit(solution)/shard_map/ppermute | solution.py:20
  133.9 6.2 %collective-permute-start.23 = (f32[3,1,32,128]{3,2,1,0:T(8,128)S(1)}, f32[3,1,32,128]{3,2,1,0:T(8,128)S(1)}, u32[]{:S(2)}, u32[]{:S(2)}) collective-permute-start(f32[3,1,32,128]{3,2,1,0:T(8,128)S(1)} %get-tuple-element.472), channel_id=1, source_target_pairs={{2,0},{4,2},{6,4},{8,6},{10,8},{12,10},{14,12},{16,14},{18,16},{20... | collective-permute-start | bytes 147464 | tf_op jit(solution)/shard_map/ppermute | solution.py:21
  140.1 3.7 %collective-permute-start.24 = (f32[3,6,1,128]{3,2,1,0:T(1,128)S(1)}, f32[3,6,1,128]{3,2,1,0:T(1,128)S(1)}, u32[]{:S(2)}, u32[]{:S(2)}) collective-permute-start(f32[3,6,1,128]{3,2,1,0:T(1,128)S(1)} %get-tuple-element.513), channel_id=1, source_target_pairs={{0,1},{1,0},{2,3},{3,2},{4,5},{5,4},{6,7},{7,6},{8,9},{9,8},{10,11... | collective-permute-start | bytes 27656 | tf_op jit(solution)/shard_map/ppermute | solution.py:20
  140.6 3.7 %collective-permute-start.25 = (f32[3,6,1,128]{3,2,1,0:T(1,128)S(1)}, f32[3,6,1,128]{3,2,1,0:T(1,128)S(1)}, u32[]{:S(2)}, u32[]{:S(2)}) collective-permute-start(f32[3,6,1,128]{3,2,1,0:T(1,128)S(1)} %get-tuple-element.514), channel_id=1, source_target_pairs={{1,0},{0,1},{3,2},{2,3},{5,4},{4,5},{7,6},{6,7},{9,8},{8,9},{11,10... | collective-permute-start | bytes 27656 | tf_op jit(solution)/shard_map/ppermute | solution.py:21
  144.9 11.8 %copy-start.2 = (f32[3,4,32,128]{3,2,1,0:T(8,128)}, f32[3,4,32,128]{3,2,1,0:T(8,128)S(1)}, u32[]{:S(2)}) copy-start(f32[3,4,32,128]{3,2,1,0:T(8,128)S(1)} %pad_maximum_fusion.29) | copy-start | bytes 589828
  144.9 6.3 %collective-permute-start.26 = (f32[3,1,32,128]{3,2,1,0:T(8,128)S(1)}, f32[3,1,32,128]{3,2,1,0:T(8,128)S(1)}, u32[]{:S(2)}, u32[]{:S(2)}) collective-permute-start(f32[3,1,32,128]{3,2,1,0:T(8,128)S(1)} %get-tuple-element.515), channel_id=1, source_target_pairs={{0,2},{2,4},{4,6},{6,8},{8,10},{10,12},{12,14},{14,16},{16,18},{18... | collective-permute-start | bytes 147464 | tf_op jit(solution)/shard_map/ppermute | solution.py:20
  145.0 6.2 %collective-permute-start.27 = (f32[3,1,32,128]{3,2,1,0:T(8,128)S(1)}, f32[3,1,32,128]{3,2,1,0:T(8,128)S(1)}, u32[]{:S(2)}, u32[]{:S(2)}) collective-permute-start(f32[3,1,32,128]{3,2,1,0:T(8,128)S(1)} %get-tuple-element.516), channel_id=1, source_target_pairs={{2,0},{4,2},{6,4},{8,6},{10,8},{12,10},{14,12},{16,14},{18,16},{20... | collective-permute-start | bytes 147464 | tf_op jit(solution)/shard_map/ppermute | solution.py:21
  151.2 3.7 %collective-permute-start.28 = (f32[3,6,1,128]{3,2,1,0:T(1,128)S(1)}, f32[3,6,1,128]{3,2,1,0:T(1,128)S(1)}, u32[]{:S(2)}, u32[]{:S(2)}) collective-permute-start(f32[3,6,1,128]{3,2,1,0:T(1,128)S(1)} %get-tuple-element.511), channel_id=1, source_target_pairs={{0,1},{1,0},{2,3},{3,2},{4,5},{5,4},{6,7},{7,6},{8,9},{9,8},{10,11... | collective-permute-start | bytes 27656 | tf_op jit(solution)/shard_map/ppermute | solution.py:20
  152.9 3.7 %collective-permute-start.29 = (f32[3,6,1,128]{3,2,1,0:T(1,128)S(1)}, f32[3,6,1,128]{3,2,1,0:T(1,128)S(1)}, u32[]{:S(2)}, u32[]{:S(2)}) collective-permute-start(f32[3,6,1,128]{3,2,1,0:T(1,128)S(1)} %get-tuple-element.512), channel_id=1, source_target_pairs={{1,0},{0,1},{3,2},{2,3},{5,4},{4,5},{7,6},{6,7},{9,8},{8,9},{11,10... | collective-permute-start | bytes 27656 | tf_op jit(solution)/shard_map/ppermute | solution.py:21
where the time goes:
time: 158 us
  starting transfers between devices  51.6 us (33%)
  other arithmetic  36.5 us (23%)
  waiting for transfers between devices  35.6 us (23%)
  matrix products  15.9 us (10%)
  local copies, waits for them, and re-layouts  11.9 us (8%)
  between operations  4.52 us (3%)
  loops' own time  2.12 us (1%)
    ppermute x14, starting transfers between devices, padded(): after = lax.ppermute(leading, axis, down)  37.2 us
    ppermute x14, waiting for transfers between devices, padded(): before = lax.ppermute(last, axis, up)  27.5 us
    add x19, other arithmetic, one_block(): along_z + jnp.where(span_z[None] == ((cell_z + tap - 1) % NZ)[:, None], w...  21.8 us
    dot_general x19, matrix products, one_block(): jnp.einsum('pq,cpz->cqz', plane_weight, line_weight, preferred_element_ty...  15.9 us
    ppermute x14, starting transfers between devices, padded(): before = lax.ppermute(last, axis, up)  8.92 us
    ppermute x14, waiting for transfers between devices, padded(): after = lax.ppermute(leading, axis, down)  8.07 us
    ppermute x2, starting transfers between devices, passed_along(): return lax.ppermute(block, axis, route)  5.54 us
    slice x23, local copies, waits for them, and re-layouts, jacobi_sweep(): jnp.roll(centre, -1, -1)  3.81 us
  transfers between devices with their start and end apart: 30, of which 21 were waited for; matrix products, arithmetic and copies ran while one was open for 1% of the time, Pallas kernels for 0%

commit v1 on v0

v1 whole, which is shorter than its diff:
```python
import functools

import jax
import jax.numpy as jnp
from jax import lax
from jax.experimental import pallas as pl
from jax.experimental.pallas import tpu as pltpu
from jax.sharding import PartitionSpec as P

CX = 4
CY = 32
NZ = 128
OUTER = 4
SWEEPS = 3
F32 = jnp.float32
BF16 = jnp.bfloat16
ROWS = CY + 8
PLANES = CX + 3
SPREAD = 288
QUANTITIES = 31
VMEM_BYTES = 48 * 1024 * 1024


def in_vmem(count):
    return [pl.BlockSpec(memory_space=pltpu.VMEM)] * count


def in_smem():
    return pl.BlockSpec(memory_space=pltpu.SMEM)


def params():
    return pltpu.CompilerParams(vmem_limit_bytes=VMEM_BYTES)


def across(n):
    return [(i, (i + 1) % n if i % 2 else (i - 1) % n) for i in range(n)]


def within(n):
    return [(i, i ^ 1) for i in range(n)]


def swap_x(to_within, to_across):
    n = lax.axis_size("gx")
    got_across = lax.ppermute(to_across, "gx", across(n))
    got_within = lax.ppermute(to_within, "gx", within(n))
    return got_within, got_across


def m4_weights(offset):
    remain = 1.0 - offset
    return (
        -0.5 * offset * remain * remain,
        1.0 - 2.5 * offset * offset + 1.5 * offset * offset * offset,
        1.0 - 2.5 * remain * remain + 1.5 * remain * remain * remain,
        -0.5 * offset * offset * remain,
    )


def prepare(cells, offsets, strengths, table, rows):
    weight_x, weight_y, weight_z = (m4_weights(offset) for offset in offsets)
    cell_x = cells // (CY * NZ)
    cell_y = cells // NZ % CY
    cell_z = cells % NZ
    for plane in range(PLANES):
        along = jnp.zeros_like(offsets[0])
        for tap in range(4):
            along = jnp.where(cell_x == plane - tap, weight_x[tap], along)
        table[plane, rows] = along
    for tap in range(4):
        node_y = cell_y + (tap - 1)
        if tap == 0:
            node_y = jnp.where(cell_y == 0, ROWS - 1, node_y)
        table[7 + tap, rows] = weight_y[tap]
        table[11 + tap, rows] = node_y.astype(F32)
        table[15 + tap, rows] = ((cell_z + (tap - 1)) & (NZ - 1)).astype(F32)
        for comp in range(3):
            table[19 + tap * 3 + comp, rows] = weight_z[tap] * strengths[comp]


def spread(table, first, tiles, planes, lines):
    row_ids = lax.broadcasted_iota(jnp.int32, (ROWS, 128), 0).astype(F32)
    z_ids = lax.broadcasted_iota(jnp.int32, (NZ, 128), 0).astype(F32).astype(BF16)
    for tile in range(tiles):
        lanes = slice(tile * 128, (tile + 1) * 128)

        def figure(k):
            return table[k, pl.ds(first + tile, 1)]

        along_y = jnp.zeros((ROWS, 128), F32)
        for tap in range(4):
            along_y = jnp.where(row_ids == figure(11 + tap), figure(7 + tap), along_y)
        parts = [figure(plane) * along_y for plane in range(PLANES)]
        parts.append(jnp.zeros((SPREAD - PLANES * ROWS, 128), F32))
        planes[:, lanes] = jnp.concatenate(parts, axis=0).astype(BF16)
        masks = [z_ids == figure(15 + tap).astype(BF16) for tap in range(4)]
        for comp in range(3):
            line = jnp.zeros((NZ, 128), BF16)
            for tap in range(4):
                line = jnp.where(masks[tap], figure(19 + tap * 3 + comp).astype(BF16), line)
            lines[comp * NZ : (comp + 1) * NZ, lanes] = line


def product(planes, lines):
    return lax.dot_general(
        planes[...], lines[...], (((1,), (1,)), ((), ())), preferred_element_type=F32
    )


def staying_kernel(
    limits, cell_hbm, offset_hbm, vort_hbm, total, cells, offsets, vorts, dense, table,
    planes_a, lines_a, planes_b, lines_b, sems, *, tiles_per_chunk,
):
    first_stay = limits[0] + limits[1]
    live_len = limits[2]
    tiles = cells.shape[0]
    copies = [
        pltpu.make_async_copy(offset_hbm, offsets, sems.at[0]),
        pltpu.make_async_copy(vort_hbm, vorts, sems.at[1]),
        pltpu.make_async_copy(cell_hbm, cells, sems.at[2]),
    ]
    for copy in copies:
        copy.start()
    total[...] = jnp.zeros_like(total)
    for copy in copies:
        copy.wait()
    for tile in range(tiles):
        lanes = slice(tile * 128, (tile + 1) * 128)
        for dim in range(3):
            dense[dim, tile : tile + 1] = offsets[dim : dim + 1, lanes]
            dense[3 + dim, tile : tile + 1] = vorts[dim : dim + 1, lanes]

    def one_group(group, carry):
        rows = pl.ds(pl.multiple_of(group * 8, 8), 8)
        slot = (
            group * 1024
            + lax.broadcasted_iota(jnp.int32, (8, 128), 0) * 128
            + lax.broadcasted_iota(jnp.int32, (8, 128), 1)
        )
        keep = (slot >= first_stay) & (slot < live_len)
        prepare(
            cells[rows],
            [dense[dim, rows] for dim in range(3)],
            [jnp.where(keep, dense[3 + dim, rows], 0.0) for dim in range(3)],
            table,
            rows,
        )
        return carry

    lax.fori_loop(0, tiles // 8, one_group, 0)
    chunks = tiles // tiles_per_chunk
    spread(table, 0, tiles_per_chunk, planes_a, lines_a)

    def two_chunks(pair, carry):
        spread(table, (2 * pair + 1) * tiles_per_chunk, tiles_per_chunk, planes_b, lines_b)
        total[...] += product(planes_a, lines_a)
        spread(table, (2 * pair + 2) * tiles_per_chunk, tiles_per_chunk, planes_a, lines_a)
        total[...] += product(planes_b, lines_b)
        return carry

    lax.fori_loop(0, (chunks - 1) // 2, two_chunks, 0)
    if chunks % 2 == 0:
        spread(table, (chunks - 1) * tiles_per_chunk, tiles_per_chunk, planes_b, lines_b)
        total[...] += product(planes_a, lines_a)
        total[...] += product(planes_b, lines_b)
    else:
        total[...] += product(planes_a, lines_a)


def deposit_staying(part_cell, part_offset, part_vort, limits):
    slots = part_cell.shape[0]
    tiles = slots // 128
    per_chunk = 17
    chunk = per_chunk * 128
    return pl.pallas_call(
        functools.partial(staying_kernel, tiles_per_chunk=per_chunk),
        in_specs=[in_smem()] + [pl.BlockSpec(memory_space=pl.ANY)] * 3,
        out_specs=in_vmem(1)[0],
        out_shape=jax.ShapeDtypeStruct((SPREAD, 3 * NZ), F32),
        scratch_shapes=[
            pltpu.VMEM((tiles, 128), jnp.int32),
            pltpu.VMEM((3, slots), F32),
            pltpu.VMEM((3, slots), F32),
            pltpu.VMEM((6, tiles, 128), F32),
            pltpu.VMEM((QUANTITIES, tiles, 128), F32),
        ]
        + [pltpu.VMEM((SPREAD, chunk), BF16), pltpu.VMEM((3 * NZ, chunk), BF16)] * 2
        + [pltpu.SemaphoreType.DMA((3,))],
        compiler_params=params(),
        cost_estimate=pl.CostEstimate(
            flops=2 * SPREAD * 3 * NZ * slots, bytes_accessed=28 * slots, transcendentals=0
        ),
    )(limits, part_cell.reshape(tiles, 128), part_offset, part_vort)


def arrived_kernel(side, total, got_within, got_across, deposits, to_within, to_across, dense, table, planes, lines):
    tiles = got_within.shape[1] // 128
    for which, got in enumerate((got_within, got_across)):
        for tile in range(tiles):
            lanes = slice(tile * 128, (tile + 1) * 128)
            place = which * tiles + tile
            for k in range(7):
                dense[k, place : place + 1] = got[k : k + 1, lanes]
    for group in range(2 * tiles // 8):
        rows = slice(group * 8, (group + 1) * 8)
        prepare(
            dense[6, rows].astype(jnp.int32),
            [dense[dim, rows] for dim in range(3)],
            [dense[3 + dim, rows] for dim in range(3)],
            table,
            rows,
        )
    spread(table, 0, 2 * tiles, planes, lines)
    whole = total[...] + product(planes, lines)
    for comp in range(3):
        for plane in range(PLANES):
            deposits[comp, plane] = whole[
                plane * ROWS : (plane + 1) * ROWS, comp * NZ : (comp + 1) * NZ
            ]
    first_within = jnp.where(side[0] == 0, CX, 0)
    first_across = jnp.where(side[0] == 0, 0, CX)
    to_within[...] = deposits[:, pl.ds(first_within, 3)]
    to_across[...] = deposits[:, pl.ds(first_across, 3)]


def deposit_arrived(side, total, got_within, got_across):
    received = got_within.shape[1]
    edge = jax.ShapeDtypeStruct((3, 3, ROWS, NZ), F32)
    tiles = 2 * received // 128
    return pl.pallas_call(
        arrived_kernel,
        in_specs=[in_smem()] + in_vmem(3),
        out_specs=tuple(in_vmem(3)),
        out_shape=(jax.ShapeDtypeStruct((3, PLANES, ROWS, NZ), F32), edge, edge),
        scratch_shapes=[
            pltpu.VMEM((7, tiles, 128), F32),
            pltpu.VMEM((QUANTITIES, tiles, 128), F32),
            pltpu.VMEM((SPREAD, 2 * received), BF16),
            pltpu.VMEM((3 * NZ, 2 * received), BF16),
        ],
        compiler_params=params(),
    )(side, total, got_within, got_across)


def leaving(part_cell, part_offset, part_vort, limits):
    capacity = part_cell.shape[0] // 17
    room = 2 * capacity
    packed = jnp.concatenate(
        [part_offset[:, :room], part_vort[:, :room], part_cell[:room].astype(F32)[None]], axis=0
    )
    ids = jnp.arange(capacity, dtype=jnp.int32)[None]
    to_prev = jnp.where(ids < limits[0], packed[:, :capacity], 0.0)
    shifted = lax.dynamic_slice_in_dim(packed, limits[0], capacity, 1)
    to_next = jnp.where(ids < limits[1], shifted, 0.0)
    return to_prev, to_next


def edge_rows(low, high):
    ids = lax.broadcasted_iota(jnp.int32, (8, NZ), 0)
    return jnp.where(ids < 4, low, high)


def edged_plane(mine, other):
    return jnp.concatenate([mine, edge_rows(other[:8], other[-8:])], axis=0)


def roll_rows(value, shift):
    return pltpu.roll(value, shift % value.shape[0], 0)


def roll_z(value, shift):
    return pltpu.roll(value, shift % NZ, 1)


def relax(fields, sources):
    ids = lax.broadcasted_iota(jnp.int32, (ROWS, NZ), 0)
    frozen = (ids > CY) & (ids < ROWS - 1)
    for sweep in range(SWEEPS):
        fresh = list(fields)
        last = sweep == SWEEPS - 1
        for x in range(2 if last else 1, CX + (2 if last else 3)):
            centre = fields[x]
            summed = fields[x - 1] + fields[x + 1] + roll_rows(centre, 1) + roll_rows(centre, -1)
            summed = summed + roll_z(centre, 1) + roll_z(centre, -1) + sources[x - 1]
            fresh[x] = jnp.where(frozen, centre, summed * (1.0 / 6.0))
        fields = fresh
    return fields[2 : CX + 2]


def hand_out(side, potential, to_within, to_across):
    first_within = jnp.where(side[0] == 0, CX - 2, 0)
    first_across = jnp.where(side[0] == 0, 0, CX - 2)
    rows = to_within.shape[2]
    if rows == 2 * CY:
        to_within[...] = potential[:, pl.ds(first_within, 2)]
        to_across[...] = potential[:, pl.ds(first_across, 2)]
    else:
        for first, out in ((first_within, to_within), (first_across, to_across)):
            out[:, :, : CY + 8] = potential[:, pl.ds(first, 2), : CY + 8]
            out[:, :, CY + 8 :] = potential[:, pl.ds(first, 2), 2 * CY - 8 :]


def first_kernel(side, mine, other, omega, potential, to_within, to_across):
    ids = lax.broadcasted_iota(jnp.int32, (8, NZ), 0)

    def folded(main, edges):
        low = main[:8] + jnp.where(ids < 2, edges, 0.0)
        high = main[CY - 8 : CY] + jnp.where(ids == 7, edges, 0.0)
        return jnp.concatenate([low, main[8 : CY - 8], high], axis=0)

    def one_component(comp, carry):
        sources = ([], [])
        for x in range(CX + 2):
            a = mine[comp, x]
            b = other[comp, x]
            omega_a = folded(a[:CY], b[CY:])
            omega_b = folded(b[:CY], a[CY:])
            omega[comp, x, :CY] = omega_a
            omega[comp, x, CY:] = omega_b
            sources[0].append(edged_plane(omega_a, omega_b))
            sources[1].append(edged_plane(omega_b, omega_a))
        for block in range(2):
            fields = [jnp.zeros((ROWS, NZ), F32)] * (CX + 4)
            fields = relax(fields, sources[block])
            for x in range(CX):
                potential[comp, x, block * CY : (block + 1) * CY] = fields[x][:CY]
        return carry

    lax.fori_loop(0, 3, one_component, 0)
    hand_out(side, potential, to_within, to_across)


def ring_planes(side, got_within, got_across, comp):
    even = side[0] == 0

    def both(got, x):
        value = got[comp, x]
        if value.shape[0] == 2 * CY:
            return value[:CY], value[CY:]
        high = value[CY + 8 :]
        return value[:CY], jnp.concatenate([value[CY : CY + 8], high, high, high], axis=0)

    def chosen(pick, x):
        inner, outer = both(got_within, x), both(got_across, x)
        return tuple(jnp.where(pick, a, b) for a, b in zip(inner, outer))

    below = [chosen(jnp.logical_not(even), x) for x in range(2)]
    above = [chosen(even, x) for x in range(2)]
    return below, above


def gathered(side, potential, got_within, got_across, comp):
    below, above = ring_planes(side, got_within, got_across, comp)
    middle = [(potential[comp, x, :CY], potential[comp, x, CY:]) for x in range(CX)]
    return below + middle + above


def next_kernel(side, omega, before, got_within, got_across, potential, to_within, to_across):
    def one_component(comp, carry):
        pairs = gathered(side, before, got_within, got_across, comp)
        charge = [(omega[comp, x, :CY], omega[comp, x, CY:]) for x in range(CX + 2)]
        for block in range(2):
            fields = [edged_plane(pair[block], pair[1 - block]) for pair in pairs]
            sources = [edged_plane(pair[block], pair[1 - block]) for pair in charge]
            fields = relax(fields, sources)
            for x in range(CX):
                potential[comp, x, block * CY : (block + 1) * CY] = fields[x][:CY]
        return carry

    lax.fori_loop(0, 3, one_component, 0)
    hand_out(side, potential, to_within, to_across)


def last_kernel(side, omega, potential, got_within, got_across, velocity, stretching):
    psi = []
    for comp in range(3):
        pairs = gathered(side, potential, got_within, got_across, comp)
        psi.append([edged_plane(a, b) for a, b in pairs])

    def slope_x(planes, x):
        return (planes[x + 1] - planes[x - 1]) * 0.5

    def slope_y(plane):
        return (roll_rows(plane, -1) - roll_rows(plane, 1)) * 0.5

    def slope_z(plane):
        return (roll_z(plane, -1) - roll_z(plane, 1)) * 0.5

    speeds = ([None], [None], [None])
    for x in range(1, CX + 3):
        speeds[0].append(slope_y(psi[2][x]) - slope_z(psi[1][x]))
        speeds[1].append(slope_z(psi[0][x]) - slope_x(psi[2], x))
        speeds[2].append(slope_x(psi[1], x) - slope_y(psi[0][x]))
    for comp in range(3):
        for x in range(CX):
            centre = speeds[comp][x + 2]
            velocity[comp, x] = centre[:CY]
            stretching[comp, x] = (
                omega[0, x + 1, :CY] * slope_x(speeds[comp], x + 2)[:CY]
                + omega[1, x + 1, :CY] * slope_y(centre)[:CY]
                + omega[2, x + 1, :CY] * slope_z(centre)[:CY]
            )


def edge_shape(rows):
    return jax.ShapeDtypeStruct((3, 2, rows, NZ), F32)


def two_block_solve(side, deposits, to_within, to_across):
    got_within, got_across = swap_x(to_within, to_across)
    even = side[0] == 0
    from_prev = jnp.where(even, got_across, got_within)
    from_next = jnp.where(even, got_within, got_across)[:, :2]
    none = ((0, 0), (0, 0))
    mine = (
        deposits[:, : CX + 2]
        + jnp.pad(from_prev, ((0, 0), (0, CX - 1)) + none)
        + jnp.pad(from_next, ((0, 0), (CX, 0)) + none)
    )
    other = lax.ppermute(mine, "gy", [(0, 1), (1, 0)])
    slab = jax.ShapeDtypeStruct((3, CX, 2 * CY, NZ), F32)
    omega, potential, to_within, to_across = pl.pallas_call(
        first_kernel,
        in_specs=[in_smem()] + in_vmem(2),
        out_specs=tuple(in_vmem(4)),
        out_shape=(
            jax.ShapeDtypeStruct((3, CX + 2, 2 * CY, NZ), F32),
            slab,
            edge_shape(2 * CY),
            edge_shape(2 * CY),
        ),
        compiler_params=params(),
    )(side, mine, other)
    for _ in range(1, OUTER):
        got_within, got_across = swap_x(to_within, to_across)
        potential, to_within, to_across = pl.pallas_call(
            next_kernel,
            in_specs=[in_smem()] + in_vmem(4),
            out_specs=tuple(in_vmem(3)),
            out_shape=(slab, edge_shape(CY + 16), edge_shape(CY + 16)),
            compiler_params=params(),
        )(side, omega, potential, got_within, got_across)
    got_within, got_across = swap_x(to_within, to_across)
    block = jax.ShapeDtypeStruct((3, CX, CY, NZ), F32)
    return pl.pallas_call(
        last_kernel,
        in_specs=[in_smem()] + in_vmem(4),
        out_specs=tuple(in_vmem(2)),
        out_shape=(block, block),
        compiler_params=params(),
    )(side, omega, potential, got_within, got_across)


def padded(value, sides, width):
    for axis, dim in sides:
        devices, length = (lax.axis_size(axis), value.shape[dim])
        up = [(i, (i + 1) % devices) for i in range(devices)]
        down = [(j, i) for i, j in up]
        last = lax.slice_in_dim(value, length - width, length, axis=dim)
        leading = lax.slice_in_dim(value, 0, width, axis=dim)
        before = lax.ppermute(last, axis, up)
        after = lax.ppermute(leading, axis, down)
        value = jnp.concatenate([before, value, after], axis=dim)
    return value


def jacobi_sweep(field, source):
    centre = field[..., 1:-1, 1:-1, :]
    summed = (
        field[..., :-2, 1:-1, :]
        + field[..., 2:, 1:-1, :]
        + field[..., 1:-1, :-2, :]
        + field[..., 1:-1, 2:, :]
    )
    summed = summed + jnp.roll(centre, 1, -1) + jnp.roll(centre, -1, -1) + source
    return field.at[..., 1:-1, 1:-1, :].set(summed / 6.0)


def slope_x(field):
    return (field[2:, 1:-1] - field[:-2, 1:-1]) * 0.5


def slope_y(field):
    return (field[1:-1, 2:] - field[1:-1, :-2]) * 0.5


def slope_z(field):
    centre = field[1:-1, 1:-1]
    return (jnp.roll(centre, -1, -1) - jnp.roll(centre, 1, -1)) * 0.5


def fold_ghosts(extended, axis_dim, extent):
    centre = lax.slice_in_dim(extended, 4, extent + 4, axis=axis_dim)
    low_rim = lax.slice_in_dim(extended, 0, 2, axis=axis_dim)
    high_rim = lax.slice_in_dim(extended, extent + 6, extent + 8, axis=axis_dim)
    pad_low = [(0, 0)] * extended.ndim
    pad_high = [(0, 0)] * extended.ndim
    pad_low[axis_dim] = (0, extent - 2)
    pad_high[axis_dim] = (extent - 2, 0)
    return centre + jnp.pad(low_rim, pad_low) + jnp.pad(high_rim, pad_high)


def general_solve(deposits):
    sides = (("gx", 1), ("gy", 2))
    rows = jnp.concatenate(
        [jnp.zeros_like(deposits[:, :, :1]), deposits[:, :, ROWS - 1 :], deposits[:, :, : CY + 2]],
        axis=2,
    )
    full = jnp.pad(rows, ((0, 0), (1, 0), (0, 0), (0, 0)))
    omega = fold_ghosts(fold_ghosts(padded(full, sides, 2), 1, CX), 2, CY)
    source = padded(omega, sides, 2)[:, 1:-1, 1:-1]
    potential = jnp.zeros_like(omega)
    for _ in range(OUTER):
        field = padded(potential, sides, 2)
        for _ in range(SWEEPS):
            field = jacobi_sweep(field, source)
        potential = field[:, 2:-2, 2:-2]
    wide = padded(potential, sides, 2)
    edged_velocity = jnp.stack(
        [
            slope_y(wide[2]) - slope_z(wide[1]),
            slope_z(wide[0]) - slope_x(wide[2]),
            slope_x(wide[1]) - slope_y(wide[0]),
        ]
    )
    stretching = jnp.stack(
        [
            omega[0] * slope_x(edged_velocity[comp])
            + omega[1] * slope_y(edged_velocity[comp])
            + omega[2] * slope_z(edged_velocity[comp])
            for comp in range(3)
        ]
    )
    return edged_velocity[:, 1:-1, 1:-1], stretching


def per_device(part_cell, part_offset, part_vort, moving):
    limits = moving[0]
    side = (lax.axis_index("gx") % 2).astype(jnp.int32)[None]
    even = side[0] == 0
    to_prev, to_next = leaving(part_cell, part_offset, part_vort, limits)
    got_within, got_across = swap_x(
        jnp.where(even, to_next, to_prev), jnp.where(even, to_prev, to_next)
    )
    total = deposit_staying(part_cell, part_offset, part_vort, limits)
    deposits, to_within, to_across = deposit_arrived(side, total, got_within, got_across)
    if lax.axis_size("gy") == 2:
        return two_block_solve(side, deposits, to_within, to_across)
    return general_solve(deposits)


def solution(mesh):
    return jax.shard_map(
        per_device,
        mesh=mesh,
        in_specs=(
            P(("gx", "gy")),
            P(None, ("gx", "gy")),
            P(None, ("gx", "gy")),
            P(("gx", "gy"), None),
        ),
        out_specs=(P(None, "gx", "gy", None), P(None, "gx", "gy", None)),
        check_vma=False,
    )
```

time: 158 us -> 79.1 us (0.50)
  other arithmetic: 36.5 us -> 2.27 us
  starting transfers between devices: 51.6 us -> 18.2 us
  Pallas kernels: 0 us -> 19.9 us
  matrix products: 15.9 us -> 0 us
  local copies, waits for them, and re-layouts: 11.9 us -> 2.27 us
  loops' own time: 2.12 us -> 0 us
  waiting for transfers between devices: 35.6 us -> 33.5 us
  between operations: 4.52 us -> 2.79 us
    ppermute x30 -> x13, starting transfers between devices: 51.6 us -> 18.2 us  [the longest x6 16.3 us: swap_x(): got_across = lax.ppermute(to_across, 'gx', across(n))]
    add x78 -> x1, other arithmetic: 23.7 us -> 0.05 us  [two_block_solve(): deposits[:, :CX + 2] + jnp.pad(from_prev, ((0, 0), (0, CX - 1)) + none)]
    pallas_call x0 -> x7, Pallas kernels: none -> 19.9 us  [the longest x1 11.3 us: deposit_staying(): pl.pallas_call(functools.partial(staying_kernel, tiles_per_chunk=per_chun...]
    dot_general x19 -> x0, matrix products: 15.9 us -> none  [one_block(): jnp.einsum('pq,cpz->cqz', plane_weight, line_weight, preferred_element_ty...]
    slice x51 -> x5, local copies, waits for them, and re-layouts: 6.26 us -> 0.66 us  [the longest x1 0.58 us: leaving(): to_next = jnp.where(ids < limits[1], shifted, 0.0)]
    div x12 -> x0, other arithmetic: 3.76 us -> none  [jacobi_sweep(): return field.at[..., 1:-1, 1:-1, :].set(summed / 6.0)]
    scatter x8 -> x0, local copies, waits for them, and re-layouts: 2.52 us -> none  [jacobi_sweep(): return field.at[..., 1:-1, 1:-1, :].set(summed / 6.0)]
    convert_element_type x19 -> x0, local copies, waits for them, and re-layouts: 2.16 us -> none  [one_block(): plane_weight = (along_x[:, :, None] * along_y[:, None, :]).reshape(block_...]
  transfers between devices with their start and end apart: 30 -> 13, of which waited for: 21 -> 6; matrix products, arithmetic and copies ran while one was open for 1% -> 0% of each run, Pallas kernels for 0% -> 14%
where the time goes in v1:
time: 79.1 us; the launch traced here: 78.9 us
  waiting for transfers between devices  33.5 us (42%)
  Pallas kernels  19.9 us (25%)
  starting transfers between devices  18.2 us (23%)
  between operations  2.79 us (4%)
  local copies, waits for them, and re-layouts  2.27 us (3%)
  other arithmetic  2.27 us (3%)
    ppermute x6, waiting for transfers between devices, swap_x(): got_across = lax.ppermute(to_across, 'gx', across(n))  26.7 us
    ppermute x6, starting transfers between devices, swap_x(): got_across = lax.ppermute(to_across, 'gx', across(n))  16.3 us
    pallas_call x1, Pallas kernels, deposit_staying(): pl.pallas_call(functools.partial(staying_kernel, tiles_per_chunk=per_chun...  11.3 us
    ppermute x1, waiting for transfers between devices, two_block_solve(): other = lax.ppermute(mine, 'gy', [(0, 1), (1, 0)])  6.77 us
    pallas_call x3, Pallas kernels, two_block_solve(): pl.pallas_call(next_kernel, in_specs=[in_smem()] + in_vmem(4), out_specs=...  4.77 us
    pallas_call x1, Pallas kernels, deposit_arrived(): pl.pallas_call(arrived_kernel, in_specs=[in_smem()] + in_vmem(3), out_spe...  1.63 us
    unnamed x8, local copies, waits for them, and re-layouts  1.61 us
    ppermute x1, starting transfers between devices, two_block_solve(): other = lax.ppermute(mine, 'gy', [(0, 1), (1, 0)])  1.58 us
  transfers between devices with their start and end apart: 13, of which 6 were waited for; matrix products, arithmetic and copies ran while one was open for 0% of the time, Pallas kernels for 14%

profile of v1, /device:TPU:0, one launch (start us, length us, event | category | flops | bytes accessed | tf_op | source)
XLA Modules:
  0.0 78.9 jit_solution(9018989730481110795)
XLA Ops:
  0.6 0.0 copy-start.2
  0.7 0.6 copy-done.2
  1.3 0.6 fusion.2
  3.2 1.3 %iota_compare_fusion = (pred[1024]{0:T(1024)(128)(4,1)S(1)}, pred[1024]{0:T(1024)(128)(4,1)S(1)}) fusion(s32[]{:T(128)} %bitcast.5, s32[]{:T(128)} %bitcast.3), kind=kLoop, calls=%fused_computation.9 | loop fusion | flops 2048 | bytes 2056 | tf_op jit(solution)/shard_map/lt | solution.py:253
  4.5 0.0 copy-start.3
  4.5 0.8 slice_convert_fusion
  5.3 0.0 slice-start.1
  6.0 0.1 slice-done.1
  6.0 0.0 slice-done
  6.1 0.1 fusion
  6.2 5.5 %collective-permute-start.1 = (f32[7,1024]{1,0:T(8,128)S(1)}, f32[7,1024]{1,0:T(8,128)S(1)}, u32[]{:S(2)}, u32[]{:S(2)}) collective-permute-start(f32[7,1024]{1,0:T(8,128)S(1)} %get-tuple-element.34), channel_id=1, source_target_pairs={{0,30},{2,4},{4,2},{6,8},{8,6},{10,12},{12,10},{14,16},{16,14},{18... | collective-permute-start | bytes 86024 | tf_op jit(solution)/shard_map/ppermute | solution.py:46
  11.6 0.0 collective-permute-start
  11.6 0.0 copy-done.3
  11.6 0.0 copy-done
  11.6 0.0 copy-start.1
  11.6 0.9 %copy-done.1 = f32[3,17408]{1,0:T(4,128)S(1)} copy-done((f32[3,17408]{1,0:T(4,128)S(1)}, f32[3,17408]{1,0:T(4,128)}, u32[]{:S(2)}) %copy-start.1) | copy-done | bytes 208920
  12.6 11.3 %shard_map.59.total = f32[288,384]{1,0:T(8,128)S(1)} custom-call(s32[3]{0:T(128)S(1)} %bitcast.6, s32[136,128]{1,0:T(8,128)S(1)} %bitcast.7, f32[3,17408]{1,0:T(4,128)S(1)} %copy-done, f32[3,17408]{1,0:T(4,128)S(1)} %copy-done.1), custom_call_target="tpu_custom_call" | custom-call | flops 3850371072 | bytes 487424 | tf_op jit(solution)/shard_map/pallas_call | solution.py:176
  23.9 0.0 collective-permute-done.1.got_across
  24.0 0.0 collective-permute-done.got_within
  24.0 1.6 %shard_map.60 = (f32[3,7,40,128]{3,2,1,0:T(8,128)S(1)}, f32[3,3,40,128]{3,2,1,0:T(8,128)S(1)}, f32[3,3,40,128]{3,2,1,0:T(8,128)S(1)}) custom-call(s32[1]{0:T(128)} %bitcast.side, f32[288,384]{1,0:T(8,128)S(1)} %shard_map.59.total, f32[7,1024]{1,0:T(8,128)S(1)} %collective-permute-done.got_within, f32[7,1024]{1,0:T(8,128)S(1)} %collective-permute-done.1.got_across), custom_call_target="tpu_custom_call" | custom-call | tf_op jit(solution)/shard_map/pallas_call | solution.py:231
  25.6 0.8 %collective-permute-start.2 = (f32[3,3,40,128]{3,2,1,0:T(8,128)S(1)}, f32[3,3,40,128]{3,2,1,0:T(8,128)S(1)}, u32[]{:S(2)}, u32[]{:S(2)}) collective-permute-start(f32[3,3,40,128]{3,2,1,0:T(8,128)S(1)} %get-tuple-element.19), channel_id=1, source_target_pairs={{0,30},{2,4},{4,2},{6,8},{8,6},{10,12},{12,10},{14,16},{16,14},{18... | collective-permute-start | bytes 552968 | tf_op jit(solution)/shard_map/ppermute | solution.py:46
  26.4 0.0 collective-permute-start.3
  26.4 6.9 %collective-permute-done.2 = f32[3,3,40,128]{3,2,1,0:T(8,128)S(1)} collective-permute-done((f32[3,3,40,128]{3,2,1,0:T(8,128)S(1)}, f32[3,3,40,128]{3,2,1,0:T(8,128)S(1)}, u32[]{:S(2)}, u32[]{:S(2)}) %collective-permute-start.2) | collective-permute-done | bytes 184352 | tf_op jit(solution)/shard_map/ppermute | solution.py:46
  33.3 0.0 collective-permute-done.3
  33.4 0.1 pad_add_fusion.mine
  33.4 1.6 %collective-permute-start.4 = (f32[3,6,40,128]{3,2,1,0:T(8,128)S(1)}, f32[3,6,40,128]{3,2,1,0:T(8,128)S(1)}, u32[]{:S(2)}, u32[]{:S(2)}) collective-permute-start(f32[3,6,40,128]{3,2,1,0:T(8,128)S(1)} %pad_add_fusion.mine), channel_id=1, source_target_pairs={{0,1},{1,0},{2,3},{3,2},{4,5},{5,4},{6,7},{7,6},{8,9},{9,8},{10,11... | collective-permute-start | bytes 1105928 | tf_op jit(solution)/shard_map/ppermute | solution.py:421
  35.0 6.8 %collective-permute-done.4.other = f32[3,6,40,128]{3,2,1,0:T(8,128)S(1)} collective-permute-done((f32[3,6,40,128]{3,2,1,0:T(8,128)S(1)}, f32[3,6,40,128]{3,2,1,0:T(8,128)S(1)}, u32[]{:S(2)}, u32[]{:S(2)}) %collective-permute-start.4) | collective-permute-done | bytes 368672 | tf_op jit(solution)/shard_map/ppermute | solution.py:421
  41.8 1.1 %shard_map.61 = (f32[3,6,64,128]{3,2,1,0:T(8,128)S(1)}, f32[3,4,64,128]{3,2,1,0:T(8,128)S(1)}, f32[3,2,64,128]{3,2,1,0:T(8,128)S(1)}, f32[3,2,64,128]{3,2,1,0:T(8,128)S(1)}) custom-call(s32[1]{0:T(128)} %bitcast.side, f32[3,6,40,128]{3,2,1,0:T(8,128)S(1)} %pad_add_fusion.mine, f32[3,6,40,128]{3,2,1,0:T(8,128)S(1)} %collective-permute-done.4.other), custom_call_target="tpu_custom_call" | custom-call | tf_op jit(solution)/shard_map/pallas_call | solution.py:423
  42.9 0.1 collective-permute-start.5
  43.0 2.5 %collective-permute-start.6 = (f32[3,2,64,128]{3,2,1,0:T(8,128)S(1)}, f32[3,2,64,128]{3,2,1,0:T(8,128)S(1)}, u32[]{:S(2)}, u32[]{:S(2)}) collective-permute-start(f32[3,2,64,128]{3,2,1,0:T(8,128)S(1)} %get-tuple-element.24), channel_id=1, source_target_pairs={{0,30},{2,4},{4,2},{6,8},{8,6},{10,12},{12,10},{14,16},{16,14},{18... | collective-permute-start | bytes 589832 | tf_op jit(solution)/shard_map/ppermute | solution.py:46
  45.5 0.0 collective-permute-done.5.got_within
  45.5 5.4 %collective-permute-done.6.got_across = f32[3,2,64,128]{3,2,1,0:T(8,128)S(1)} collective-permute-done((f32[3,2,64,128]{3,2,1,0:T(8,128)S(1)}, f32[3,2,64,128]{3,2,1,0:T(8,128)S(1)}, u32[]{:S(2)}, u32[]{:S(2)}) %collective-permute-start.6) | collective-permute-done | bytes 196640 | tf_op jit(solution)/shard_map/ppermute | solution.py:46
  50.9 1.6 %shard_map.62 = (f32[3,4,64,128]{3,2,1,0:T(8,128)S(1)}, f32[3,2,48,128]{3,2,1,0:T(8,128)S(1)}, f32[3,2,48,128]{3,2,1,0:T(8,128)S(1)}) custom-call(s32[1]{0:T(128)} %bitcast.side, f32[3,6,64,128]{3,2,1,0:T(8,128)S(1)} %get-tuple-element.21.omega, f32[3,4,64,128]{3,2,1,0:T(8,128)S(1)} %get-tuple-element.22.before, ...), custom_call_target="tpu_custom_call" | custom-call | tf_op jit(solution)/shard_map/pallas_call | solution.py:437
  52.5 0.1 collective-permute-start.7
  52.6 2.5 %collective-permute-start.8 = (f32[3,2,48,128]{3,2,1,0:T(8,128)S(1)}, f32[3,2,48,128]{3,2,1,0:T(8,128)S(1)}, u32[]{:S(2)}, u32[]{:S(2)}) collective-permute-start(f32[3,2,48,128]{3,2,1,0:T(8,128)S(1)} %get-tuple-element.27), channel_id=1, source_target_pairs={{0,30},{2,4},{4,2},{6,8},{8,6},{10,12},{12,10},{14,16},{16,14},{18... | collective-permute-start | bytes 442376 | tf_op jit(solution)/shard_map/ppermute | solution.py:46
  55.1 0.0 collective-permute-done.7.got_within
  55.1 4.8 %collective-permute-done.8.got_across = f32[3,2,48,128]{3,2,1,0:T(8,128)S(1)} collective-permute-done((f32[3,2,48,128]{3,2,1,0:T(8,128)S(1)}, f32[3,2,48,128]{3,2,1,0:T(8,128)S(1)}, u32[]{:S(2)}, u32[]{:S(2)}) %collective-permute-start.8) | collective-permute-done | bytes 147488 | tf_op jit(solution)/shard_map/ppermute | solution.py:46
  59.9 1.6 %shard_map.63 = (f32[3,4,64,128]{3,2,1,0:T(8,128)S(1)}, f32[3,2,48,128]{3,2,1,0:T(8,128)S(1)}, f32[3,2,48,128]{3,2,1,0:T(8,128)S(1)}) custom-call(s32[1]{0:T(128)} %bitcast.side, f32[3,6,64,128]{3,2,1,0:T(8,128)S(1)} %get-tuple-element.21.omega, f32[3,4,64,128]{3,2,1,0:T(8,128)S(1)} %get-tuple-element.25.before, ...), custom_call_target="tpu_custom_call" | custom-call | tf_op jit(solution)/shard_map/pallas_call | solution.py:437
  61.5 0.1 collective-permute-start.9
  61.6 2.5 %collective-permute-start.10 = (f32[3,2,48,128]{3,2,1,0:T(8,128)S(1)}, f32[3,2,48,128]{3,2,1,0:T(8,128)S(1)}, u32[]{:S(2)}, u32[]{:S(2)}) collective-permute-start(f32[3,2,48,128]{3,2,1,0:T(8,128)S(1)} %get-tuple-element.30), channel_id=1, source_target_pairs={{0,30},{2,4},{4,2},{6,8},{8,6},{10,12},{12,10},{14,16},{16,14},{18... | collective-permute-start | bytes 442376 | tf_op jit(solution)/shard_map/ppermute | solution.py:46
  64.1 0.0 collective-permute-done.9.got_within
  64.1 4.8 %collective-permute-done.10.got_across = f32[3,2,48,128]{3,2,1,0:T(8,128)S(1)} collective-permute-done((f32[3,2,48,128]{3,2,1,0:T(8,128)S(1)}, f32[3,2,48,128]{3,2,1,0:T(8,128)S(1)}, u32[]{:S(2)}, u32[]{:S(2)}) %collective-permute-start.10) | collective-permute-done | bytes 147488 | tf_op jit(solution)/shard_map/ppermute | solution.py:46
  68.9 1.6 %shard_map.64 = (f32[3,4,64,128]{3,2,1,0:T(8,128)S(1)}, f32[3,2,48,128]{3,2,1,0:T(8,128)S(1)}, f32[3,2,48,128]{3,2,1,0:T(8,128)S(1)}) custom-call(s32[1]{0:T(128)} %bitcast.side, f32[3,6,64,128]{3,2,1,0:T(8,128)S(1)} %get-tuple-element.21.omega, f32[3,4,64,128]{3,2,1,0:T(8,128)S(1)} %get-tuple-element.28.before, ...), custom_call_target="tpu_custom_call" | custom-call | tf_op jit(solution)/shard_map/pallas_call | solution.py:437
  70.5 0.1 collective-permute-start.11
  70.6 2.5 %collective-permute-start.12 = (f32[3,2,48,128]{3,2,1,0:T(8,128)S(1)}, f32[3,2,48,128]{3,2,1,0:T(8,128)S(1)}, u32[]{:S(2)}, u32[]{:S(2)}) collective-permute-start(f32[3,2,48,128]{3,2,1,0:T(8,128)S(1)} %get-tuple-element.33), channel_id=1, source_target_pairs={{0,30},{2,4},{4,2},{6,8},{8,6},{10,12},{12,10},{14,16},{16,14},{18... | collective-permute-start | bytes 442376 | tf_op jit(solution)/shard_map/ppermute | solution.py:46
  73.1 0.0 collective-permute-done.11.got_within
  73.1 4.8 %collective-permute-done.12.got_across = f32[3,2,48,128]{3,2,1,0:T(8,128)S(1)} collective-permute-done((f32[3,2,48,128]{3,2,1,0:T(8,128)S(1)}, f32[3,2,48,128]{3,2,1,0:T(8,128)S(1)}, u32[]{:S(2)}, u32[]{:S(2)}) %collective-permute-start.12) | collective-permute-done | bytes 147488 | tf_op jit(solution)/shard_map/ppermute | solution.py:46
  77.9 1.0 %shard_map.65 = (f32[3,4,32,128]{3,2,1,0:T(8,128)}, f32[3,4,32,128]{3,2,1,0:T(8,128)}) custom-call(s32[1]{0:T(128)} %bitcast.side, f32[3,6,64,128]{3,2,1,0:T(8,128)S(1)} %get-tuple-element.21.omega, f32[3,4,64,128]{3,2,1,0:T(8,128)S(1)} %get-tuple-element.31.potential, f32[3,2,48,128]{3,2,1,0:T(8,128)S(1)} %collective-permute-done.11.got_within, ...), custom_call_target="tpu_custom_call" | custom-call | tf_op jit(solution)/shard_map/pallas_call | solution.py:446
  (5 shorter events, 0.1 us)
Async XLA Ops:
  0.6 0.7 copy-start.2
  4.5 7.1 %copy-start.3 = (s32[17408]{0:T(1024)S(1)}, s32[17408]{0:T(1024)}, u32[]{:S(2)}) copy-start(s32[17408]{0:T(1024)} %param.4) | copy-start | bytes 208900
  5.3 0.8 slice-start.1
  5.3 0.8 slice-start
  5.3 6.4 %copy-start = (f32[3,17408]{1,0:T(4,128)S(1)}, f32[3,17408]{1,0:T(4,128)}, u32[]{:S(2)}) copy-start(f32[3,17408]{1,0:T(4,128)} %offset_hbm.1) | copy-start | bytes 626692
  6.2 17.8 %collective-permute-start.1 = (f32[7,1024]{1,0:T(8,128)S(1)}, f32[7,1024]{1,0:T(8,128)S(1)}, u32[]{:S(2)}, u32[]{:S(2)}) collective-permute-start(f32[7,1024]{1,0:T(8,128)S(1)} %get-tuple-element.34), channel_id=1, source_target_pairs={{0,30},{2,4},{4,2},{6,8},{8,6},{10,12},{12,10},{14,16},{16,14},{18... | collective-permute-start | bytes 86024 | tf_op jit(solution)/shard_map/ppermute | solution.py:46
  11.6 12.3 %collective-permute-start = (f32[7,1024]{1,0:T(8,128)S(1)}, f32[7,1024]{1,0:T(8,128)S(1)}, u32[]{:S(2)}, u32[]{:S(2)}) collective-permute-start(f32[7,1024]{1,0:T(8,128)S(1)} %get-tuple-element.35), channel_id=1, source_target_pairs={{0,2},{2,0},{4,6},{6,4},{8,10},{10,8},{12,14},{14,12},{16,18},{18,... | collective-permute-start | bytes 86024 | tf_op jit(solution)/shard_map/ppermute | solution.py:47
  11.6 1.0 %copy-start.1 = (f32[3,17408]{1,0:T(4,128)S(1)}, f32[3,17408]{1,0:T(4,128)}, u32[]{:S(2)}) copy-start(f32[3,17408]{1,0:T(4,128)} %vort_hbm.1) | copy-start | bytes 626692
  25.6 7.7 %collective-permute-start.2 = (f32[3,3,40,128]{3,2,1,0:T(8,128)S(1)}, f32[3,3,40,128]{3,2,1,0:T(8,128)S(1)}, u32[]{:S(2)}, u32[]{:S(2)}) collective-permute-start(f32[3,3,40,128]{3,2,1,0:T(8,128)S(1)} %get-tuple-element.19), channel_id=1, source_target_pairs={{0,30},{2,4},{4,2},{6,8},{8,6},{10,12},{12,10},{14,16},{16,14},{18... | collective-permute-start | bytes 552968 | tf_op jit(solution)/shard_map/ppermute | solution.py:46
  26.4 6.9 %collective-permute-start.3 = (f32[3,3,40,128]{3,2,1,0:T(8,128)S(1)}, f32[3,3,40,128]{3,2,1,0:T(8,128)S(1)}, u32[]{:S(2)}, u32[]{:S(2)}) collective-permute-start(f32[3,3,40,128]{3,2,1,0:T(8,128)S(1)} %get-tuple-element.20), channel_id=1, source_target_pairs={{0,2},{2,0},{4,6},{6,4},{8,10},{10,8},{12,14},{14,12},{16,18},{18,... | collective-permute-start | bytes 552968 | tf_op jit(solution)/shard_map/ppermute | solution.py:47
  33.4 8.4 %collective-permute-start.4 = (f32[3,6,40,128]{3,2,1,0:T(8,128)S(1)}, f32[3,6,40,128]{3,2,1,0:T(8,128)S(1)}, u32[]{:S(2)}, u32[]{:S(2)}) collective-permute-start(f32[3,6,40,128]{3,2,1,0:T(8,128)S(1)} %pad_add_fusion.mine), channel_id=1, source_target_pairs={{0,1},{1,0},{2,3},{3,2},{4,5},{5,4},{6,7},{7,6},{8,9},{9,8},{10,11... | collective-permute-start | bytes 1105928 | tf_op jit(solution)/shard_map/ppermute | solution.py:421
  42.9 2.6 %collective-permute-start.5 = (f32[3,2,64,128]{3,2,1,0:T(8,128)S(1)}, f32[3,2,64,128]{3,2,1,0:T(8,128)S(1)}, u32[]{:S(2)}, u32[]{:S(2)}) collective-permute-start(f32[3,2,64,128]{3,2,1,0:T(8,128)S(1)} %get-tuple-element.23), channel_id=1, source_target_pairs={{0,2},{2,0},{4,6},{6,4},{8,10},{10,8},{12,14},{14,12},{16,18},{18,... | collective-permute-start | bytes 589832 | tf_op jit(solution)/shard_map/ppermute | solution.py:47
  43.0 7.9 %collective-permute-start.6 = (f32[3,2,64,128]{3,2,1,0:T(8,128)S(1)}, f32[3,2,64,128]{3,2,1,0:T(8,128)S(1)}, u32[]{:S(2)}, u32[]{:S(2)}) collective-permute-start(f32[3,2,64,128]{3,2,1,0:T(8,128)S(1)} %get-tuple-element.24), channel_id=1, source_target_pairs={{0,30},{2,4},{4,2},{6,8},{8,6},{10,12},{12,10},{14,16},{16,14},{18... | collective-permute-start | bytes 589832 | tf_op jit(solution)/shard_map/ppermute | solution.py:46
  52.5 2.6 %collective-permute-start.7 = (f32[3,2,48,128]{3,2,1,0:T(8,128)S(1)}, f32[3,2,48,128]{3,2,1,0:T(8,128)S(1)}, u32[]{:S(2)}, u32[]{:S(2)}) collective-permute-start(f32[3,2,48,128]{3,2,1,0:T(8,128)S(1)} %get-tuple-element.26), channel_id=1, source_target_pairs={{0,2},{2,0},{4,6},{6,4},{8,10},{10,8},{12,14},{14,12},{16,18},{18,... | collective-permute-start | bytes 442376 | tf_op jit(solution)/shard_map/ppermute | solution.py:47
  52.6 7.3 %collective-permute-start.8 = (f32[3,2,48,128]{3,2,1,0:T(8,128)S(1)}, f32[3,2,48,128]{3,2,1,0:T(8,128)S(1)}, u32[]{:S(2)}, u32[]{:S(2)}) collective-permute-start(f32[3,2,48,128]{3,2,1,0:T(8,128)S(1)} %get-tuple-element.27), channel_id=1, source_target_pairs={{0,30},{2,4},{4,2},{6,8},{8,6},{10,12},{12,10},{14,16},{16,14},{18... | collective-permute-start | bytes 442376 | tf_op jit(solution)/shard_map/ppermute | solution.py:46
  61.5 2.6 %collective-permute-start.9 = (f32[3,2,48,128]{3,2,1,0:T(8,128)S(1)}, f32[3,2,48,128]{3,2,1,0:T(8,128)S(1)}, u32[]{:S(2)}, u32[]{:S(2)}) collective-permute-start(f32[3,2,48,128]{3,2,1,0:T(8,128)S(1)} %get-tuple-element.29), channel_id=1, source_target_pairs={{0,2},{2,0},{4,6},{6,4},{8,10},{10,8},{12,14},{14,12},{16,18},{18,... | collective-permute-start | bytes 442376 | tf_op jit(solution)/shard_map/ppermute | solution.py:47
  61.6 7.3 %collective-permute-start.10 = (f32[3,2,48,128]{3,2,1,0:T(8,128)S(1)}, f32[3,2,48,128]{3,2,1,0:T(8,128)S(1)}, u32[]{:S(2)}, u32[]{:S(2)}) collective-permute-start(f32[3,2,48,128]{3,2,1,0:T(8,128)S(1)} %get-tuple-element.30), channel_id=1, source_target_pairs={{0,30},{2,4},{4,2},{6,8},{8,6},{10,12},{12,10},{14,16},{16,14},{18... | collective-permute-start | bytes 442376 | tf_op jit(solution)/shard_map/ppermute | solution.py:46
  70.5 2.6 %collective-permute-start.11 = (f32[3,2,48,128]{3,2,1,0:T(8,128)S(1)}, f32[3,2,48,128]{3,2,1,0:T(8,128)S(1)}, u32[]{:S(2)}, u32[]{:S(2)}) collective-permute-start(f32[3,2,48,128]{3,2,1,0:T(8,128)S(1)} %get-tuple-element.32), channel_id=1, source_target_pairs={{0,2},{2,0},{4,6},{6,4},{8,10},{10,8},{12,14},{14,12},{16,18},{18,... | collective-permute-start | bytes 442376 | tf_op jit(solution)/shard_map/ppermute | solution.py:47
  70.6 7.3 %collective-permute-start.12 = (f32[3,2,48,128]{3,2,1,0:T(8,128)S(1)}, f32[3,2,48,128]{3,2,1,0:T(8,128)S(1)}, u32[]{:S(2)}, u32[]{:S(2)}) collective-permute-start(f32[3,2,48,128]{3,2,1,0:T(8,128)S(1)} %get-tuple-element.33), channel_id=1, source_target_pairs={{0,30},{2,4},{4,2},{6,8},{8,6},{10,12},{12,10},{14,16},{16,14},{18... | collective-permute-start | bytes 442376 | tf_op jit(solution)/shard_map/ppermute | solution.py:46

commit v2 on v1

--- a/solution.py
+++ b/solution.py
@@ -17,7 +17,7 @@
 ROWS = CY + 8
 PLANES = CX + 3
 SPREAD = 288
-QUANTITIES = 31
+QUANTITIES = 25
 VMEM_BYTES = 48 * 1024 * 1024
 
 
@@ -31,6 +31,10 @@
 
 def params():
     return pltpu.CompilerParams(vmem_limit_bytes=VMEM_BYTES)
+
+
+def is_even():
+    return lax.axis_index("gx") % 2 == 0
 
 
 def across(n):
@@ -68,38 +72,53 @@
         for tap in range(4):
             along = jnp.where(cell_x == plane - tap, weight_x[tap], along)
         table[plane, rows] = along
+    table[11, rows] = (cell_y - 1).astype(F32)
+    table[12, rows] = ((cell_z - 1) & (NZ - 1)).astype(F32)
     for tap in range(4):
-        node_y = cell_y + (tap - 1)
-        if tap == 0:
-            node_y = jnp.where(cell_y == 0, ROWS - 1, node_y)
         table[7 + tap, rows] = weight_y[tap]
-        table[11 + tap, rows] = node_y.astype(F32)
-        table[15 + tap, rows] = ((cell_z + (tap - 1)) & (NZ - 1)).astype(F32)
         for comp in range(3):
-            table[19 + tap * 3 + comp, rows] = weight_z[tap] * strengths[comp]
+            table[13 + tap * 3 + comp, rows] = weight_z[tap] * strengths[comp]
 
 
 def spread(table, first, tiles, planes, lines):
-    row_ids = lax.broadcasted_iota(jnp.int32, (ROWS, 128), 0).astype(F32)
-    z_ids = lax.broadcasted_iota(jnp.int32, (NZ, 128), 0).astype(F32).astype(BF16)
+    ids = lax.broadcasted_iota(jnp.int32, (8, 128), 0)
+    zero = jnp.zeros((8, 128), F32)
+    half = lax.broadcasted_iota(jnp.int32, (16, 128), 0) // 8
+    none = jnp.zeros((16, 128), BF16)
     for tile in range(tiles):
         lanes = slice(tile * 128, (tile + 1) * 128)
 
         def figure(k):
             return table[k, pl.ds(first + tile, 1)]
 
-        along_y = jnp.zeros((ROWS, 128), F32)
+        first_row = figure(11).astype(jnp.int32)
+        tap_of = (ids - first_row) & 7
+        row = first_row + tap_of
+        row_tile = jnp.where(row < 0, CY // 8, row >> 3)
+        taps = zero
         for tap in range(4):
-            along_y = jnp.where(row_ids == figure(11 + tap), figure(7 + tap), along_y)
-        parts = [figure(plane) * along_y for plane in range(PLANES)]
-        parts.append(jnp.zeros((SPREAD - PLANES * ROWS, 128), F32))
+            taps = jnp.where(tap_of == tap, figure(7 + tap), taps)
+        along_y = [jnp.where(row_tile == k, taps, 0.0) for k in range(ROWS // 8)]
+        parts = [figure(plane) * piece for plane in range(PLANES) for piece in along_y]
+        parts += [zero] * ((SPREAD - PLANES * ROWS) // 8)
         planes[:, lanes] = jnp.concatenate(parts, axis=0).astype(BF16)
-        masks = [z_ids == figure(15 + tap).astype(BF16) for tap in range(4)]
+
+        first_z = figure(12).astype(jnp.int32)
+        tap_of = (ids - first_z) & 7
+        z_tile = (((first_z + tap_of) & (NZ - 1)) >> 3).astype(F32)
+        where_tap = [tap_of == tap for tap in range(4)]
+        pair = (jnp.concatenate([z_tile, z_tile], axis=0) - half.astype(F32)).astype(BF16)
+        doubled = []
         for comp in range(3):
-            line = jnp.zeros((NZ, 128), BF16)
+            taps = zero
             for tap in range(4):
-                line = jnp.where(masks[tap], figure(19 + tap * 3 + comp).astype(BF16), line)
-            lines[comp * NZ : (comp + 1) * NZ, lanes] = line
+                taps = jnp.where(where_tap[tap], figure(13 + tap * 3 + comp), taps)
+            doubled.append(jnp.concatenate([taps, taps], axis=0).astype(BF16))
+        for k in range(NZ // 16):
+            here = pair == jnp.asarray(2.0 * k, BF16)
+            for comp in range(3):
+                start = comp * NZ + 16 * k
+                lines[start : start + 16, lanes] = jnp.where(here, doubled[comp], none)
 
 
 def product(planes, lines):
@@ -108,13 +127,9 @@
     )
 
 
-def staying_kernel(
-    limits, cell_hbm, offset_hbm, vort_hbm, total, cells, offsets, vorts, dense, table,
-    planes_a, lines_a, planes_b, lines_b, sems, *, tiles_per_chunk,
+def leaving_kernel(
+    moving, cell_hbm, offset_hbm, vort_hbm, cells, offsets, vorts, to_within, to_across, packed, sems, *, capacity
 ):
-    first_stay = limits[0] + limits[1]
-    live_len = limits[2]
-    tiles = cells.shape[0]
     copies = [
         pltpu.make_async_copy(offset_hbm, offsets, sems.at[0]),
         pltpu.make_async_copy(vort_hbm, vorts, sems.at[1]),
@@ -122,9 +137,54 @@
     ]
     for copy in copies:
         copy.start()
-    total[...] = jnp.zeros_like(total)
+    even = is_even()
+    prev_count = moving[0, 0]
+    next_count = moving[0, 1]
     for copy in copies:
         copy.wait()
+    room = 2 * capacity
+    packed[0:3] = offsets[:, :room]
+    packed[3:6] = vorts[:, :room]
+    for tile in range(room // 128):
+        packed[6:7, tile * 128 : (tile + 1) * 128] = cells[tile : tile + 1].astype(F32)
+    packed[7:8] = jnp.zeros((1, room), F32)
+    ids = lax.broadcasted_iota(jnp.int32, (8, capacity), 1)
+    listed = packed[...]
+    shifted = pltpu.roll(listed, (room - prev_count) % room, 1)
+    for_prev = jnp.where(ids < prev_count, listed[:, :capacity], 0.0)
+    for_next = jnp.where(ids < next_count, shifted[:, :capacity], 0.0)
+    to_within[...] = jnp.where(even, for_next, for_prev)
+    to_across[...] = jnp.where(even, for_prev, for_next)
+
+
+def pack_leaving(part_cell, part_offset, part_vort, moving):
+    slots = part_cell.shape[0]
+    capacity = slots // 17
+    tiles = slots // 128
+    message = jax.ShapeDtypeStruct((8, capacity), F32)
+    return pl.pallas_call(
+        functools.partial(leaving_kernel, capacity=capacity),
+        in_specs=[in_smem()] + [pl.BlockSpec(memory_space=pltpu.HBM)] * 3,
+        out_specs=tuple(in_vmem(5)),
+        out_shape=(
+            jax.ShapeDtypeStruct((tiles, 128), jnp.int32),
+            jax.ShapeDtypeStruct((3, slots), F32),
+            jax.ShapeDtypeStruct((3, slots), F32),
+            message,
+            message,
+        ),
+        scratch_shapes=[pltpu.VMEM((8, 2 * capacity), F32), pltpu.SemaphoreType.DMA((3,))],
+        compiler_params=params(),
+    )(moving, part_cell.reshape(tiles, 128), part_offset, part_vort)
+
+
+def staying_kernel(
+    moving, cells, offsets, vorts, total, dense, table, planes_a, lines_a, planes_b, lines_b, *, tiles_per_chunk
+):
+    first_stay = moving[0, 0] + moving[0, 1]
+    live_len = moving[0, 2]
+    tiles = cells.shape[0]
+    total[...] = jnp.zeros_like(total)
     for tile in range(tiles):
         lanes = slice(tile * 128, (tile + 1) * 128)
         for dim in range(3):
@@ -168,33 +228,29 @@
         total[...] += product(planes_a, lines_a)
 
 
-def deposit_staying(part_cell, part_offset, part_vort, limits):
-    slots = part_cell.shape[0]
-    tiles = slots // 128
+def deposit_staying(cells, offsets, vorts, moving):
+    tiles = cells.shape[0]
+    slots = tiles * 128
     per_chunk = 17
     chunk = per_chunk * 128
     return pl.pallas_call(
         functools.partial(staying_kernel, tiles_per_chunk=per_chunk),
-        in_specs=[in_smem()] + [pl.BlockSpec(memory_space=pl.ANY)] * 3,
+        in_specs=[in_smem()] + in_vmem(3),
         out_specs=in_vmem(1)[0],
         out_shape=jax.ShapeDtypeStruct((SPREAD, 3 * NZ), F32),
         scratch_shapes=[
-            pltpu.VMEM((tiles, 128), jnp.int32),
-            pltpu.VMEM((3, slots), F32),
-            pltpu.VMEM((3, slots), F32),
             pltpu.VMEM((6, tiles, 128), F32),
             pltpu.VMEM((QUANTITIES, tiles, 128), F32),
         ]
-        + [pltpu.VMEM((SPREAD, chunk), BF16), pltpu.VMEM((3 * NZ, chunk), BF16)] * 2
-        + [pltpu.SemaphoreType.DMA((3,))],
+        + [pltpu.VMEM((SPREAD, chunk), BF16), pltpu.VMEM((3 * NZ, chunk), BF16)] * 2,
         compiler_params=params(),
         cost_estimate=pl.CostEstimate(
             flops=2 * SPREAD * 3 * NZ * slots, bytes_accessed=28 * slots, transcendentals=0
         ),
-    )(limits, part_cell.reshape(tiles, 128), part_offset, part_vort)
-
-
-def arrived_kernel(side, total, got_within, got_across, deposits, to_within, to_across, dense, table, planes, lines):
+    )(moving, cells, offsets, vorts)
+
+
+def arrived_kernel(total, got_within, got_across, deposits, to_within, to_across, dense, table, planes, lines):
     tiles = got_within.shape[1] // 128
     for which, got in enumerate((got_within, got_across)):
         for tile in range(tiles):
@@ -218,19 +274,20 @@
             deposits[comp, plane] = whole[
                 plane * ROWS : (plane + 1) * ROWS, comp * NZ : (comp + 1) * NZ
             ]
-    first_within = jnp.where(side[0] == 0, CX, 0)
-    first_across = jnp.where(side[0] == 0, 0, CX)
+    even = is_even()
+    first_within = jnp.where(even, CX, 0)
+    first_across = jnp.where(even, 0, CX)
     to_within[...] = deposits[:, pl.ds(first_within, 3)]
     to_across[...] = deposits[:, pl.ds(first_across, 3)]
 
 
-def deposit_arrived(side, total, got_within, got_across):
+def deposit_arrived(total, got_within, got_across):
     received = got_within.shape[1]
     edge = jax.ShapeDtypeStruct((3, 3, ROWS, NZ), F32)
     tiles = 2 * received // 128
     return pl.pallas_call(
         arrived_kernel,
-        in_specs=[in_smem()] + in_vmem(3),
+        in_specs=in_vmem(3),
         out_specs=tuple(in_vmem(3)),
         out_shape=(jax.ShapeDtypeStruct((3, PLANES, ROWS, NZ), F32), edge, edge),
         scratch_shapes=[
@@ -240,20 +297,7 @@
             pltpu.VMEM((3 * NZ, 2 * received), BF16),
         ],
         compiler_params=params(),
-    )(side, total, got_within, got_across)
-
-
-def leaving(part_cell, part_offset, part_vort, limits):
-    capacity = part_cell.shape[0] // 17
-    room = 2 * capacity
-    packed = jnp.concatenate(
-        [part_offset[:, :room], part_vort[:, :room], part_cell[:room].astype(F32)[None]], axis=0
-    )
-    ids = jnp.arange(capacity, dtype=jnp.int32)[None]
-    to_prev = jnp.where(ids < limits[0], packed[:, :capacity], 0.0)
-    shifted = lax.dynamic_slice_in_dim(packed, limits[0], capacity, 1)
-    to_next = jnp.where(ids < limits[1], shifted, 0.0)
-    return to_prev, to_next
+    )(total, got_within, got_across)
 
 
 def edge_rows(low, high):
@@ -288,20 +332,54 @@
     return fields[2 : CX + 2]
 
 
-def hand_out(side, potential, to_within, to_across):
-    first_within = jnp.where(side[0] == 0, CX - 2, 0)
-    first_across = jnp.where(side[0] == 0, 0, CX - 2)
+def pack_rows(a, b, rows):
+    ids = lax.broadcasted_iota(jnp.int32, (8, NZ), 0)
+    first, last = b[:8], b[CY - 8 :]
+    if rows == CY + 8:
+        return jnp.concatenate([a, jnp.where(ids < 4, first, last)], axis=0)
+    if rows == CY + 16:
+        return jnp.concatenate([a, first, last], axis=0)
+    middle = jnp.where(ids < 4, b[8:16], b[CY - 16 : CY - 8])
+    return jnp.concatenate([a, first, middle, last], axis=0)
+
+
+def unpack_rows(packed):
+    a, rest = packed[:CY], packed[CY:]
+    first, last = rest[:8], rest[rest.shape[0] - 8 :]
+    middle = rest[8:16] if rest.shape[0] == 24 else last
+    return a, jnp.concatenate([first, middle, middle, last], axis=0)
+
+
+def hand_out(potential, to_within, to_across):
+    even = is_even()
     rows = to_within.shape[2]
-    if rows == 2 * CY:
-        to_within[...] = potential[:, pl.ds(first_within, 2)]
-        to_across[...] = potential[:, pl.ds(first_across, 2)]
-    else:
-        for first, out in ((first_within, to_within), (first_across, to_across)):
-            out[:, :, : CY + 8] = potential[:, pl.ds(first, 2), : CY + 8]
-            out[:, :, CY + 8 :] = potential[:, pl.ds(first, 2), 2 * CY - 8 :]
-
-
-def first_kernel(side, mine, other, omega, potential, to_within, to_across):
+    for comp in range(3):
+        for x in range(2):
+            low, high = (
+                pack_rows(potential[comp, at, :CY], potential[comp, at, CY:], rows)
+                for at in (x, CX - 2 + x)
+            )
+            to_within[comp, x] = jnp.where(even, high, low)
+            to_across[comp, x] = jnp.where(even, low, high)
+
+
+def fold_kernel(deposits, got_within, got_across, mine, message):
+    even = is_even()
+    ids = lax.broadcasted_iota(jnp.int32, (8, NZ), 0)
+    for comp in range(3):
+        for x in range(CX + 2):
+            value = deposits[comp, x]
+            if x < 3:
+                value = value + jnp.where(even, got_across[comp, x], got_within[comp, x])
+            if x >= CX:
+                value = value + jnp.where(even, got_within[comp, x - CX], got_across[comp, x - CX])
+            mine[comp, x] = value
+            edges = value[CY:]
+            third = jnp.where(ids < 2, edges, jnp.where(ids == 2, roll_rows(edges, 3), value[16:24]))
+            message[comp, x] = jnp.concatenate([value[:16], third, value[24:CY]], axis=0)
+
+
+def first_kernel(mine, other, omega, potential, to_within, to_across):
     ids = lax.broadcasted_iota(jnp.int32, (8, NZ), 0)
 
     def folded(main, edges):
@@ -314,8 +392,10 @@
         for x in range(CX + 2):
             a = mine[comp, x]
             b = other[comp, x]
-            omega_a = folded(a[:CY], b[CY:])
-            omega_b = folded(b[:CY], a[CY:])
+            third = b[16:24]
+            b_edges = jnp.where(ids < 2, third, roll_rows(third, 5))
+            omega_a = folded(a[:CY], b_edges)
+            omega_b = folded(b, a[CY:])
             omega[comp, x, :CY] = omega_a
             omega[comp, x, CY:] = omega_b
             sources[0].append(edged_plane(omega_a, omega_b))
@@ -328,37 +408,24 @@
         return carry
 
     lax.fori_loop(0, 3, one_component, 0)
-    hand_out(side, potential, to_within, to_across)
-
-
-def ring_planes(side, got_within, got_across, comp):
-    even = side[0] == 0
-
-    def both(got, x):
-        value = got[comp, x]
-        if value.shape[0] == 2 * CY:
-            return value[:CY], value[CY:]
-        high = value[CY + 8 :]
-        return value[:CY], jnp.concatenate([value[CY : CY + 8], high, high, high], axis=0)
+    hand_out(potential, to_within, to_across)
+
+
+def gathered(potential, got_within, got_across, comp):
+    even = is_even()
 
     def chosen(pick, x):
-        inner, outer = both(got_within, x), both(got_across, x)
-        return tuple(jnp.where(pick, a, b) for a, b in zip(inner, outer))
+        return unpack_rows(jnp.where(pick, got_within[comp, x], got_across[comp, x]))
 
     below = [chosen(jnp.logical_not(even), x) for x in range(2)]
     above = [chosen(even, x) for x in range(2)]
-    return below, above
-
-
-def gathered(side, potential, got_within, got_across, comp):
-    below, above = ring_planes(side, got_within, got_across, comp)
     middle = [(potential[comp, x, :CY], potential[comp, x, CY:]) for x in range(CX)]
     return below + middle + above
 
 
-def next_kernel(side, omega, before, got_within, got_across, potential, to_within, to_across):
+def next_kernel(omega, before, got_within, got_across, potential, to_within, to_across):
     def one_component(comp, carry):
-        pairs = gathered(side, before, got_within, got_across, comp)
+        pairs = gathered(before, got_within, got_across, comp)
         charge = [(omega[comp, x, :CY], omega[comp, x, CY:]) for x in range(CX + 2)]
         for block in range(2):
             fields = [edged_plane(pair[block], pair[1 - block]) for pair in pairs]
@@ -369,13 +436,13 @@
         return carry
 
     lax.fori_loop(0, 3, one_component, 0)
-    hand_out(side, potential, to_within, to_across)
-
-
-def last_kernel(side, omega, potential, got_within, got_across, velocity, stretching):
+    hand_out(potential, to_within, to_across)
+
+
+def last_kernel(omega, potential, got_within, got_across, velocity, stretching):
     psi = []
     for comp in range(3):
-        pairs = gathered(side, potential, got_within, got_across, comp)
+        pairs = gathered(potential, got_within, got_across, comp)
         psi.append([edged_plane(a, b) for a, b in pairs])
 
     def slope_x(planes, x):
@@ -403,53 +470,44 @@
             )
 
 
-def edge_shape(rows):
-    return jax.ShapeDtypeStruct((3, 2, rows, NZ), F32)
-
-
-def two_block_solve(side, deposits, to_within, to_across):
-    got_within, got_across = swap_x(to_within, to_across)
-    even = side[0] == 0
-    from_prev = jnp.where(even, got_across, got_within)
-    from_next = jnp.where(even, got_within, got_across)[:, :2]
-    none = ((0, 0), (0, 0))
-    mine = (
-        deposits[:, : CX + 2]
-        + jnp.pad(from_prev, ((0, 0), (0, CX - 1)) + none)
-        + jnp.pad(from_next, ((0, 0), (CX, 0)) + none)
-    )
-    other = lax.ppermute(mine, "gy", [(0, 1), (1, 0)])
-    slab = jax.ShapeDtypeStruct((3, CX, 2 * CY, NZ), F32)
-    omega, potential, to_within, to_across = pl.pallas_call(
-        first_kernel,
-        in_specs=[in_smem()] + in_vmem(2),
-        out_specs=tuple(in_vmem(4)),
-        out_shape=(
-            jax.ShapeDtypeStruct((3, CX + 2, 2 * CY, NZ), F32),
-            slab,
-            edge_shape(2 * CY),
-            edge_shape(2 * CY),
-        ),
+def array(*shape):
+    return jax.ShapeDtypeStruct(shape, F32)
+
+
+def on_vmem(kernel, outs, *args):
+    return pl.pallas_call(
+        kernel,
+        in_specs=in_vmem(len(args)),
+        out_specs=tuple(in_vmem(len(outs))),
+        out_shape=outs,
         compiler_params=params(),
-    )(side, mine, other)
-    for _ in range(1, OUTER):
-        got_within, got_across = swap_x(to_within, to_across)
-        potential, to_within, to_across = pl.pallas_call(
-            next_kernel,
-            in_specs=[in_smem()] + in_vmem(4),
-            out_specs=tuple(in_vmem(3)),
-            out_shape=(slab, edge_shape(CY + 16), edge_shape(CY + 16)),
-            compiler_params=params(),
-        )(side, omega, potential, got_within, got_across)
-    got_within, got_across = swap_x(to_within, to_across)
-    block = jax.ShapeDtypeStruct((3, CX, CY, NZ), F32)
-    return pl.pallas_call(
-        last_kernel,
-        in_specs=[in_smem()] + in_vmem(4),
-        out_specs=tuple(in_vmem(2)),
-        out_shape=(block, block),
-        compiler_params=params(),
-    )(side, omega, potential, got_within, got_across)
+    )(*args)
+
+
+def two_block_solve(deposits, to_within, to_across):
+    planes = CX + 2
+    mine, message = on_vmem(
+        fold_kernel,
+        (array(3, planes, ROWS, NZ), array(3, planes, CY, NZ)),
+        deposits,
+        *swap_x(to_within, to_across),
+    )
+    other = lax.ppermute(message, "gy", [(0, 1), (1, 0)])
+    slab = array(3, CX, 2 * CY, NZ)
+    depths = [CY + 24, CY + 16, CY + 16, CY + 8]
+    edge = array(3, 2, depths[0], NZ)
+    omega, potential, to_within, to_across = on_vmem(
+        first_kernel, (array(3, planes, 2 * CY, NZ), slab, edge, edge), mine, other
+    )
+    for depth in depths[1:]:
+        edge = array(3, 2, depth, NZ)
+        potential, to_within, to_across = on_vmem(
+            next_kernel, (slab, edge, edge), omega, potential, *swap_x(to_within, to_across)
+        )
+    block = array(3, CX, CY, NZ)
+    return on_vmem(
+        last_kernel, (block, block), omega, potential, *swap_x(to_within, to_across)
+    )
 
 
 def padded(value, sides, width):
@@ -536,17 +594,14 @@
 
 
 def per_device(part_cell, part_offset, part_vort, moving):
-    limits = moving[0]
-    side = (lax.axis_index("gx") % 2).astype(jnp.int32)[None]
-    even = side[0] == 0
-    to_prev, to_next = leaving(part_cell, part_offset, part_vort, limits)
-    got_within, got_across = swap_x(
-        jnp.where(even, to_next, to_prev), jnp.where(even, to_prev, to_next)
-    )
-    total = deposit_staying(part_cell, part_offset, part_vort, limits)
-    deposits, to_within, to_across = deposit_arrived(side, total, got_within, got_across)
+    cells, offsets, vorts, to_within, to_across = pack_leaving(
+        part_cell, part_offset, part_vort, moving
+    )
+    got_within, got_across = swap_x(to_within, to_across)
+    total = deposit_staying(cells, offsets, vorts, moving)
+    deposits, to_within, to_across = deposit_arrived(total, got_within, got_across)
     if lax.axis_size("gy") == 2:
-        return two_block_solve(side, deposits, to_within, to_across)
+        return two_block_solve(deposits, to_within, to_across)
     return general_solve(deposits)
 
 

time: 79.1 us -> 72.3 us (0.914)
  Pallas kernels: 19.9 us -> 17.5 us
  other arithmetic: 2.27 us -> 0 us
  between operations: 2.79 us -> 0.76 us
  starting transfers between devices: 18.2 us -> 16.6 us
  local copies, waits for them, and re-layouts: 2.27 us -> 3.44 us
    pallas_call x1, Pallas kernels: 11.3 us -> 8.54 us  [deposit_staying(): pl.pallas_call(functools.partial(staying_kernel, tiles_per_chunk=per_chun...]
    ppermute x6, starting transfers between devices: 16.3 us -> 14.1 us  [swap_x(): got_across = lax.ppermute(to_across, 'gx', across(n))]
    unnamed x8, local copies, waits for them, and re-layouts: 1.61 us -> 3.44 us
    ppermute x1, waiting for transfers between devices: 6.77 us -> 5.2 us  [two_block_solve(): other = lax.ppermute(message, 'gy', [(0, 1), (1, 0)])]
    lt x1 -> x0, other arithmetic: 1.3 us -> none  [leaving(): to_prev = jnp.where(ids < limits[0], packed[:, :capacity], 0.0)]
    ppermute x6, waiting for transfers between devices: 26.7 us -> 27.8 us  [swap_x(): got_across = lax.ppermute(to_across, 'gx', across(n))]
    pallas_call x6 -> x8, Pallas kernels: 8.51 us -> 8.97 us  [the longest x6 6.95 us: on_vmem(): pl.pallas_call(kernel, in_specs=in_vmem(len(args)), out_specs=tuple(in_vm...]
  transfers between devices with their start and end apart: 13 -> 13, of which waited for: 6 -> 7; matrix products, arithmetic and copies ran while one was open for 0% -> 0% of each run, Pallas kernels for 14% -> 12%
where the time goes in v2:
time: 72.3 us; the launch traced here: 72.1 us
  waiting for transfers between devices  33.8 us (47%)
  Pallas kernels  17.5 us (24%)
  starting transfers between devices  16.6 us (23%)
  local copies, waits for them, and re-layouts  3.44 us (5%)
  between operations  0.76 us (1%)
    ppermute x6, waiting for transfers between devices, swap_x(): got_across = lax.ppermute(to_across, 'gx', across(n))  27.8 us
    ppermute x6, starting transfers between devices, swap_x(): got_across = lax.ppermute(to_across, 'gx', across(n))  14.1 us
    pallas_call x1, Pallas kernels, deposit_staying(): pl.pallas_call(functools.partial(staying_kernel, tiles_per_chunk=per_chun...  8.54 us
    pallas_call x6, Pallas kernels, on_vmem(): pl.pallas_call(kernel, in_specs=in_vmem(len(args)), out_specs=tuple(in_vm...  6.95 us
    ppermute x1, waiting for transfers between devices, two_block_solve(): other = lax.ppermute(message, 'gy', [(0, 1), (1, 0)])  5.2 us
    unnamed x8, local copies, waits for them, and re-layouts  3.44 us
    ppermute x1, starting transfers between devices, two_block_solve(): other = lax.ppermute(message, 'gy', [(0, 1), (1, 0)])  1.58 us
  transfers between devices with their start and end apart: 13, of which 7 were waited for; matrix products, arithmetic and copies ran while one was open for 0% of the time, Pallas kernels for 12%

profile of v2, /device:TPU:0, one launch (start us, length us, event | category | flops | bytes accessed | tf_op | source)
XLA Modules:
  0.0 72.1 jit_solution(6280254651103479359)
XLA Ops:
  0.6 0.0 copy-start.3
  0.6 0.6 copy-done.3
  1.3 0.0 copy-start
  1.3 1.0 %copy-done = f32[3,17408]{1,0:T(4,128)S(1)} copy-done((f32[3,17408]{1,0:T(4,128)S(1)}, f32[3,17408]{1,0:T(4,128)}, u32[]{:S(2)}) %copy-start) | copy-done | bytes 208920
  2.2 0.0 copy-start.1
  2.2 1.0 %copy-done.1 = f32[3,17408]{1,0:T(4,128)S(1)} copy-done((f32[3,17408]{1,0:T(4,128)S(1)}, f32[3,17408]{1,0:T(4,128)}, u32[]{:S(2)}) %copy-start.1) | copy-done | bytes 208920
  3.2 0.0 copy-start.2
  3.2 0.9 %copy-done.2 = s32[17408]{0:T(1024)S(1)} copy-done((s32[17408]{0:T(1024)S(1)}, s32[17408]{0:T(1024)}, u32[]{:S(2)}) %copy-start.2) | copy-done | bytes 69656
  4.1 0.9 %shard_map.59 = (s32[136,128]{1,0:T(8,128)S(1)}, f32[3,17408]{1,0:T(4,128)S(1)}, f32[3,17408]{1,0:T(4,128)S(1)}, f32[8,1024]{1,0:T(8,128)S(1)}, f32[8,1024]{1,0:T(8,128)S(1)}) custom-call(s32[1,3]{1,0:T(1,128)S(1)} %copy-done.3, s32[136,128]{1,0:T(8,128)S(1)} %bitcast.1, f32[3,17408]{1,0:T(4,128)S(1)} %copy-done, f32[3,17408]{1,0:T(4,128)S(1)} %copy-done.1), custom_call_target="tpu_custom_call" | custom-call | tf_op jit(solution)/shard_map/pallas_call | solution.py:165
  5.0 0.5 collective-permute-start
  5.5 5.6 %collective-permute-start.1 = (f32[8,1024]{1,0:T(8,128)S(1)}, f32[8,1024]{1,0:T(8,128)S(1)}, u32[]{:S(2)}, u32[]{:S(2)}) collective-permute-start(f32[8,1024]{1,0:T(8,128)S(1)} %get-tuple-element.29), channel_id=1, source_target_pairs={{0,30},{2,4},{4,2},{6,8},{8,6},{10,12},{12,10},{14,16},{16,14},{18... | collective-permute-start | bytes 98312 | tf_op jit(solution)/shard_map/ppermute | solution.py:50
  11.1 8.5 %shard_map.60.total = f32[288,384]{1,0:T(8,128)S(1)} custom-call(s32[1,3]{1,0:T(1,128)S(1)} %copy-done.3, s32[136,128]{1,0:T(8,128)S(1)} %get-tuple-element.25.cells, f32[3,17408]{1,0:T(4,128)S(1)} %get-tuple-element.26.offsets, f32[3,17408]{1,0:T(4,128)S(1)} %get-tuple-element.27.vorts), custom_call_target="tpu_custom_call" | custom-call | flops 3850371072 | bytes 487424 | tf_op jit(solution)/shard_map/pallas_call | solution.py:236
  19.7 0.0 collective-permute-done.got_within
  19.7 0.0 collective-permute-done.1.got_across
  19.7 1.2 %shard_map.61 = (f32[3,7,40,128]{3,2,1,0:T(8,128)S(1)}, f32[3,3,40,128]{3,2,1,0:T(8,128)S(1)}, f32[3,3,40,128]{3,2,1,0:T(8,128)S(1)}) custom-call(f32[288,384]{1,0:T(8,128)S(1)} %shard_map.60.total, f32[8,1024]{1,0:T(8,128)S(1)} %collective-permute-done.got_within, f32[8,1024]{1,0:T(8,128)S(1)} %collective-permute-done.1.got_across), custom_call_target="tpu_custom_call" | custom-call | tf_op jit(solution)/shard_map/pallas_call | solution.py:288
  20.8 0.1 collective-permute-start.2
  20.9 0.6 collective-permute-start.3
  21.5 0.8 %collective-permute-done.2.got_within = f32[3,3,40,128]{3,2,1,0:T(8,128)S(1)} collective-permute-done((f32[3,3,40,128]{3,2,1,0:T(8,128)S(1)}, f32[3,3,40,128]{3,2,1,0:T(8,128)S(1)}, u32[]{:S(2)}, u32[]{:S(2)}) %collective-permute-start.2) | collective-permute-done | bytes 184352 | tf_op jit(solution)/shard_map/ppermute | solution.py:51
  22.3 6.3 %collective-permute-done.3.got_across = f32[3,3,40,128]{3,2,1,0:T(8,128)S(1)} collective-permute-done((f32[3,3,40,128]{3,2,1,0:T(8,128)S(1)}, f32[3,3,40,128]{3,2,1,0:T(8,128)S(1)}, u32[]{:S(2)}, u32[]{:S(2)}) %collective-permute-start.3) | collective-permute-done | bytes 184352 | tf_op jit(solution)/shard_map/ppermute | solution.py:50
  28.6 0.1 shard_map.62
  28.7 1.6 %collective-permute-start.4 = (f32[3,6,32,128]{3,2,1,0:T(8,128)S(1)}, f32[3,6,32,128]{3,2,1,0:T(8,128)S(1)}, u32[]{:S(2)}, u32[]{:S(2)}) collective-permute-start(f32[3,6,32,128]{3,2,1,0:T(8,128)S(1)} %get-tuple-element.34), channel_id=1, source_target_pairs={{0,1},{1,0},{2,3},{3,2},{4,5},{5,4},{6,7},{7,6},{8,9},{9,8},{10,11... | collective-permute-start | bytes 884744 | tf_op jit(solution)/shard_map/ppermute | solution.py:495
  30.3 5.2 %collective-permute-done.4.other = f32[3,6,32,128]{3,2,1,0:T(8,128)S(1)} collective-permute-done((f32[3,6,32,128]{3,2,1,0:T(8,128)S(1)}, f32[3,6,32,128]{3,2,1,0:T(8,128)S(1)}, u32[]{:S(2)}, u32[]{:S(2)}) %collective-permute-start.4) | collective-permute-done | bytes 294944 | tf_op jit(solution)/shard_map/ppermute | solution.py:495
  35.5 1.1 %shard_map.63 = (f32[3,6,64,128]{3,2,1,0:T(8,128)S(1)}, f32[3,4,64,128]{3,2,1,0:T(8,128)S(1)}, f32[3,2,56,128]{3,2,1,0:T(8,128)S(1)}, f32[3,2,56,128]{3,2,1,0:T(8,128)S(1)}) custom-call(f32[3,6,40,128]{3,2,1,0:T(8,128)S(1)} %get-tuple-element.33.mine, f32[3,6,32,128]{3,2,1,0:T(8,128)S(1)} %collective-permute-done.4.other), custom_call_target="tpu_custom_call" | custom-call | tf_op jit(solution)/shard_map/pallas_call | solution.py:478
  36.6 0.1 collective-permute-start.5
  36.7 2.0 %collective-permute-start.6 = (f32[3,2,56,128]{3,2,1,0:T(8,128)S(1)}, f32[3,2,56,128]{3,2,1,0:T(8,128)S(1)}, u32[]{:S(2)}, u32[]{:S(2)}) collective-permute-start(f32[3,2,56,128]{3,2,1,0:T(8,128)S(1)} %get-tuple-element.38), channel_id=1, source_target_pairs={{0,30},{2,4},{4,2},{6,8},{8,6},{10,12},{12,10},{14,16},{16,14},{18... | collective-permute-start | bytes 516104 | tf_op jit(solution)/shard_map/ppermute | solution.py:50
  38.7 0.0 collective-permute-done.5.got_within
  38.7 5.6 %collective-permute-done.6.got_across = f32[3,2,56,128]{3,2,1,0:T(8,128)S(1)} collective-permute-done((f32[3,2,56,128]{3,2,1,0:T(8,128)S(1)}, f32[3,2,56,128]{3,2,1,0:T(8,128)S(1)}, u32[]{:S(2)}, u32[]{:S(2)}) %collective-permute-start.6) | collective-permute-done | bytes 172064 | tf_op jit(solution)/shard_map/ppermute | solution.py:50
  44.3 1.6 %shard_map.64 = (f32[3,4,64,128]{3,2,1,0:T(8,128)S(1)}, f32[3,2,48,128]{3,2,1,0:T(8,128)S(1)}, f32[3,2,48,128]{3,2,1,0:T(8,128)S(1)}) custom-call(f32[3,6,64,128]{3,2,1,0:T(8,128)S(1)} %get-tuple-element.35.omega, f32[3,4,64,128]{3,2,1,0:T(8,128)S(1)} %get-tuple-element.36.before, f32[3,2,56,128]{3,2,1,0:T(8,128)S(1)} %collective-permute-done.5.got_within, ...), custom_call_target="tpu_custom_call" | custom-call | tf_op jit(solution)/shard_map/pallas_call | solution.py:478
  45.9 0.1 collective-permute-start.7
  46.0 2.0 %collective-permute-start.8 = (f32[3,2,48,128]{3,2,1,0:T(8,128)S(1)}, f32[3,2,48,128]{3,2,1,0:T(8,128)S(1)}, u32[]{:S(2)}, u32[]{:S(2)}) collective-permute-start(f32[3,2,48,128]{3,2,1,0:T(8,128)S(1)} %get-tuple-element.41), channel_id=1, source_target_pairs={{0,30},{2,4},{4,2},{6,8},{8,6},{10,12},{12,10},{14,16},{16,14},{18... | collective-permute-start | bytes 442376 | tf_op jit(solution)/shard_map/ppermute | solution.py:50
  47.9 0.0 collective-permute-done.7.got_within
  47.9 5.4 %collective-permute-done.8.got_across = f32[3,2,48,128]{3,2,1,0:T(8,128)S(1)} collective-permute-done((f32[3,2,48,128]{3,2,1,0:T(8,128)S(1)}, f32[3,2,48,128]{3,2,1,0:T(8,128)S(1)}, u32[]{:S(2)}, u32[]{:S(2)}) %collective-permute-start.8) | collective-permute-done | bytes 147488 | tf_op jit(solution)/shard_map/ppermute | solution.py:50
  53.3 1.6 %shard_map.65 = (f32[3,4,64,128]{3,2,1,0:T(8,128)S(1)}, f32[3,2,48,128]{3,2,1,0:T(8,128)S(1)}, f32[3,2,48,128]{3,2,1,0:T(8,128)S(1)}) custom-call(f32[3,6,64,128]{3,2,1,0:T(8,128)S(1)} %get-tuple-element.35.omega, f32[3,4,64,128]{3,2,1,0:T(8,128)S(1)} %get-tuple-element.39.before, f32[3,2,48,128]{3,2,1,0:T(8,128)S(1)} %collective-permute-done.7.got_within, ...), custom_call_target="tpu_custom_call" | custom-call | tf_op jit(solution)/shard_map/pallas_call | solution.py:478
  54.9 0.1 collective-permute-start.9
  55.0 2.0 %collective-permute-start.10 = (f32[3,2,48,128]{3,2,1,0:T(8,128)S(1)}, f32[3,2,48,128]{3,2,1,0:T(8,128)S(1)}, u32[]{:S(2)}, u32[]{:S(2)}) collective-permute-start(f32[3,2,48,128]{3,2,1,0:T(8,128)S(1)} %get-tuple-element.44), channel_id=1, source_target_pairs={{0,30},{2,4},{4,2},{6,8},{8,6},{10,12},{12,10},{14,16},{16,14},{18... | collective-permute-start | bytes 442376 | tf_op jit(solution)/shard_map/ppermute | solution.py:50
  56.9 0.0 collective-permute-done.9.got_within
  57.0 5.4 %collective-permute-done.10.got_across = f32[3,2,48,128]{3,2,1,0:T(8,128)S(1)} collective-permute-done((f32[3,2,48,128]{3,2,1,0:T(8,128)S(1)}, f32[3,2,48,128]{3,2,1,0:T(8,128)S(1)}, u32[]{:S(2)}, u32[]{:S(2)}) %collective-permute-start.10) | collective-permute-done | bytes 147488 | tf_op jit(solution)/shard_map/ppermute | solution.py:50
  62.3 1.6 %shard_map.66 = (f32[3,4,64,128]{3,2,1,0:T(8,128)S(1)}, f32[3,2,40,128]{3,2,1,0:T(8,128)S(1)}, f32[3,2,40,128]{3,2,1,0:T(8,128)S(1)}) custom-call(f32[3,6,64,128]{3,2,1,0:T(8,128)S(1)} %get-tuple-element.35.omega, f32[3,4,64,128]{3,2,1,0:T(8,128)S(1)} %get-tuple-element.42.before, f32[3,2,48,128]{3,2,1,0:T(8,128)S(1)} %collective-permute-done.9.got_within, ...), custom_call_target="tpu_custom_call" | custom-call | tf_op jit(solution)/shard_map/pallas_call | solution.py:478
  63.9 0.1 collective-permute-start.11
  64.0 2.0 %collective-permute-start.12 = (f32[3,2,40,128]{3,2,1,0:T(8,128)S(1)}, f32[3,2,40,128]{3,2,1,0:T(8,128)S(1)}, u32[]{:S(2)}, u32[]{:S(2)}) collective-permute-start(f32[3,2,40,128]{3,2,1,0:T(8,128)S(1)} %get-tuple-element.47), channel_id=1, source_target_pairs={{0,30},{2,4},{4,2},{6,8},{8,6},{10,12},{12,10},{14,16},{16,14},{18... | collective-permute-start | bytes 368648 | tf_op jit(solution)/shard_map/ppermute | solution.py:50
  66.0 0.0 collective-permute-done.11.got_within
  66.0 5.1 %collective-permute-done.12.got_across = f32[3,2,40,128]{3,2,1,0:T(8,128)S(1)} collective-permute-done((f32[3,2,40,128]{3,2,1,0:T(8,128)S(1)}, f32[3,2,40,128]{3,2,1,0:T(8,128)S(1)}, u32[]{:S(2)}, u32[]{:S(2)}) %collective-permute-start.12) | collective-permute-done | bytes 122912 | tf_op jit(solution)/shard_map/ppermute | solution.py:50
  71.1 1.0 %shard_map.67 = (f32[3,4,32,128]{3,2,1,0:T(8,128)}, f32[3,4,32,128]{3,2,1,0:T(8,128)}) custom-call(f32[3,6,64,128]{3,2,1,0:T(8,128)S(1)} %get-tuple-element.35.omega, f32[3,4,64,128]{3,2,1,0:T(8,128)S(1)} %get-tuple-element.45.potential, f32[3,2,40,128]{3,2,1,0:T(8,128)S(1)} %collective-permute-done.11.got_within, ...), custom_call_target="tpu_custom_call" | custom-call | tf_op jit(solution)/shard_map/pallas_call | solution.py:478
Async XLA Ops:
  0.6 0.7 copy-start.3
  1.3 1.0 %copy-start = (f32[3,17408]{1,0:T(4,128)S(1)}, f32[3,17408]{1,0:T(4,128)}, u32[]{:S(2)}) copy-start(f32[3,17408]{1,0:T(4,128)} %offset_hbm.1) | copy-start | bytes 626692
  2.2 1.0 %copy-start.1 = (f32[3,17408]{1,0:T(4,128)S(1)}, f32[3,17408]{1,0:T(4,128)}, u32[]{:S(2)}) copy-start(f32[3,17408]{1,0:T(4,128)} %vort_hbm.1) | copy-start | bytes 626692
  3.2 0.9 %copy-start.2 = (s32[17408]{0:T(1024)S(1)}, s32[17408]{0:T(1024)}, u32[]{:S(2)}) copy-start(s32[17408]{0:T(1024)} %param.4) | copy-start | bytes 208900
  5.0 14.7 %collective-permute-start = (f32[8,1024]{1,0:T(8,128)S(1)}, f32[8,1024]{1,0:T(8,128)S(1)}, u32[]{:S(2)}, u32[]{:S(2)}) collective-permute-start(f32[8,1024]{1,0:T(8,128)S(1)} %get-tuple-element.28), channel_id=1, source_target_pairs={{0,2},{2,0},{4,6},{6,4},{8,10},{10,8},{12,14},{14,12},{16,18},{18,... | collective-permute-start | bytes 98312 | tf_op jit(solution)/shard_map/ppermute | solution.py:51
  5.5 14.2 %collective-permute-start.1 = (f32[8,1024]{1,0:T(8,128)S(1)}, f32[8,1024]{1,0:T(8,128)S(1)}, u32[]{:S(2)}, u32[]{:S(2)}) collective-permute-start(f32[8,1024]{1,0:T(8,128)S(1)} %get-tuple-element.29), channel_id=1, source_target_pairs={{0,30},{2,4},{4,2},{6,8},{8,6},{10,12},{12,10},{14,16},{16,14},{18... | collective-permute-start | bytes 98312 | tf_op jit(solution)/shard_map/ppermute | solution.py:50
  20.8 1.5 %collective-permute-start.2 = (f32[3,3,40,128]{3,2,1,0:T(8,128)S(1)}, f32[3,3,40,128]{3,2,1,0:T(8,128)S(1)}, u32[]{:S(2)}, u32[]{:S(2)}) collective-permute-start(f32[3,3,40,128]{3,2,1,0:T(8,128)S(1)} %get-tuple-element.31), channel_id=1, source_target_pairs={{0,2},{2,0},{4,6},{6,4},{8,10},{10,8},{12,14},{14,12},{16,18},{18,... | collective-permute-start | bytes 552968 | tf_op jit(solution)/shard_map/ppermute | solution.py:51
  20.9 7.7 %collective-permute-start.3 = (f32[3,3,40,128]{3,2,1,0:T(8,128)S(1)}, f32[3,3,40,128]{3,2,1,0:T(8,128)S(1)}, u32[]{:S(2)}, u32[]{:S(2)}) collective-permute-start(f32[3,3,40,128]{3,2,1,0:T(8,128)S(1)} %get-tuple-element.32), channel_id=1, source_target_pairs={{0,30},{2,4},{4,2},{6,8},{8,6},{10,12},{12,10},{14,16},{16,14},{18... | collective-permute-start | bytes 552968 | tf_op jit(solution)/shard_map/ppermute | solution.py:50
  28.7 6.8 %collective-permute-start.4 = (f32[3,6,32,128]{3,2,1,0:T(8,128)S(1)}, f32[3,6,32,128]{3,2,1,0:T(8,128)S(1)}, u32[]{:S(2)}, u32[]{:S(2)}) collective-permute-start(f32[3,6,32,128]{3,2,1,0:T(8,128)S(1)} %get-tuple-element.34), channel_id=1, source_target_pairs={{0,1},{1,0},{2,3},{3,2},{4,5},{5,4},{6,7},{7,6},{8,9},{9,8},{10,11... | collective-permute-start | bytes 884744 | tf_op jit(solution)/shard_map/ppermute | solution.py:495
  36.6 2.0 %collective-permute-start.5 = (f32[3,2,56,128]{3,2,1,0:T(8,128)S(1)}, f32[3,2,56,128]{3,2,1,0:T(8,128)S(1)}, u32[]{:S(2)}, u32[]{:S(2)}) collective-permute-start(f32[3,2,56,128]{3,2,1,0:T(8,128)S(1)} %get-tuple-element.37), channel_id=1, source_target_pairs={{0,2},{2,0},{4,6},{6,4},{8,10},{10,8},{12,14},{14,12},{16,18},{18,... | collective-permute-start | bytes 516104 | tf_op jit(solution)/shard_map/ppermute | solution.py:51
  36.7 7.6 %collective-permute-start.6 = (f32[3,2,56,128]{3,2,1,0:T(8,128)S(1)}, f32[3,2,56,128]{3,2,1,0:T(8,128)S(1)}, u32[]{:S(2)}, u32[]{:S(2)}) collective-permute-start(f32[3,2,56,128]{3,2,1,0:T(8,128)S(1)} %get-tuple-element.38), channel_id=1, source_target_pairs={{0,30},{2,4},{4,2},{6,8},{8,6},{10,12},{12,10},{14,16},{16,14},{18... | collective-permute-start | bytes 516104 | tf_op jit(solution)/shard_map/ppermute | solution.py:50
  45.9 2.0 %collective-permute-start.7 = (f32[3,2,48,128]{3,2,1,0:T(8,128)S(1)}, f32[3,2,48,128]{3,2,1,0:T(8,128)S(1)}, u32[]{:S(2)}, u32[]{:S(2)}) collective-permute-start(f32[3,2,48,128]{3,2,1,0:T(8,128)S(1)} %get-tuple-element.40), channel_id=1, source_target_pairs={{0,2},{2,0},{4,6},{6,4},{8,10},{10,8},{12,14},{14,12},{16,18},{18,... | collective-permute-start | bytes 442376 | tf_op jit(solution)/shard_map/ppermute | solution.py:51
  46.0 7.3 %collective-permute-start.8 = (f32[3,2,48,128]{3,2,1,0:T(8,128)S(1)}, f32[3,2,48,128]{3,2,1,0:T(8,128)S(1)}, u32[]{:S(2)}, u32[]{:S(2)}) collective-permute-start(f32[3,2,48,128]{3,2,1,0:T(8,128)S(1)} %get-tuple-element.41), channel_id=1, source_target_pairs={{0,30},{2,4},{4,2},{6,8},{8,6},{10,12},{12,10},{14,16},{16,14},{18... | collective-permute-start | bytes 442376 | tf_op jit(solution)/shard_map/ppermute | solution.py:50
  54.9 2.0 %collective-permute-start.9 = (f32[3,2,48,128]{3,2,1,0:T(8,128)S(1)}, f32[3,2,48,128]{3,2,1,0:T(8,128)S(1)}, u32[]{:S(2)}, u32[]{:S(2)}) collective-permute-start(f32[3,2,48,128]{3,2,1,0:T(8,128)S(1)} %get-tuple-element.43), channel_id=1, source_target_pairs={{0,2},{2,0},{4,6},{6,4},{8,10},{10,8},{12,14},{14,12},{16,18},{18,... | collective-permute-start | bytes 442376 | tf_op jit(solution)/shard_map/ppermute | solution.py:51
  55.0 7.3 %collective-permute-start.10 = (f32[3,2,48,128]{3,2,1,0:T(8,128)S(1)}, f32[3,2,48,128]{3,2,1,0:T(8,128)S(1)}, u32[]{:S(2)}, u32[]{:S(2)}) collective-permute-start(f32[3,2,48,128]{3,2,1,0:T(8,128)S(1)} %get-tuple-element.44), channel_id=1, source_target_pairs={{0,30},{2,4},{4,2},{6,8},{8,6},{10,12},{12,10},{14,16},{16,14},{18... | collective-permute-start | bytes 442376 | tf_op jit(solution)/shard_map/ppermute | solution.py:50
  63.9 2.0 %collective-permute-start.11 = (f32[3,2,40,128]{3,2,1,0:T(8,128)S(1)}, f32[3,2,40,128]{3,2,1,0:T(8,128)S(1)}, u32[]{:S(2)}, u32[]{:S(2)}) collective-permute-start(f32[3,2,40,128]{3,2,1,0:T(8,128)S(1)} %get-tuple-element.46), channel_id=1, source_target_pairs={{0,2},{2,0},{4,6},{6,4},{8,10},{10,8},{12,14},{14,12},{16,18},{18,... | collective-permute-start | bytes 368648 | tf_op jit(solution)/shard_map/ppermute | solution.py:51
  64.0 7.1 %collective-permute-start.12 = (f32[3,2,40,128]{3,2,1,0:T(8,128)S(1)}, f32[3,2,40,128]{3,2,1,0:T(8,128)S(1)}, u32[]{:S(2)}, u32[]{:S(2)}) collective-permute-start(f32[3,2,40,128]{3,2,1,0:T(8,128)S(1)} %get-tuple-element.47), channel_id=1, source_target_pairs={{0,30},{2,4},{4,2},{6,8},{8,6},{10,12},{12,10},{14,16},{16,14},{18... | collective-permute-start | bytes 368648 | tf_op jit(solution)/shard_map/ppermute | solution.py:50

commit v3 on v2

--- a/solution.py
+++ b/solution.py
@@ -19,6 +19,8 @@
 SPREAD = 288
 QUANTITIES = 25
 VMEM_BYTES = 48 * 1024 * 1024
+ALL_VMEM_BYTES = 63 * 1024 * 1024
+STAY_VMEM_BYTES = 63 * 1024 * 1024
 
 
 def in_vmem(count):
@@ -29,8 +31,8 @@
     return pl.BlockSpec(memory_space=pltpu.SMEM)
 
 
-def params():
-    return pltpu.CompilerParams(vmem_limit_bytes=VMEM_BYTES)
+def params(vmem_bytes=VMEM_BYTES):
+    return pltpu.CompilerParams(vmem_limit_bytes=vmem_bytes)
 
 
 def is_even():
@@ -128,12 +130,13 @@
 
 
 def leaving_kernel(
-    moving, cell_hbm, offset_hbm, vort_hbm, cells, offsets, vorts, to_within, to_across, packed, sems, *, capacity
+    moving, cell_hbm, offset_hbm, vort_hbm, to_within, to_across, cells, offsets, vorts, packed, sems, *, capacity
 ):
+    room = 2 * capacity
     copies = [
-        pltpu.make_async_copy(offset_hbm, offsets, sems.at[0]),
-        pltpu.make_async_copy(vort_hbm, vorts, sems.at[1]),
-        pltpu.make_async_copy(cell_hbm, cells, sems.at[2]),
+        pltpu.make_async_copy(offset_hbm.at[:, pl.ds(0, room)], offsets, sems.at[0]),
+        pltpu.make_async_copy(vort_hbm.at[:, pl.ds(0, room)], vorts, sems.at[1]),
+        pltpu.make_async_copy(cell_hbm.at[pl.ds(0, room // 128)], cells, sems.at[2]),
     ]
     for copy in copies:
         copy.start()
@@ -142,9 +145,8 @@
     next_count = moving[0, 1]
     for copy in copies:
         copy.wait()
-    room = 2 * capacity
-    packed[0:3] = offsets[:, :room]
-    packed[3:6] = vorts[:, :room]
+    packed[0:3] = offsets[...]
+    packed[3:6] = vorts[...]
     for tile in range(room // 128):
         packed[6:7, tile * 128 : (tile + 1) * 128] = cells[tile : tile + 1].astype(F32)
     packed[7:8] = jnp.zeros((1, room), F32)
@@ -157,34 +159,48 @@
     to_across[...] = jnp.where(even, for_prev, for_next)
 
 
-def pack_leaving(part_cell, part_offset, part_vort, moving):
-    slots = part_cell.shape[0]
+def particle_specs():
+    return [in_smem()] + [pl.BlockSpec(memory_space=pl.ANY)] * 3
+
+
+def pack_leaving(moving, cells, part_offset, part_vort):
+    slots = part_offset.shape[1]
     capacity = slots // 17
-    tiles = slots // 128
+    room = 2 * capacity
     message = jax.ShapeDtypeStruct((8, capacity), F32)
     return pl.pallas_call(
         functools.partial(leaving_kernel, capacity=capacity),
-        in_specs=[in_smem()] + [pl.BlockSpec(memory_space=pltpu.HBM)] * 3,
-        out_specs=tuple(in_vmem(5)),
-        out_shape=(
-            jax.ShapeDtypeStruct((tiles, 128), jnp.int32),
-            jax.ShapeDtypeStruct((3, slots), F32),
-            jax.ShapeDtypeStruct((3, slots), F32),
-            message,
-            message,
-        ),
-        scratch_shapes=[pltpu.VMEM((8, 2 * capacity), F32), pltpu.SemaphoreType.DMA((3,))],
-        compiler_params=params(),
-    )(moving, part_cell.reshape(tiles, 128), part_offset, part_vort)
+        in_specs=particle_specs(),
+        out_specs=tuple(in_vmem(2)),
+        out_shape=(message, message),
+        scratch_shapes=[
+            pltpu.VMEM((room // 128, 128), jnp.int32),
+            pltpu.VMEM((3, room), F32),
+            pltpu.VMEM((3, room), F32),
+            pltpu.VMEM((8, room), F32),
+            pltpu.SemaphoreType.DMA((3,)),
+        ],
+        compiler_params=params(ALL_VMEM_BYTES),
+    )(moving, cells, part_offset, part_vort)
 
 
 def staying_kernel(
-    moving, cells, offsets, vorts, total, dense, table, planes_a, lines_a, planes_b, lines_b, *, tiles_per_chunk
+    moving, cell_hbm, offset_hbm, vort_hbm, total, cells, offsets, vorts, dense, table,
+    planes_a, lines_a, planes_b, lines_b, sems, *, tiles_per_chunk,
 ):
+    copies = [
+        pltpu.make_async_copy(offset_hbm, offsets, sems.at[0]),
+        pltpu.make_async_copy(vort_hbm, vorts, sems.at[1]),
+        pltpu.make_async_copy(cell_hbm, cells, sems.at[2]),
+    ]
+    for copy in copies:
+        copy.start()
     first_stay = moving[0, 0] + moving[0, 1]
     live_len = moving[0, 2]
     tiles = cells.shape[0]
     total[...] = jnp.zeros_like(total)
+    for copy in copies:
+        copy.wait()
     for tile in range(tiles):
         lanes = slice(tile * 128, (tile + 1) * 128)
         for dim in range(3):
@@ -228,26 +244,30 @@
         total[...] += product(planes_a, lines_a)
 
 
-def deposit_staying(cells, offsets, vorts, moving):
+def deposit_staying(moving, cells, part_offset, part_vort):
     tiles = cells.shape[0]
     slots = tiles * 128
     per_chunk = 17
     chunk = per_chunk * 128
     return pl.pallas_call(
         functools.partial(staying_kernel, tiles_per_chunk=per_chunk),
-        in_specs=[in_smem()] + in_vmem(3),
+        in_specs=particle_specs(),
         out_specs=in_vmem(1)[0],
         out_shape=jax.ShapeDtypeStruct((SPREAD, 3 * NZ), F32),
         scratch_shapes=[
+            pltpu.VMEM((tiles, 128), jnp.int32),
+            pltpu.VMEM((3, slots), F32),
+            pltpu.VMEM((3, slots), F32),
             pltpu.VMEM((6, tiles, 128), F32),
             pltpu.VMEM((QUANTITIES, tiles, 128), F32),
         ]
-        + [pltpu.VMEM((SPREAD, chunk), BF16), pltpu.VMEM((3 * NZ, chunk), BF16)] * 2,
-        compiler_params=params(),
+        + [pltpu.VMEM((SPREAD, chunk), BF16), pltpu.VMEM((3 * NZ, chunk), BF16)] * 2
+        + [pltpu.SemaphoreType.DMA((3,))],
+        compiler_params=params(STAY_VMEM_BYTES),
         cost_estimate=pl.CostEstimate(
             flops=2 * SPREAD * 3 * NZ * slots, bytes_accessed=28 * slots, transcendentals=0
         ),
-    )(moving, cells, offsets, vorts)
+    )(moving, cells, part_offset, part_vort)
 
 
 def arrived_kernel(total, got_within, got_across, deposits, to_within, to_across, dense, table, planes, lines):
@@ -594,11 +614,9 @@
 
 
 def per_device(part_cell, part_offset, part_vort, moving):
-    cells, offsets, vorts, to_within, to_across = pack_leaving(
-        part_cell, part_offset, part_vort, moving
-    )
-    got_within, got_across = swap_x(to_within, to_across)
-    total = deposit_staying(cells, offsets, vorts, moving)
+    particles = (moving, part_cell.reshape(-1, 128), part_offset, part_vort)
+    got_within, got_across = swap_x(*pack_leaving(*particles))
+    total = deposit_staying(*particles)
     deposits, to_within, to_across = deposit_arrived(total, got_within, got_across)
     if lax.axis_size("gy") == 2:
         return two_block_solve(deposits, to_within, to_across)

time: 72.3 us -> 73.1 us (1.011)
  Pallas kernels: 17.5 us -> 20.7 us
  local copies, waits for them, and re-layouts: 3.44 us -> 1.01 us
    unnamed x8 -> x2, local copies, waits for them, and re-layouts: 3.44 us -> 1.01 us
    pallas_call x1, Pallas kernels: 8.54 us -> 10.4 us  [deposit_staying(): pl.pallas_call(functools.partial(staying_kernel, tiles_per_chunk=per_chun...]
    pallas_call x1, Pallas kernels: 0.86 us -> 2.2 us  [pack_leaving(): pl.pallas_call(functools.partial(leaving_kernel, capacity=capacity), in_s...]
  transfers between devices with their start and end apart: 13 -> 13, of which waited for: 7 -> 7; matrix products, arithmetic and copies ran while one was open for 0% -> 0% of each run, Pallas kernels for 12% -> 14%
where the time goes in v3:
time: 73.1 us; the launch traced here: 72.9 us
  waiting for transfers between devices  33.8 us (46%)
  Pallas kernels  20.7 us (28%)
  starting transfers between devices  16.6 us (23%)
  local copies, waits for them, and re-layouts  1.01 us (1%)
  between operations  0.75 us (1%)
    ppermute x6, waiting for transfers between devices, swap_x(): got_across = lax.ppermute(to_across, 'gx', across(n))  27.8 us
    ppermute x6, starting transfers between devices, swap_x(): got_across = lax.ppermute(to_across, 'gx', across(n))  14.1 us
    pallas_call x1, Pallas kernels, deposit_staying(): pl.pallas_call(functools.partial(staying_kernel, tiles_per_chunk=per_chun...  10.4 us
    pallas_call x6, Pallas kernels, on_vmem(): pl.pallas_call(kernel, in_specs=in_vmem(len(args)), out_specs=tuple(in_vm...  6.96 us
    ppermute x1, waiting for transfers between devices, two_block_solve(): other = lax.ppermute(message, 'gy', [(0, 1), (1, 0)])  5.2 us
    pallas_call x1, Pallas kernels, pack_leaving(): pl.pallas_call(functools.partial(leaving_kernel, capacity=capacity), in_s...  2.2 us
    ppermute x1, starting transfers between devices, two_block_solve(): other = lax.ppermute(message, 'gy', [(0, 1), (1, 0)])  1.58 us
  transfers between devices with their start and end apart: 13, of which 7 were waited for; matrix products, arithmetic and copies ran while one was open for 0% of the time, Pallas kernels for 14%

profile of v3, /device:TPU:0, one launch (start us, length us, event | category | flops | bytes accessed | tf_op | source)
XLA Modules:
  0.0 72.9 jit_solution(507024338049401912)
XLA Ops:
  0.6 2.2 %shard_map.60 = (f32[8,1024]{1,0:T(8,128)}, f32[8,1024]{1,0:T(8,128)}) custom-call(s32[1,3]{1,0:T(1,128)} %moving.3, s32[136,128]{1,0:T(8,128)} %bitcast.1, f32[3,17408]{1,0:T(4,128)} %offset_hbm.3, f32[3,17408]{1,0:T(4,128)} %vort_hbm.3), custom_call_target="tpu_custom_call" | custom-call | tf_op jit(solution)/shard_map/pallas_call | solution.py:171
  2.8 0.5 collective-permute-start
  3.4 5.6 %collective-permute-start.1 = (f32[8,1024]{1,0:T(8,128)}, f32[8,1024]{1,0:T(8,128)S(1)}, u32[]{:S(2)}, u32[]{:S(2)}) collective-permute-start(f32[8,1024]{1,0:T(8,128)} %get-tuple-element.23), channel_id=1, source_target_pairs={{0,30},{2,4},{4,2},{6,8},{8,6},{10,12},{12,10},{14,16},{16,14},{18... | collective-permute-start | bytes 98312 | tf_op jit(solution)/shard_map/ppermute | solution.py:52
  9.0 10.4 %shard_map.59.total = f32[288,384]{1,0:T(8,128)} custom-call(s32[1,3]{1,0:T(1,128)} %moving.3, s32[136,128]{1,0:T(8,128)} %bitcast.2, f32[3,17408]{1,0:T(4,128)} %offset_hbm.3, f32[3,17408]{1,0:T(4,128)} %vort_hbm.3), custom_call_target="tpu_custom_call" | custom-call | flops 3850371072 | bytes 487424 | tf_op jit(solution)/shard_map/pallas_call | solution.py:252
  19.4 0.0 collective-permute-done.got_within
  19.5 0.0 collective-permute-done.1.got_across
  19.5 0.0 copy-start
  19.5 1.0 %copy-done = f32[288,384]{1,0:T(8,128)S(1)} copy-done((f32[288,384]{1,0:T(8,128)S(1)}, f32[288,384]{1,0:T(8,128)}, u32[]{:S(2)}) %copy-start) | copy-done | bytes 442392
  20.5 1.1 %shard_map.61 = (f32[3,7,40,128]{3,2,1,0:T(8,128)S(1)}, f32[3,3,40,128]{3,2,1,0:T(8,128)S(1)}, f32[3,3,40,128]{3,2,1,0:T(8,128)S(1)}) custom-call(f32[288,384]{1,0:T(8,128)S(1)} %copy-done, f32[8,1024]{1,0:T(8,128)S(1)} %collective-permute-done.got_within, f32[8,1024]{1,0:T(8,128)S(1)} %collective-permute-done.1.got_across), custom_call_target="tpu_custom_call" | custom-call | tf_op jit(solution)/shard_map/pallas_call | solution.py:308
  21.6 0.1 collective-permute-start.2
  21.7 0.6 collective-permute-start.3
  22.3 0.8 %collective-permute-done.2.got_within = f32[3,3,40,128]{3,2,1,0:T(8,128)S(1)} collective-permute-done((f32[3,3,40,128]{3,2,1,0:T(8,128)S(1)}, f32[3,3,40,128]{3,2,1,0:T(8,128)S(1)}, u32[]{:S(2)}, u32[]{:S(2)}) %collective-permute-start.2) | collective-permute-done | bytes 184352 | tf_op jit(solution)/shard_map/ppermute | solution.py:53
  23.1 6.3 %collective-permute-done.3.got_across = f32[3,3,40,128]{3,2,1,0:T(8,128)S(1)} collective-permute-done((f32[3,3,40,128]{3,2,1,0:T(8,128)S(1)}, f32[3,3,40,128]{3,2,1,0:T(8,128)S(1)}, u32[]{:S(2)}, u32[]{:S(2)}) %collective-permute-start.3) | collective-permute-done | bytes 184352 | tf_op jit(solution)/shard_map/ppermute | solution.py:52
  29.4 0.1 shard_map.62
  29.5 1.6 %collective-permute-start.4 = (f32[3,6,32,128]{3,2,1,0:T(8,128)S(1)}, f32[3,6,32,128]{3,2,1,0:T(8,128)S(1)}, u32[]{:S(2)}, u32[]{:S(2)}) collective-permute-start(f32[3,6,32,128]{3,2,1,0:T(8,128)S(1)} %get-tuple-element.28), channel_id=1, source_target_pairs={{0,1},{1,0},{2,3},{3,2},{4,5},{5,4},{6,7},{7,6},{8,9},{9,8},{10,11... | collective-permute-start | bytes 884744 | tf_op jit(solution)/shard_map/ppermute | solution.py:515
  31.1 5.2 %collective-permute-done.4.other = f32[3,6,32,128]{3,2,1,0:T(8,128)S(1)} collective-permute-done((f32[3,6,32,128]{3,2,1,0:T(8,128)S(1)}, f32[3,6,32,128]{3,2,1,0:T(8,128)S(1)}, u32[]{:S(2)}, u32[]{:S(2)}) %collective-permute-start.4) | collective-permute-done | bytes 294944 | tf_op jit(solution)/shard_map/ppermute | solution.py:515
  36.3 1.1 %shard_map.63 = (f32[3,6,64,128]{3,2,1,0:T(8,128)S(1)}, f32[3,4,64,128]{3,2,1,0:T(8,128)S(1)}, f32[3,2,56,128]{3,2,1,0:T(8,128)S(1)}, f32[3,2,56,128]{3,2,1,0:T(8,128)S(1)}) custom-call(f32[3,6,40,128]{3,2,1,0:T(8,128)S(1)} %get-tuple-element.27.mine, f32[3,6,32,128]{3,2,1,0:T(8,128)S(1)} %collective-permute-done.4.other), custom_call_target="tpu_custom_call" | custom-call | tf_op jit(solution)/shard_map/pallas_call | solution.py:498
  37.4 0.1 collective-permute-start.5
  37.5 2.0 %collective-permute-start.6 = (f32[3,2,56,128]{3,2,1,0:T(8,128)S(1)}, f32[3,2,56,128]{3,2,1,0:T(8,128)S(1)}, u32[]{:S(2)}, u32[]{:S(2)}) collective-permute-start(f32[3,2,56,128]{3,2,1,0:T(8,128)S(1)} %get-tuple-element.32), channel_id=1, source_target_pairs={{0,30},{2,4},{4,2},{6,8},{8,6},{10,12},{12,10},{14,16},{16,14},{18... | collective-permute-start | bytes 516104 | tf_op jit(solution)/shard_map/ppermute | solution.py:52
  39.5 0.0 collective-permute-done.5.got_within
  39.5 5.6 %collective-permute-done.6.got_across = f32[3,2,56,128]{3,2,1,0:T(8,128)S(1)} collective-permute-done((f32[3,2,56,128]{3,2,1,0:T(8,128)S(1)}, f32[3,2,56,128]{3,2,1,0:T(8,128)S(1)}, u32[]{:S(2)}, u32[]{:S(2)}) %collective-permute-start.6) | collective-permute-done | bytes 172064 | tf_op jit(solution)/shard_map/ppermute | solution.py:52
  45.1 1.6 %shard_map.64 = (f32[3,4,64,128]{3,2,1,0:T(8,128)S(1)}, f32[3,2,48,128]{3,2,1,0:T(8,128)S(1)}, f32[3,2,48,128]{3,2,1,0:T(8,128)S(1)}) custom-call(f32[3,6,64,128]{3,2,1,0:T(8,128)S(1)} %get-tuple-element.29.omega, f32[3,4,64,128]{3,2,1,0:T(8,128)S(1)} %get-tuple-element.30.before, f32[3,2,56,128]{3,2,1,0:T(8,128)S(1)} %collective-permute-done.5.got_within, ...), custom_call_target="tpu_custom_call" | custom-call | tf_op jit(solution)/shard_map/pallas_call | solution.py:498
  46.7 0.1 collective-permute-start.7
  46.8 2.0 %collective-permute-start.8 = (f32[3,2,48,128]{3,2,1,0:T(8,128)S(1)}, f32[3,2,48,128]{3,2,1,0:T(8,128)S(1)}, u32[]{:S(2)}, u32[]{:S(2)}) collective-permute-start(f32[3,2,48,128]{3,2,1,0:T(8,128)S(1)} %get-tuple-element.35), channel_id=1, source_target_pairs={{0,30},{2,4},{4,2},{6,8},{8,6},{10,12},{12,10},{14,16},{16,14},{18... | collective-permute-start | bytes 442376 | tf_op jit(solution)/shard_map/ppermute | solution.py:52
  48.7 0.0 collective-permute-done.7.got_within
  48.7 5.4 %collective-permute-done.8.got_across = f32[3,2,48,128]{3,2,1,0:T(8,128)S(1)} collective-permute-done((f32[3,2,48,128]{3,2,1,0:T(8,128)S(1)}, f32[3,2,48,128]{3,2,1,0:T(8,128)S(1)}, u32[]{:S(2)}, u32[]{:S(2)}) %collective-permute-start.8) | collective-permute-done | bytes 147488 | tf_op jit(solution)/shard_map/ppermute | solution.py:52
  54.1 1.6 %shard_map.65 = (f32[3,4,64,128]{3,2,1,0:T(8,128)S(1)}, f32[3,2,48,128]{3,2,1,0:T(8,128)S(1)}, f32[3,2,48,128]{3,2,1,0:T(8,128)S(1)}) custom-call(f32[3,6,64,128]{3,2,1,0:T(8,128)S(1)} %get-tuple-element.29.omega, f32[3,4,64,128]{3,2,1,0:T(8,128)S(1)} %get-tuple-element.33.before, f32[3,2,48,128]{3,2,1,0:T(8,128)S(1)} %collective-permute-done.7.got_within, ...), custom_call_target="tpu_custom_call" | custom-call | tf_op jit(solution)/shard_map/pallas_call | solution.py:498
  55.7 0.1 collective-permute-start.9
  55.8 2.0 %collective-permute-start.10 = (f32[3,2,48,128]{3,2,1,0:T(8,128)S(1)}, f32[3,2,48,128]{3,2,1,0:T(8,128)S(1)}, u32[]{:S(2)}, u32[]{:S(2)}) collective-permute-start(f32[3,2,48,128]{3,2,1,0:T(8,128)S(1)} %get-tuple-element.38), channel_id=1, source_target_pairs={{0,30},{2,4},{4,2},{6,8},{8,6},{10,12},{12,10},{14,16},{16,14},{18... | collective-permute-start | bytes 442376 | tf_op jit(solution)/shard_map/ppermute | solution.py:52
  57.7 0.0 collective-permute-done.9.got_within
  57.8 5.4 %collective-permute-done.10.got_across = f32[3,2,48,128]{3,2,1,0:T(8,128)S(1)} collective-permute-done((f32[3,2,48,128]{3,2,1,0:T(8,128)S(1)}, f32[3,2,48,128]{3,2,1,0:T(8,128)S(1)}, u32[]{:S(2)}, u32[]{:S(2)}) %collective-permute-start.10) | collective-permute-done | bytes 147488 | tf_op jit(solution)/shard_map/ppermute | solution.py:52
  63.1 1.6 %shard_map.66 = (f32[3,4,64,128]{3,2,1,0:T(8,128)S(1)}, f32[3,2,40,128]{3,2,1,0:T(8,128)S(1)}, f32[3,2,40,128]{3,2,1,0:T(8,128)S(1)}) custom-call(f32[3,6,64,128]{3,2,1,0:T(8,128)S(1)} %get-tuple-element.29.omega, f32[3,4,64,128]{3,2,1,0:T(8,128)S(1)} %get-tuple-element.36.before, f32[3,2,48,128]{3,2,1,0:T(8,128)S(1)} %collective-permute-done.9.got_within, ...), custom_call_target="tpu_custom_call" | custom-call | tf_op jit(solution)/shard_map/pallas_call | solution.py:498
  64.7 0.1 collective-permute-start.11
  64.8 2.0 %collective-permute-start.12 = (f32[3,2,40,128]{3,2,1,0:T(8,128)S(1)}, f32[3,2,40,128]{3,2,1,0:T(8,128)S(1)}, u32[]{:S(2)}, u32[]{:S(2)}) collective-permute-start(f32[3,2,40,128]{3,2,1,0:T(8,128)S(1)} %get-tuple-element.41), channel_id=1, source_target_pairs={{0,30},{2,4},{4,2},{6,8},{8,6},{10,12},{12,10},{14,16},{16,14},{18... | collective-permute-start | bytes 368648 | tf_op jit(solution)/shard_map/ppermute | solution.py:52
  66.8 0.0 collective-permute-done.11.got_within
  66.8 5.1 %collective-permute-done.12.got_across = f32[3,2,40,128]{3,2,1,0:T(8,128)S(1)} collective-permute-done((f32[3,2,40,128]{3,2,1,0:T(8,128)S(1)}, f32[3,2,40,128]{3,2,1,0:T(8,128)S(1)}, u32[]{:S(2)}, u32[]{:S(2)}) %collective-permute-start.12) | collective-permute-done | bytes 122912 | tf_op jit(solution)/shard_map/ppermute | solution.py:52
  71.9 1.0 %shard_map.67 = (f32[3,4,32,128]{3,2,1,0:T(8,128)}, f32[3,4,32,128]{3,2,1,0:T(8,128)}) custom-call(f32[3,6,64,128]{3,2,1,0:T(8,128)S(1)} %get-tuple-element.29.omega, f32[3,4,64,128]{3,2,1,0:T(8,128)S(1)} %get-tuple-element.39.potential, f32[3,2,40,128]{3,2,1,0:T(8,128)S(1)} %collective-permute-done.11.got_within, ...), custom_call_target="tpu_custom_call" | custom-call | tf_op jit(solution)/shard_map/pallas_call | solution.py:498
Async XLA Ops:
  2.8 16.6 %collective-permute-start = (f32[8,1024]{1,0:T(8,128)}, f32[8,1024]{1,0:T(8,128)S(1)}, u32[]{:S(2)}, u32[]{:S(2)}) collective-permute-start(f32[8,1024]{1,0:T(8,128)} %get-tuple-element.22), channel_id=1, source_target_pairs={{0,2},{2,0},{4,6},{6,4},{8,10},{10,8},{12,14},{14,12},{16,18},{18,... | collective-permute-start | bytes 98312 | tf_op jit(solution)/shard_map/ppermute | solution.py:53
  3.4 16.1 %collective-permute-start.1 = (f32[8,1024]{1,0:T(8,128)}, f32[8,1024]{1,0:T(8,128)S(1)}, u32[]{:S(2)}, u32[]{:S(2)}) collective-permute-start(f32[8,1024]{1,0:T(8,128)} %get-tuple-element.23), channel_id=1, source_target_pairs={{0,30},{2,4},{4,2},{6,8},{8,6},{10,12},{12,10},{14,16},{16,14},{18... | collective-permute-start | bytes 98312 | tf_op jit(solution)/shard_map/ppermute | solution.py:52
  19.5 1.0 %copy-start = (f32[288,384]{1,0:T(8,128)S(1)}, f32[288,384]{1,0:T(8,128)}, u32[]{:S(2)}) copy-start(f32[288,384]{1,0:T(8,128)} %shard_map.59.total) | copy-start | bytes 1327108
  21.6 1.5 %collective-permute-start.2 = (f32[3,3,40,128]{3,2,1,0:T(8,128)S(1)}, f32[3,3,40,128]{3,2,1,0:T(8,128)S(1)}, u32[]{:S(2)}, u32[]{:S(2)}) collective-permute-start(f32[3,3,40,128]{3,2,1,0:T(8,128)S(1)} %get-tuple-element.25), channel_id=1, source_target_pairs={{0,2},{2,0},{4,6},{6,4},{8,10},{10,8},{12,14},{14,12},{16,18},{18,... | collective-permute-start | bytes 552968 | tf_op jit(solution)/shard_map/ppermute | solution.py:53
  21.7 7.7 %collective-permute-start.3 = (f32[3,3,40,128]{3,2,1,0:T(8,128)S(1)}, f32[3,3,40,128]{3,2,1,0:T(8,128)S(1)}, u32[]{:S(2)}, u32[]{:S(2)}) collective-permute-start(f32[3,3,40,128]{3,2,1,0:T(8,128)S(1)} %get-tuple-element.26), channel_id=1, source_target_pairs={{0,30},{2,4},{4,2},{6,8},{8,6},{10,12},{12,10},{14,16},{16,14},{18... | collective-permute-start | bytes 552968 | tf_op jit(solution)/shard_map/ppermute | solution.py:52
  29.5 6.8 %collective-permute-start.4 = (f32[3,6,32,128]{3,2,1,0:T(8,128)S(1)}, f32[3,6,32,128]{3,2,1,0:T(8,128)S(1)}, u32[]{:S(2)}, u32[]{:S(2)}) collective-permute-start(f32[3,6,32,128]{3,2,1,0:T(8,128)S(1)} %get-tuple-element.28), channel_id=1, source_target_pairs={{0,1},{1,0},{2,3},{3,2},{4,5},{5,4},{6,7},{7,6},{8,9},{9,8},{10,11... | collective-permute-start | bytes 884744 | tf_op jit(solution)/shard_map/ppermute | solution.py:515
  37.4 2.0 %collective-permute-start.5 = (f32[3,2,56,128]{3,2,1,0:T(8,128)S(1)}, f32[3,2,56,128]{3,2,1,0:T(8,128)S(1)}, u32[]{:S(2)}, u32[]{:S(2)}) collective-permute-start(f32[3,2,56,128]{3,2,1,0:T(8,128)S(1)} %get-tuple-element.31), channel_id=1, source_target_pairs={{0,2},{2,0},{4,6},{6,4},{8,10},{10,8},{12,14},{14,12},{16,18},{18,... | collective-permute-start | bytes 516104 | tf_op jit(solution)/shard_map/ppermute | solution.py:53
  37.5 7.6 %collective-permute-start.6 = (f32[3,2,56,128]{3,2,1,0:T(8,128)S(1)}, f32[3,2,56,128]{3,2,1,0:T(8,128)S(1)}, u32[]{:S(2)}, u32[]{:S(2)}) collective-permute-start(f32[3,2,56,128]{3,2,1,0:T(8,128)S(1)} %get-tuple-element.32), channel_id=1, source_target_pairs={{0,30},{2,4},{4,2},{6,8},{8,6},{10,12},{12,10},{14,16},{16,14},{18... | collective-permute-start | bytes 516104 | tf_op jit(solution)/shard_map/ppermute | solution.py:52
  46.7 2.0 %collective-permute-start.7 = (f32[3,2,48,128]{3,2,1,0:T(8,128)S(1)}, f32[3,2,48,128]{3,2,1,0:T(8,128)S(1)}, u32[]{:S(2)}, u32[]{:S(2)}) collective-permute-start(f32[3,2,48,128]{3,2,1,0:T(8,128)S(1)} %get-tuple-element.34), channel_id=1, source_target_pairs={{0,2},{2,0},{4,6},{6,4},{8,10},{10,8},{12,14},{14,12},{16,18},{18,... | collective-permute-start | bytes 442376 | tf_op jit(solution)/shard_map/ppermute | solution.py:53
  46.8 7.3 %collective-permute-start.8 = (f32[3,2,48,128]{3,2,1,0:T(8,128)S(1)}, f32[3,2,48,128]{3,2,1,0:T(8,128)S(1)}, u32[]{:S(2)}, u32[]{:S(2)}) collective-permute-start(f32[3,2,48,128]{3,2,1,0:T(8,128)S(1)} %get-tuple-element.35), channel_id=1, source_target_pairs={{0,30},{2,4},{4,2},{6,8},{8,6},{10,12},{12,10},{14,16},{16,14},{18... | collective-permute-start | bytes 442376 | tf_op jit(solution)/shard_map/ppermute | solution.py:52
  55.7 2.0 %collective-permute-start.9 = (f32[3,2,48,128]{3,2,1,0:T(8,128)S(1)}, f32[3,2,48,128]{3,2,1,0:T(8,128)S(1)}, u32[]{:S(2)}, u32[]{:S(2)}) collective-permute-start(f32[3,2,48,128]{3,2,1,0:T(8,128)S(1)} %get-tuple-element.37), channel_id=1, source_target_pairs={{0,2},{2,0},{4,6},{6,4},{8,10},{10,8},{12,14},{14,12},{16,18},{18,... | collective-permute-start | bytes 442376 | tf_op jit(solution)/shard_map/ppermute | solution.py:53
  55.8 7.3 %collective-permute-start.10 = (f32[3,2,48,128]{3,2,1,0:T(8,128)S(1)}, f32[3,2,48,128]{3,2,1,0:T(8,128)S(1)}, u32[]{:S(2)}, u32[]{:S(2)}) collective-permute-start(f32[3,2,48,128]{3,2,1,0:T(8,128)S(1)} %get-tuple-element.38), channel_id=1, source_target_pairs={{0,30},{2,4},{4,2},{6,8},{8,6},{10,12},{12,10},{14,16},{16,14},{18... | collective-permute-start | bytes 442376 | tf_op jit(solution)/shard_map/ppermute | solution.py:52
  64.7 2.0 %collective-permute-start.11 = (f32[3,2,40,128]{3,2,1,0:T(8,128)S(1)}, f32[3,2,40,128]{3,2,1,0:T(8,128)S(1)}, u32[]{:S(2)}, u32[]{:S(2)}) collective-permute-start(f32[3,2,40,128]{3,2,1,0:T(8,128)S(1)} %get-tuple-element.40), channel_id=1, source_target_pairs={{0,2},{2,0},{4,6},{6,4},{8,10},{10,8},{12,14},{14,12},{16,18},{18,... | collective-permute-start | bytes 368648 | tf_op jit(solution)/shard_map/ppermute | solution.py:53
  64.8 7.1 %collective-permute-start.12 = (f32[3,2,40,128]{3,2,1,0:T(8,128)S(1)}, f32[3,2,40,128]{3,2,1,0:T(8,128)S(1)}, u32[]{:S(2)}, u32[]{:S(2)}) collective-permute-start(f32[3,2,40,128]{3,2,1,0:T(8,128)S(1)} %get-tuple-element.41), channel_id=1, source_target_pairs={{0,30},{2,4},{4,2},{6,8},{8,6},{10,12},{12,10},{14,16},{16,14},{18... | collective-permute-start | bytes 368648 | tf_op jit(solution)/shard_map/ppermute | solution.py:52

commit v4 on v3

--- a/solution.py
+++ b/solution.py
@@ -20,7 +20,6 @@
 QUANTITIES = 25
 VMEM_BYTES = 48 * 1024 * 1024
 ALL_VMEM_BYTES = 63 * 1024 * 1024
-STAY_VMEM_BYTES = 63 * 1024 * 1024
 
 
 def in_vmem(count):
@@ -185,22 +184,12 @@
 
 
 def staying_kernel(
-    moving, cell_hbm, offset_hbm, vort_hbm, total, cells, offsets, vorts, dense, table,
-    planes_a, lines_a, planes_b, lines_b, sems, *, tiles_per_chunk,
+    moving, cells, offsets, vorts, total, dense, table, planes_a, lines_a, planes_b, lines_b, *, tiles_per_chunk
 ):
-    copies = [
-        pltpu.make_async_copy(offset_hbm, offsets, sems.at[0]),
-        pltpu.make_async_copy(vort_hbm, vorts, sems.at[1]),
-        pltpu.make_async_copy(cell_hbm, cells, sems.at[2]),
-    ]
-    for copy in copies:
-        copy.start()
     first_stay = moving[0, 0] + moving[0, 1]
     live_len = moving[0, 2]
     tiles = cells.shape[0]
     total[...] = jnp.zeros_like(total)
-    for copy in copies:
-        copy.wait()
     for tile in range(tiles):
         lanes = slice(tile * 128, (tile + 1) * 128)
         for dim in range(3):
@@ -251,19 +240,15 @@
     chunk = per_chunk * 128
     return pl.pallas_call(
         functools.partial(staying_kernel, tiles_per_chunk=per_chunk),
-        in_specs=particle_specs(),
+        in_specs=[in_smem()] + in_vmem(3),
         out_specs=in_vmem(1)[0],
         out_shape=jax.ShapeDtypeStruct((SPREAD, 3 * NZ), F32),
         scratch_shapes=[
-            pltpu.VMEM((tiles, 128), jnp.int32),
-            pltpu.VMEM((3, slots), F32),
-            pltpu.VMEM((3, slots), F32),
             pltpu.VMEM((6, tiles, 128), F32),
             pltpu.VMEM((QUANTITIES, tiles, 128), F32),
         ]
-        + [pltpu.VMEM((SPREAD, chunk), BF16), pltpu.VMEM((3 * NZ, chunk), BF16)] * 2
-        + [pltpu.SemaphoreType.DMA((3,))],
-        compiler_params=params(STAY_VMEM_BYTES),
+        + [pltpu.VMEM((SPREAD, chunk), BF16), pltpu.VMEM((3 * NZ, chunk), BF16)] * 2,
+        compiler_params=params(),
         cost_estimate=pl.CostEstimate(
             flops=2 * SPREAD * 3 * NZ * slots, bytes_accessed=28 * slots, transcendentals=0
         ),

time: 73.1 us -> 70.3 us (0.962)
  Pallas kernels: 20.7 us -> 19 us
  local copies, waits for them, and re-layouts: 1.01 us -> 0.02 us
    pallas_call x1, Pallas kernels: 10.4 us -> 8.54 us  [deposit_staying(): pl.pallas_call(functools.partial(staying_kernel, tiles_per_chunk=per_chun...]
    unnamed x2 -> x8, local copies, waits for them, and re-layouts: 1.01 us -> 0.02 us
  transfers between devices with their start and end apart: 13 -> 13, of which waited for: 7 -> 7; matrix products, arithmetic and copies ran while one was open for 0% -> 0% of each run, Pallas kernels for 14% -> 12%
where the time goes in v4:
time: 70.3 us; the launch traced here: 70.1 us
  waiting for transfers between devices  33.8 us (48%)
  Pallas kernels  19 us (27%)
  starting transfers between devices  16.6 us (24%)
  between operations  0.78 us (1%)
    ppermute x6, waiting for transfers between devices, swap_x(): got_across = lax.ppermute(to_across, 'gx', across(n))  27.8 us
    ppermute x6, starting transfers between devices, swap_x(): got_across = lax.ppermute(to_across, 'gx', across(n))  14.1 us
    pallas_call x1, Pallas kernels, deposit_staying(): pl.pallas_call(functools.partial(staying_kernel, tiles_per_chunk=per_chun...  8.54 us
    pallas_call x6, Pallas kernels, on_vmem(): pl.pallas_call(kernel, in_specs=in_vmem(len(args)), out_specs=tuple(in_vm...  6.95 us
    ppermute x1, waiting for transfers between devices, two_block_solve(): other = lax.ppermute(message, 'gy', [(0, 1), (1, 0)])  5.2 us
    pallas_call x1, Pallas kernels, pack_leaving(): pl.pallas_call(functools.partial(leaving_kernel, capacity=capacity), in_s...  2.33 us
    ppermute x1, starting transfers between devices, two_block_solve(): other = lax.ppermute(message, 'gy', [(0, 1), (1, 0)])  1.58 us
  transfers between devices with their start and end apart: 13, of which 7 were waited for; matrix products, arithmetic and copies ran while one was open for 0% of the time, Pallas kernels for 12%

profile of v4, /device:TPU:0, one launch (start us, length us, event | category | flops | bytes accessed | tf_op | source)
XLA Modules:
  0.0 70.1 jit_solution(7438325887235270843)
XLA Ops:
  0.6 0.0 copy-start
  0.6 0.0 copy-start.1
  0.6 0.0 copy-start.2
  0.7 2.3 %shard_map.60 = (f32[8,1024]{1,0:T(8,128)}, f32[8,1024]{1,0:T(8,128)}) custom-call(s32[1,3]{1,0:T(1,128)} %moving.3, s32[136,128]{1,0:T(8,128)} %bitcast.1, f32[3,17408]{1,0:T(4,128)} %offset_hbm.1, f32[3,17408]{1,0:T(4,128)} %vort_hbm.1), custom_call_target="tpu_custom_call" | custom-call | tf_op jit(solution)/shard_map/pallas_call | solution.py:170
  3.0 0.0 copy-start.3
  3.0 0.5 collective-permute-start
  3.5 5.6 %collective-permute-start.1 = (f32[8,1024]{1,0:T(8,128)}, f32[8,1024]{1,0:T(8,128)S(1)}, u32[]{:S(2)}, u32[]{:S(2)}) collective-permute-start(f32[8,1024]{1,0:T(8,128)} %get-tuple-element.23), channel_id=1, source_target_pairs={{0,30},{2,4},{4,2},{6,8},{8,6},{10,12},{12,10},{14,16},{16,14},{18... | collective-permute-start | bytes 98312 | tf_op jit(solution)/shard_map/ppermute | solution.py:51
  9.2 0.0 copy-done
  9.2 0.0 copy-done.1
  9.2 0.0 copy-done.2
  9.2 0.0 copy-done.3
  9.2 8.5 %shard_map.59.total = f32[288,384]{1,0:T(8,128)S(1)} custom-call(s32[1,3]{1,0:T(1,128)S(1)} %copy-done.3, s32[136,128]{1,0:T(8,128)S(1)} %bitcast.2, f32[3,17408]{1,0:T(4,128)S(1)} %copy-done, f32[3,17408]{1,0:T(4,128)S(1)} %copy-done.1), custom_call_target="tpu_custom_call" | custom-call | flops 3850371072 | bytes 487424 | tf_op jit(solution)/shard_map/pallas_call | solution.py:241
  17.7 0.0 collective-permute-done.got_within
  17.7 0.0 collective-permute-done.1.got_across
  17.7 1.2 %shard_map.61 = (f32[3,7,40,128]{3,2,1,0:T(8,128)S(1)}, f32[3,3,40,128]{3,2,1,0:T(8,128)S(1)}, f32[3,3,40,128]{3,2,1,0:T(8,128)S(1)}) custom-call(f32[288,384]{1,0:T(8,128)S(1)} %shard_map.59.total, f32[8,1024]{1,0:T(8,128)S(1)} %collective-permute-done.got_within, f32[8,1024]{1,0:T(8,128)S(1)} %collective-permute-done.1.got_across), custom_call_target="tpu_custom_call" | custom-call | tf_op jit(solution)/shard_map/pallas_call | solution.py:293
  18.9 0.1 collective-permute-start.2
  19.0 0.6 collective-permute-start.3
  19.6 0.8 %collective-permute-done.2.got_within = f32[3,3,40,128]{3,2,1,0:T(8,128)S(1)} collective-permute-done((f32[3,3,40,128]{3,2,1,0:T(8,128)S(1)}, f32[3,3,40,128]{3,2,1,0:T(8,128)S(1)}, u32[]{:S(2)}, u32[]{:S(2)}) %collective-permute-start.2) | collective-permute-done | bytes 184352 | tf_op jit(solution)/shard_map/ppermute | solution.py:52
  20.4 6.3 %collective-permute-done.3.got_across = f32[3,3,40,128]{3,2,1,0:T(8,128)S(1)} collective-permute-done((f32[3,3,40,128]{3,2,1,0:T(8,128)S(1)}, f32[3,3,40,128]{3,2,1,0:T(8,128)S(1)}, u32[]{:S(2)}, u32[]{:S(2)}) %collective-permute-start.3) | collective-permute-done | bytes 184352 | tf_op jit(solution)/shard_map/ppermute | solution.py:51
  26.7 0.1 shard_map.62
  26.8 1.6 %collective-permute-start.4 = (f32[3,6,32,128]{3,2,1,0:T(8,128)S(1)}, f32[3,6,32,128]{3,2,1,0:T(8,128)S(1)}, u32[]{:S(2)}, u32[]{:S(2)}) collective-permute-start(f32[3,6,32,128]{3,2,1,0:T(8,128)S(1)} %get-tuple-element.28), channel_id=1, source_target_pairs={{0,1},{1,0},{2,3},{3,2},{4,5},{5,4},{6,7},{7,6},{8,9},{9,8},{10,11... | collective-permute-start | bytes 884744 | tf_op jit(solution)/shard_map/ppermute | solution.py:500
  28.4 5.2 %collective-permute-done.4.other = f32[3,6,32,128]{3,2,1,0:T(8,128)S(1)} collective-permute-done((f32[3,6,32,128]{3,2,1,0:T(8,128)S(1)}, f32[3,6,32,128]{3,2,1,0:T(8,128)S(1)}, u32[]{:S(2)}, u32[]{:S(2)}) %collective-permute-start.4) | collective-permute-done | bytes 294944 | tf_op jit(solution)/shard_map/ppermute | solution.py:500
  33.6 1.1 %shard_map.63 = (f32[3,6,64,128]{3,2,1,0:T(8,128)S(1)}, f32[3,4,64,128]{3,2,1,0:T(8,128)S(1)}, f32[3,2,56,128]{3,2,1,0:T(8,128)S(1)}, f32[3,2,56,128]{3,2,1,0:T(8,128)S(1)}) custom-call(f32[3,6,40,128]{3,2,1,0:T(8,128)S(1)} %get-tuple-element.27.mine, f32[3,6,32,128]{3,2,1,0:T(8,128)S(1)} %collective-permute-done.4.other), custom_call_target="tpu_custom_call" | custom-call | tf_op jit(solution)/shard_map/pallas_call | solution.py:483
  34.7 0.1 collective-permute-start.5
  34.8 2.0 %collective-permute-start.6 = (f32[3,2,56,128]{3,2,1,0:T(8,128)S(1)}, f32[3,2,56,128]{3,2,1,0:T(8,128)S(1)}, u32[]{:S(2)}, u32[]{:S(2)}) collective-permute-start(f32[3,2,56,128]{3,2,1,0:T(8,128)S(1)} %get-tuple-element.32), channel_id=1, source_target_pairs={{0,30},{2,4},{4,2},{6,8},{8,6},{10,12},{12,10},{14,16},{16,14},{18... | collective-permute-start | bytes 516104 | tf_op jit(solution)/shard_map/ppermute | solution.py:51
  36.7 0.0 collective-permute-done.5.got_within
  36.7 5.6 %collective-permute-done.6.got_across = f32[3,2,56,128]{3,2,1,0:T(8,128)S(1)} collective-permute-done((f32[3,2,56,128]{3,2,1,0:T(8,128)S(1)}, f32[3,2,56,128]{3,2,1,0:T(8,128)S(1)}, u32[]{:S(2)}, u32[]{:S(2)}) %collective-permute-start.6) | collective-permute-done | bytes 172064 | tf_op jit(solution)/shard_map/ppermute | solution.py:51
  42.3 1.6 %shard_map.64 = (f32[3,4,64,128]{3,2,1,0:T(8,128)S(1)}, f32[3,2,48,128]{3,2,1,0:T(8,128)S(1)}, f32[3,2,48,128]{3,2,1,0:T(8,128)S(1)}) custom-call(f32[3,6,64,128]{3,2,1,0:T(8,128)S(1)} %get-tuple-element.29.omega, f32[3,4,64,128]{3,2,1,0:T(8,128)S(1)} %get-tuple-element.30.before, f32[3,2,56,128]{3,2,1,0:T(8,128)S(1)} %collective-permute-done.5.got_within, ...), custom_call_target="tpu_custom_call" | custom-call | tf_op jit(solution)/shard_map/pallas_call | solution.py:483
  44.0 0.1 collective-permute-start.7
  44.0 2.0 %collective-permute-start.8 = (f32[3,2,48,128]{3,2,1,0:T(8,128)S(1)}, f32[3,2,48,128]{3,2,1,0:T(8,128)S(1)}, u32[]{:S(2)}, u32[]{:S(2)}) collective-permute-start(f32[3,2,48,128]{3,2,1,0:T(8,128)S(1)} %get-tuple-element.35), channel_id=1, source_target_pairs={{0,30},{2,4},{4,2},{6,8},{8,6},{10,12},{12,10},{14,16},{16,14},{18... | collective-permute-start | bytes 442376 | tf_op jit(solution)/shard_map/ppermute | solution.py:51
  46.0 0.0 collective-permute-done.7.got_within
  46.0 5.4 %collective-permute-done.8.got_across = f32[3,2,48,128]{3,2,1,0:T(8,128)S(1)} collective-permute-done((f32[3,2,48,128]{3,2,1,0:T(8,128)S(1)}, f32[3,2,48,128]{3,2,1,0:T(8,128)S(1)}, u32[]{:S(2)}, u32[]{:S(2)}) %collective-permute-start.8) | collective-permute-done | bytes 147488 | tf_op jit(solution)/shard_map/ppermute | solution.py:51
  51.4 1.6 %shard_map.65 = (f32[3,4,64,128]{3,2,1,0:T(8,128)S(1)}, f32[3,2,48,128]{3,2,1,0:T(8,128)S(1)}, f32[3,2,48,128]{3,2,1,0:T(8,128)S(1)}) custom-call(f32[3,6,64,128]{3,2,1,0:T(8,128)S(1)} %get-tuple-element.29.omega, f32[3,4,64,128]{3,2,1,0:T(8,128)S(1)} %get-tuple-element.33.before, f32[3,2,48,128]{3,2,1,0:T(8,128)S(1)} %collective-permute-done.7.got_within, ...), custom_call_target="tpu_custom_call" | custom-call | tf_op jit(solution)/shard_map/pallas_call | solution.py:483
  53.0 0.1 collective-permute-start.9
  53.1 2.0 %collective-permute-start.10 = (f32[3,2,48,128]{3,2,1,0:T(8,128)S(1)}, f32[3,2,48,128]{3,2,1,0:T(8,128)S(1)}, u32[]{:S(2)}, u32[]{:S(2)}) collective-permute-start(f32[3,2,48,128]{3,2,1,0:T(8,128)S(1)} %get-tuple-element.38), channel_id=1, source_target_pairs={{0,30},{2,4},{4,2},{6,8},{8,6},{10,12},{12,10},{14,16},{16,14},{18... | collective-permute-start | bytes 442376 | tf_op jit(solution)/shard_map/ppermute | solution.py:51
  55.0 0.0 collective-permute-done.9.got_within
  55.0 5.4 %collective-permute-done.10.got_across = f32[3,2,48,128]{3,2,1,0:T(8,128)S(1)} collective-permute-done((f32[3,2,48,128]{3,2,1,0:T(8,128)S(1)}, f32[3,2,48,128]{3,2,1,0:T(8,128)S(1)}, u32[]{:S(2)}, u32[]{:S(2)}) %collective-permute-start.10) | collective-permute-done | bytes 147488 | tf_op jit(solution)/shard_map/ppermute | solution.py:51
  60.4 1.6 %shard_map.66 = (f32[3,4,64,128]{3,2,1,0:T(8,128)S(1)}, f32[3,2,40,128]{3,2,1,0:T(8,128)S(1)}, f32[3,2,40,128]{3,2,1,0:T(8,128)S(1)}) custom-call(f32[3,6,64,128]{3,2,1,0:T(8,128)S(1)} %get-tuple-element.29.omega, f32[3,4,64,128]{3,2,1,0:T(8,128)S(1)} %get-tuple-element.36.before, f32[3,2,48,128]{3,2,1,0:T(8,128)S(1)} %collective-permute-done.9.got_within, ...), custom_call_target="tpu_custom_call" | custom-call | tf_op jit(solution)/shard_map/pallas_call | solution.py:483
  62.0 0.1 collective-permute-start.11
  62.1 2.0 %collective-permute-start.12 = (f32[3,2,40,128]{3,2,1,0:T(8,128)S(1)}, f32[3,2,40,128]{3,2,1,0:T(8,128)S(1)}, u32[]{:S(2)}, u32[]{:S(2)}) collective-permute-start(f32[3,2,40,128]{3,2,1,0:T(8,128)S(1)} %get-tuple-element.41), channel_id=1, source_target_pairs={{0,30},{2,4},{4,2},{6,8},{8,6},{10,12},{12,10},{14,16},{16,14},{18... | collective-permute-start | bytes 368648 | tf_op jit(solution)/shard_map/ppermute | solution.py:51
  64.0 0.0 collective-permute-done.11.got_within
  64.0 5.1 %collective-permute-done.12.got_across = f32[3,2,40,128]{3,2,1,0:T(8,128)S(1)} collective-permute-done((f32[3,2,40,128]{3,2,1,0:T(8,128)S(1)}, f32[3,2,40,128]{3,2,1,0:T(8,128)S(1)}, u32[]{:S(2)}, u32[]{:S(2)}) %collective-permute-start.12) | collective-permute-done | bytes 122912 | tf_op jit(solution)/shard_map/ppermute | solution.py:51
  69.1 1.0 %shard_map.67 = (f32[3,4,32,128]{3,2,1,0:T(8,128)}, f32[3,4,32,128]{3,2,1,0:T(8,128)}) custom-call(f32[3,6,64,128]{3,2,1,0:T(8,128)S(1)} %get-tuple-element.29.omega, f32[3,4,64,128]{3,2,1,0:T(8,128)S(1)} %get-tuple-element.39.potential, f32[3,2,40,128]{3,2,1,0:T(8,128)S(1)} %collective-permute-done.11.got_within, ...), custom_call_target="tpu_custom_call" | custom-call | tf_op jit(solution)/shard_map/pallas_call | solution.py:483
Async XLA Ops:
  0.6 8.5 %copy-start = (f32[3,17408]{1,0:T(4,128)S(1)}, f32[3,17408]{1,0:T(4,128)}, u32[]{:S(2)}) copy-start(f32[3,17408]{1,0:T(4,128)} %offset_hbm.1) | copy-start | bytes 626692
  0.6 8.5 %copy-start.1 = (f32[3,17408]{1,0:T(4,128)S(1)}, f32[3,17408]{1,0:T(4,128)}, u32[]{:S(2)}) copy-start(f32[3,17408]{1,0:T(4,128)} %vort_hbm.1) | copy-start | bytes 626692
  0.6 8.5 %copy-start.2 = (s32[17408]{0:T(1024)S(1)}, s32[17408]{0:T(1024)}, u32[]{:S(2)}) copy-start(s32[17408]{0:T(1024)} %param.4) | copy-start | bytes 208900
  3.0 6.2 %copy-start.3 = (s32[1,3]{1,0:T(1,128)S(1)}, s32[1,3]{1,0:T(1,128)}, u32[]{:S(2)}) copy-start(s32[1,3]{1,0:T(1,128)} %moving.3) | copy-start | bytes 40
  3.0 14.7 %collective-permute-start = (f32[8,1024]{1,0:T(8,128)}, f32[8,1024]{1,0:T(8,128)S(1)}, u32[]{:S(2)}, u32[]{:S(2)}) collective-permute-start(f32[8,1024]{1,0:T(8,128)} %get-tuple-element.22), channel_id=1, source_target_pairs={{0,2},{2,0},{4,6},{6,4},{8,10},{10,8},{12,14},{14,12},{16,18},{18,... | collective-permute-start | bytes 98312 | tf_op jit(solution)/shard_map/ppermute | solution.py:52
  3.5 14.2 %collective-permute-start.1 = (f32[8,1024]{1,0:T(8,128)}, f32[8,1024]{1,0:T(8,128)S(1)}, u32[]{:S(2)}, u32[]{:S(2)}) collective-permute-start(f32[8,1024]{1,0:T(8,128)} %get-tuple-element.23), channel_id=1, source_target_pairs={{0,30},{2,4},{4,2},{6,8},{8,6},{10,12},{12,10},{14,16},{16,14},{18... | collective-permute-start | bytes 98312 | tf_op jit(solution)/shard_map/ppermute | solution.py:51
  18.9 1.5 %collective-permute-start.2 = (f32[3,3,40,128]{3,2,1,0:T(8,128)S(1)}, f32[3,3,40,128]{3,2,1,0:T(8,128)S(1)}, u32[]{:S(2)}, u32[]{:S(2)}) collective-permute-start(f32[3,3,40,128]{3,2,1,0:T(8,128)S(1)} %get-tuple-element.25), channel_id=1, source_target_pairs={{0,2},{2,0},{4,6},{6,4},{8,10},{10,8},{12,14},{14,12},{16,18},{18,... | collective-permute-start | bytes 552968 | tf_op jit(solution)/shard_map/ppermute | solution.py:52
  19.0 7.7 %collective-permute-start.3 = (f32[3,3,40,128]{3,2,1,0:T(8,128)S(1)}, f32[3,3,40,128]{3,2,1,0:T(8,128)S(1)}, u32[]{:S(2)}, u32[]{:S(2)}) collective-permute-start(f32[3,3,40,128]{3,2,1,0:T(8,128)S(1)} %get-tuple-element.26), channel_id=1, source_target_pairs={{0,30},{2,4},{4,2},{6,8},{8,6},{10,12},{12,10},{14,16},{16,14},{18... | collective-permute-start | bytes 552968 | tf_op jit(solution)/shard_map/ppermute | solution.py:51
  26.8 6.8 %collective-permute-start.4 = (f32[3,6,32,128]{3,2,1,0:T(8,128)S(1)}, f32[3,6,32,128]{3,2,1,0:T(8,128)S(1)}, u32[]{:S(2)}, u32[]{:S(2)}) collective-permute-start(f32[3,6,32,128]{3,2,1,0:T(8,128)S(1)} %get-tuple-element.28), channel_id=1, source_target_pairs={{0,1},{1,0},{2,3},{3,2},{4,5},{5,4},{6,7},{7,6},{8,9},{9,8},{10,11... | collective-permute-start | bytes 884744 | tf_op jit(solution)/shard_map/ppermute | solution.py:500
  34.7 2.0 %collective-permute-start.5 = (f32[3,2,56,128]{3,2,1,0:T(8,128)S(1)}, f32[3,2,56,128]{3,2,1,0:T(8,128)S(1)}, u32[]{:S(2)}, u32[]{:S(2)}) collective-permute-start(f32[3,2,56,128]{3,2,1,0:T(8,128)S(1)} %get-tuple-element.31), channel_id=1, source_target_pairs={{0,2},{2,0},{4,6},{6,4},{8,10},{10,8},{12,14},{14,12},{16,18},{18,... | collective-permute-start | bytes 516104 | tf_op jit(solution)/shard_map/ppermute | solution.py:52
  34.8 7.6 %collective-permute-start.6 = (f32[3,2,56,128]{3,2,1,0:T(8,128)S(1)}, f32[3,2,56,128]{3,2,1,0:T(8,128)S(1)}, u32[]{:S(2)}, u32[]{:S(2)}) collective-permute-start(f32[3,2,56,128]{3,2,1,0:T(8,128)S(1)} %get-tuple-element.32), channel_id=1, source_target_pairs={{0,30},{2,4},{4,2},{6,8},{8,6},{10,12},{12,10},{14,16},{16,14},{18... | collective-permute-start | bytes 516104 | tf_op jit(solution)/shard_map/ppermute | solution.py:51
  44.0 2.0 %collective-permute-start.7 = (f32[3,2,48,128]{3,2,1,0:T(8,128)S(1)}, f32[3,2,48,128]{3,2,1,0:T(8,128)S(1)}, u32[]{:S(2)}, u32[]{:S(2)}) collective-permute-start(f32[3,2,48,128]{3,2,1,0:T(8,128)S(1)} %get-tuple-element.34), channel_id=1, source_target_pairs={{0,2},{2,0},{4,6},{6,4},{8,10},{10,8},{12,14},{14,12},{16,18},{18,... | collective-permute-start | bytes 442376 | tf_op jit(solution)/shard_map/ppermute | solution.py:52
  44.0 7.3 %collective-permute-start.8 = (f32[3,2,48,128]{3,2,1,0:T(8,128)S(1)}, f32[3,2,48,128]{3,2,1,0:T(8,128)S(1)}, u32[]{:S(2)}, u32[]{:S(2)}) collective-permute-start(f32[3,2,48,128]{3,2,1,0:T(8,128)S(1)} %get-tuple-element.35), channel_id=1, source_target_pairs={{0,30},{2,4},{4,2},{6,8},{8,6},{10,12},{12,10},{14,16},{16,14},{18... | collective-permute-start | bytes 442376 | tf_op jit(solution)/shard_map/ppermute | solution.py:51
  53.0 2.0 %collective-permute-start.9 = (f32[3,2,48,128]{3,2,1,0:T(8,128)S(1)}, f32[3,2,48,128]{3,2,1,0:T(8,128)S(1)}, u32[]{:S(2)}, u32[]{:S(2)}) collective-permute-start(f32[3,2,48,128]{3,2,1,0:T(8,128)S(1)} %get-tuple-element.37), channel_id=1, source_target_pairs={{0,2},{2,0},{4,6},{6,4},{8,10},{10,8},{12,14},{14,12},{16,18},{18,... | collective-permute-start | bytes 442376 | tf_op jit(solution)/shard_map/ppermute | solution.py:52
  53.1 7.3 %collective-permute-start.10 = (f32[3,2,48,128]{3,2,1,0:T(8,128)S(1)}, f32[3,2,48,128]{3,2,1,0:T(8,128)S(1)}, u32[]{:S(2)}, u32[]{:S(2)}) collective-permute-start(f32[3,2,48,128]{3,2,1,0:T(8,128)S(1)} %get-tuple-element.38), channel_id=1, source_target_pairs={{0,30},{2,4},{4,2},{6,8},{8,6},{10,12},{12,10},{14,16},{16,14},{18... | collective-permute-start | bytes 442376 | tf_op jit(solution)/shard_map/ppermute | solution.py:51
  62.0 2.0 %collective-permute-start.11 = (f32[3,2,40,128]{3,2,1,0:T(8,128)S(1)}, f32[3,2,40,128]{3,2,1,0:T(8,128)S(1)}, u32[]{:S(2)}, u32[]{:S(2)}) collective-permute-start(f32[3,2,40,128]{3,2,1,0:T(8,128)S(1)} %get-tuple-element.40), channel_id=1, source_target_pairs={{0,2},{2,0},{4,6},{6,4},{8,10},{10,8},{12,14},{14,12},{16,18},{18,... | collective-permute-start | bytes 368648 | tf_op jit(solution)/shard_map/ppermute | solution.py:52
  62.1 7.1 %collective-permute-start.12 = (f32[3,2,40,128]{3,2,1,0:T(8,128)S(1)}, f32[3,2,40,128]{3,2,1,0:T(8,128)S(1)}, u32[]{:S(2)}, u32[]{:S(2)}) collective-permute-start(f32[3,2,40,128]{3,2,1,0:T(8,128)S(1)} %get-tuple-element.41), channel_id=1, source_target_pairs={{0,30},{2,4},{4,2},{6,8},{8,6},{10,12},{12,10},{14,16},{16,14},{18... | collective-permute-start | bytes 368648 | tf_op jit(solution)/shard_map/ppermute | solution.py:51

commit v5 on v4

--- a/solution.py
+++ b/solution.py
@@ -184,68 +184,72 @@
 
 
 def staying_kernel(
-    moving, cells, offsets, vorts, total, dense, table, planes_a, lines_a, planes_b, lines_b, *, tiles_per_chunk
+    moving, cells, offsets, vorts, total, dense, table, planes_a, lines_a, planes_b, lines_b, *, per_chunk
 ):
     first_stay = moving[0, 0] + moving[0, 1]
     live_len = moving[0, 2]
     tiles = cells.shape[0]
+    chunks = tiles // per_chunk
     total[...] = jnp.zeros_like(total)
-    for tile in range(tiles):
-        lanes = slice(tile * 128, (tile + 1) * 128)
-        for dim in range(3):
-            dense[dim, tile : tile + 1] = offsets[dim : dim + 1, lanes]
-            dense[3 + dim, tile : tile + 1] = vorts[dim : dim + 1, lanes]
-
-    def one_group(group, carry):
-        rows = pl.ds(pl.multiple_of(group * 8, 8), 8)
-        slot = (
-            group * 1024
-            + lax.broadcasted_iota(jnp.int32, (8, 128), 0) * 128
-            + lax.broadcasted_iota(jnp.int32, (8, 128), 1)
-        )
-        keep = (slot >= first_stay) & (slot < live_len)
-        prepare(
-            cells[rows],
-            [dense[dim, rows] for dim in range(3)],
-            [jnp.where(keep, dense[3 + dim, rows], 0.0) for dim in range(3)],
-            table,
-            rows,
-        )
-        return carry
-
-    lax.fori_loop(0, tiles // 8, one_group, 0)
-    chunks = tiles // tiles_per_chunk
-    spread(table, 0, tiles_per_chunk, planes_a, lines_a)
+
+    def make(chunk, count, planes, lines):
+        first = pl.multiple_of(chunk * per_chunk, 8)
+        for tile in range(count):
+            lanes = pl.ds(pl.multiple_of((first + tile) * 128, 128), 128)
+            for dim in range(3):
+                dense[dim, tile : tile + 1] = offsets[dim : dim + 1, lanes]
+                dense[3 + dim, tile : tile + 1] = vorts[dim : dim + 1, lanes]
+        slot = lax.broadcasted_iota(jnp.int32, (8, 128), 0) * 128
+        slot = slot + lax.broadcasted_iota(jnp.int32, (8, 128), 1)
+        for group in range(count // 8):
+            rows = slice(group * 8, (group + 1) * 8)
+            own_slot = slot + (first + group * 8) * 128
+            keep = (own_slot >= first_stay) & (own_slot < live_len)
+            prepare(
+                cells[pl.ds(pl.multiple_of(first + group * 8, 8), 8)],
+                [dense[dim, rows] for dim in range(3)],
+                [jnp.where(keep, dense[3 + dim, rows], 0.0) for dim in range(3)],
+                table,
+                rows,
+            )
+        spread(table, 0, count, planes, lines)
+
+    make(0, per_chunk, planes_a, lines_a)
 
     def two_chunks(pair, carry):
-        spread(table, (2 * pair + 1) * tiles_per_chunk, tiles_per_chunk, planes_b, lines_b)
+        make(2 * pair + 1, per_chunk, planes_b, lines_b)
         total[...] += product(planes_a, lines_a)
-        spread(table, (2 * pair + 2) * tiles_per_chunk, tiles_per_chunk, planes_a, lines_a)
+        make(2 * pair + 2, per_chunk, planes_a, lines_a)
         total[...] += product(planes_b, lines_b)
         return carry
 
     lax.fori_loop(0, (chunks - 1) // 2, two_chunks, 0)
+    done, spare = (planes_a, lines_a), (planes_b, lines_b)
     if chunks % 2 == 0:
-        spread(table, (chunks - 1) * tiles_per_chunk, tiles_per_chunk, planes_b, lines_b)
-        total[...] += product(planes_a, lines_a)
-        total[...] += product(planes_b, lines_b)
-    else:
-        total[...] += product(planes_a, lines_a)
+        make(chunks - 1, per_chunk, *spare)
+        total[...] += product(*done)
+        done, spare = spare, done
+    rest = tiles % per_chunk
+    if rest:
+        make(chunks, rest, *spare)
+        total[...] += product(*done)
+        done = tuple(ref.at[:, : rest * 128] for ref in spare)
+    total[...] += product(*done)
 
 
 def deposit_staying(moving, cells, part_offset, part_vort):
     tiles = cells.shape[0]
     slots = tiles * 128
-    per_chunk = 17
+    per_chunk = 16
     chunk = per_chunk * 128
     return pl.pallas_call(
-        functools.partial(staying_kernel, tiles_per_chunk=per_chunk),
+        functools.partial(staying_kernel, per_chunk=per_chunk),
         in_specs=[in_smem()] + in_vmem(3),
         out_specs=in_vmem(1)[0],
         out_shape=jax.ShapeDtypeStruct((SPREAD, 3 * NZ), F32),
         scratch_shapes=[
-            pltpu.VMEM((6, tiles, 128), F32),
-            pltpu.VMEM((QUANTITIES, tiles, 128), F32),
+            pltpu.VMEM((6, per_chunk, 128), F32),
+            pltpu.VMEM((QUANTITIES, per_chunk, 128), F32),
         ]
         + [pltpu.VMEM((SPREAD, chunk), BF16), pltpu.VMEM((3 * NZ, chunk), BF16)] * 2,
         compiler_params=params(),
@@ -310,8 +314,11 @@
     return jnp.where(ids < 4, low, high)
 
 
-def edged_plane(mine, other):
-    return jnp.concatenate([mine, edge_rows(other[:8], other[-8:])], axis=0)
+def edged_plane(mine, other, ends_only=False):
+    edges = edge_rows(other[:8], other[-8:])
+    if ends_only:
+        return jnp.concatenate([mine[-8:], edges, mine[:8]], axis=0)
+    return jnp.concatenate([mine, edges], axis=0)
 
 
 def roll_rows(value, shift):
@@ -323,8 +330,10 @@
 
 
 def relax(fields, sources):
-    ids = lax.broadcasted_iota(jnp.int32, (ROWS, NZ), 0)
-    frozen = (ids > CY) & (ids < ROWS - 1)
+    rows = fields[0].shape[0]
+    first_edge = CY if rows == ROWS else 8
+    ids = lax.broadcasted_iota(jnp.int32, (rows, NZ), 0)
+    frozen = (ids > first_edge) & (ids < first_edge + 7)
     for sweep in range(SWEEPS):
         fresh = list(fields)
         last = sweep == SWEEPS - 1
@@ -337,9 +346,10 @@
     return fields[2 : CX + 2]
 
 
-def pack_rows(a, b, rows):
+def pack_rows(value, rows):
     ids = lax.broadcasted_iota(jnp.int32, (8, NZ), 0)
-    first, last = b[:8], b[CY - 8 :]
+    a, b = value[:CY], value[CY:]
+    first, last = b[:8], b[-8:]
     if rows == CY + 8:
         return jnp.concatenate([a, jnp.where(ids < 4, first, last)], axis=0)
     if rows == CY + 16:
@@ -349,10 +359,10 @@
 
 
 def unpack_rows(packed):
-    a, rest = packed[:CY], packed[CY:]
-    first, last = rest[:8], rest[rest.shape[0] - 8 :]
-    middle = rest[8:16] if rest.shape[0] == 24 else last
-    return a, jnp.concatenate([first, middle, middle, last], axis=0)
+    a, b = packed[:CY], packed[CY:]
+    if b.shape[0] == 24:
+        b = jnp.concatenate([b[:16], b[8:]], axis=0)
+    return a, b
 
 
 def hand_out(potential, to_within, to_across):
@@ -360,10 +370,7 @@
     rows = to_within.shape[2]
     for comp in range(3):
         for x in range(2):
-            low, high = (
-                pack_rows(potential[comp, at, :CY], potential[comp, at, CY:], rows)
-                for at in (x, CX - 2 + x)
-            )
+            low, high = (pack_rows(potential[comp, at], rows) for at in (x, CX - 2 + x))
             to_within[comp, x] = jnp.where(even, high, low)
             to_across[comp, x] = jnp.where(even, low, high)
 
@@ -392,7 +399,7 @@
         high = main[CY - 8 : CY] + jnp.where(ids == 7, edges, 0.0)
         return jnp.concatenate([low, main[8 : CY - 8], high], axis=0)
 
-    def one_component(comp, carry):
+    for comp in range(3):
         sources = ([], [])
         for x in range(CX + 2):
             a = mine[comp, x]
@@ -410,9 +417,6 @@
             fields = relax(fields, sources[block])
             for x in range(CX):
                 potential[comp, x, block * CY : (block + 1) * CY] = fields[x][:CY]
-        return carry
-
-    lax.fori_loop(0, 3, one_component, 0)
     hand_out(potential, to_within, to_across)
 
 
@@ -424,23 +428,27 @@
 
     below = [chosen(jnp.logical_not(even), x) for x in range(2)]
     above = [chosen(even, x) for x in range(2)]
-    middle = [(potential[comp, x, :CY], potential[comp, x, CY:]) for x in range(CX)]
+    middle = [unpack_rows(potential[comp, x]) for x in range(CX)]
     return below + middle + above
 
 
 def next_kernel(omega, before, got_within, got_across, potential, to_within, to_across):
-    def one_component(comp, carry):
+    ends_only = before.shape[2] == CY + 16
+    for comp in range(3):
         pairs = gathered(before, got_within, got_across, comp)
         charge = [(omega[comp, x, :CY], omega[comp, x, CY:]) for x in range(CX + 2)]
-        for block in range(2):
-            fields = [edged_plane(pair[block], pair[1 - block]) for pair in pairs]
-            sources = [edged_plane(pair[block], pair[1 - block]) for pair in charge]
-            fields = relax(fields, sources)
-            for x in range(CX):
-                potential[comp, x, block * CY : (block + 1) * CY] = fields[x][:CY]
-        return carry
-
-    lax.fori_loop(0, 3, one_component, 0)
+        fields = relax([edged_plane(a, b) for a, b in pairs], [edged_plane(a, b) for a, b in charge])
+        for x in range(CX):
+            potential[comp, x, :CY] = fields[x][:CY]
+        fields = relax(
+            [edged_plane(b, a, ends_only) for a, b in pairs],
+            [edged_plane(b, a, ends_only) for a, b in charge],
+        )
+        first = 16 if ends_only else 0
+        last = 0 if ends_only else CY - 8
+        for x in range(CX):
+            potential[comp, x, CY : CY + 8] = fields[x][first : first + 8]
+            potential[comp, x, CY + 8 :] = fields[x][last : last + 8]
     hand_out(potential, to_within, to_across)
 
 
@@ -498,16 +506,16 @@
         *swap_x(to_within, to_across),
     )
     other = lax.ppermute(message, "gy", [(0, 1), (1, 0)])
-    slab = array(3, CX, 2 * CY, NZ)
+    whole, ends = array(3, CX, 2 * CY, NZ), array(3, CX, CY + 16, NZ)
     depths = [CY + 24, CY + 16, CY + 16, CY + 8]
     edge = array(3, 2, depths[0], NZ)
     omega, potential, to_within, to_across = on_vmem(
-        first_kernel, (array(3, planes, 2 * CY, NZ), slab, edge, edge), mine, other
+        first_kernel, (array(3, planes, 2 * CY, NZ), whole, edge, edge), mine, other
     )
     for depth in depths[1:]:
         edge = array(3, 2, depth, NZ)
         potential, to_within, to_across = on_vmem(
-            next_kernel, (slab, edge, edge), omega, potential, *swap_x(to_within, to_across)
+            next_kernel, (ends, edge, edge), omega, potential, *swap_x(to_within, to_across)
         )
     block = array(3, CX, CY, NZ)
     return on_vmem(

time: 70.3 us -> 69.8 us (level)
    pallas_call x6, Pallas kernels: 6.95 us -> 5.73 us  [on_vmem(): pl.pallas_call(kernel, in_specs=in_vmem(len(args)), out_specs=tuple(in_vm...]
    pallas_call x1, Pallas kernels: 8.54 us -> 9.3 us  [deposit_staying(): pl.pallas_call(functools.partial(staying_kernel, per_chunk=per_chunk), in...]
  transfers between devices with their start and end apart: 13 -> 13, of which waited for: 7 -> 7; matrix products, arithmetic and copies ran while one was open for 0% -> 0% of each run, Pallas kernels for 12% -> 13%
where the time goes in v5:
time: 69.8 us; the launch traced here: 69.7 us
  waiting for transfers between devices  33.7 us (48%)
  Pallas kernels  18.5 us (27%)
  starting transfers between devices  16.6 us (24%)
  between operations  0.78 us (1%)
    ppermute x6, waiting for transfers between devices, swap_x(): got_across = lax.ppermute(to_across, 'gx', across(n))  27.7 us
    ppermute x6, starting transfers between devices, swap_x(): got_across = lax.ppermute(to_across, 'gx', across(n))  14.2 us
    pallas_call x1, Pallas kernels, deposit_staying(): pl.pallas_call(functools.partial(staying_kernel, per_chunk=per_chunk), in...  9.3 us
    pallas_call x6, Pallas kernels, on_vmem(): pl.pallas_call(kernel, in_specs=in_vmem(len(args)), out_specs=tuple(in_vm...  5.73 us
    ppermute x1, waiting for transfers between devices, two_block_solve(): other = lax.ppermute(message, 'gy', [(0, 1), (1, 0)])  5.2 us
    pallas_call x1, Pallas kernels, pack_leaving(): pl.pallas_call(functools.partial(leaving_kernel, capacity=capacity), in_s...  2.33 us
    ppermute x1, starting transfers between devices, two_block_solve(): other = lax.ppermute(message, 'gy', [(0, 1), (1, 0)])  1.58 us
  transfers between devices with their start and end apart: 13, of which 7 were waited for; matrix products, arithmetic and copies ran while one was open for 0% of the time, Pallas kernels for 13%

profile of v5, /device:TPU:0, one launch (start us, length us, event | category | flops | bytes accessed | tf_op | source)
XLA Modules:
  0.0 69.7 jit_solution(18026773679029968064)
XLA Ops:
  0.6 0.0 copy-start
  0.6 0.0 copy-start.1
  0.6 0.0 copy-start.2
  0.7 2.3 %shard_map.60 = (f32[8,1024]{1,0:T(8,128)}, f32[8,1024]{1,0:T(8,128)}) custom-call(s32[1,3]{1,0:T(1,128)} %moving.3, s32[136,128]{1,0:T(8,128)} %bitcast.1, f32[3,17408]{1,0:T(4,128)} %offset_hbm.1, f32[3,17408]{1,0:T(4,128)} %vort_hbm.1), custom_call_target="tpu_custom_call" | custom-call | tf_op jit(solution)/shard_map/pallas_call | solution.py:170
  3.0 0.0 copy-start.3
  3.0 0.5 collective-permute-start
  3.5 5.6 %collective-permute-start.1 = (f32[8,1024]{1,0:T(8,128)}, f32[8,1024]{1,0:T(8,128)S(1)}, u32[]{:S(2)}, u32[]{:S(2)}) collective-permute-start(f32[8,1024]{1,0:T(8,128)} %get-tuple-element.23), channel_id=1, source_target_pairs={{0,30},{2,4},{4,2},{6,8},{8,6},{10,12},{12,10},{14,16},{16,14},{18... | collective-permute-start | bytes 98312 | tf_op jit(solution)/shard_map/ppermute | solution.py:51
  9.2 0.0 copy-done
  9.2 0.0 copy-done.1
  9.2 0.0 copy-done.2
  9.2 0.0 copy-done.3
  9.2 9.3 %shard_map.59.total = f32[288,384]{1,0:T(8,128)S(1)} custom-call(s32[1,3]{1,0:T(1,128)S(1)} %copy-done.3, s32[136,128]{1,0:T(8,128)S(1)} %bitcast.2, f32[3,17408]{1,0:T(4,128)S(1)} %copy-done, f32[3,17408]{1,0:T(4,128)S(1)} %copy-done.1), custom_call_target="tpu_custom_call" | custom-call | flops 3850371072 | bytes 487424 | tf_op jit(solution)/shard_map/pallas_call | solution.py:245
  18.5 0.0 collective-permute-done.got_within
  18.5 0.0 collective-permute-done.1.got_across
  18.5 1.2 %shard_map.61 = (f32[3,7,40,128]{3,2,1,0:T(8,128)S(1)}, f32[3,3,40,128]{3,2,1,0:T(8,128)S(1)}, f32[3,3,40,128]{3,2,1,0:T(8,128)S(1)}) custom-call(f32[288,384]{1,0:T(8,128)S(1)} %shard_map.59.total, f32[8,1024]{1,0:T(8,128)S(1)} %collective-permute-done.got_within, f32[8,1024]{1,0:T(8,128)S(1)} %collective-permute-done.1.got_across), custom_call_target="tpu_custom_call" | custom-call | tf_op jit(solution)/shard_map/pallas_call | solution.py:297
  19.7 0.1 collective-permute-start.2
  19.7 0.6 collective-permute-start.3
  20.4 0.8 %collective-permute-done.2.got_within = f32[3,3,40,128]{3,2,1,0:T(8,128)S(1)} collective-permute-done((f32[3,3,40,128]{3,2,1,0:T(8,128)S(1)}, f32[3,3,40,128]{3,2,1,0:T(8,128)S(1)}, u32[]{:S(2)}, u32[]{:S(2)}) %collective-permute-start.2) | collective-permute-done | bytes 184352 | tf_op jit(solution)/shard_map/ppermute | solution.py:52
  21.1 6.3 %collective-permute-done.3.got_across = f32[3,3,40,128]{3,2,1,0:T(8,128)S(1)} collective-permute-done((f32[3,3,40,128]{3,2,1,0:T(8,128)S(1)}, f32[3,3,40,128]{3,2,1,0:T(8,128)S(1)}, u32[]{:S(2)}, u32[]{:S(2)}) %collective-permute-start.3) | collective-permute-done | bytes 184352 | tf_op jit(solution)/shard_map/ppermute | solution.py:51
  27.5 0.1 shard_map.62
  27.5 1.6 %collective-permute-start.4 = (f32[3,6,32,128]{3,2,1,0:T(8,128)S(1)}, f32[3,6,32,128]{3,2,1,0:T(8,128)S(1)}, u32[]{:S(2)}, u32[]{:S(2)}) collective-permute-start(f32[3,6,32,128]{3,2,1,0:T(8,128)S(1)} %get-tuple-element.28), channel_id=1, source_target_pairs={{0,1},{1,0},{2,3},{3,2},{4,5},{5,4},{6,7},{7,6},{8,9},{9,8},{10,11... | collective-permute-start | bytes 884744 | tf_op jit(solution)/shard_map/ppermute | solution.py:508
  29.1 5.2 %collective-permute-done.4.other = f32[3,6,32,128]{3,2,1,0:T(8,128)S(1)} collective-permute-done((f32[3,6,32,128]{3,2,1,0:T(8,128)S(1)}, f32[3,6,32,128]{3,2,1,0:T(8,128)S(1)}, u32[]{:S(2)}, u32[]{:S(2)}) %collective-permute-start.4) | collective-permute-done | bytes 294944 | tf_op jit(solution)/shard_map/ppermute | solution.py:508
  34.3 0.9 %shard_map.63 = (f32[3,6,64,128]{3,2,1,0:T(8,128)S(1)}, f32[3,4,64,128]{3,2,1,0:T(8,128)S(1)}, f32[3,2,56,128]{3,2,1,0:T(8,128)S(1)}, f32[3,2,56,128]{3,2,1,0:T(8,128)S(1)}) custom-call(f32[3,6,40,128]{3,2,1,0:T(8,128)S(1)} %get-tuple-element.27.mine, f32[3,6,32,128]{3,2,1,0:T(8,128)S(1)} %collective-permute-done.4.other), custom_call_target="tpu_custom_call" | custom-call | tf_op jit(solution)/shard_map/pallas_call | solution.py:491
  35.2 0.1 collective-permute-start.5
  35.3 2.0 %collective-permute-start.6 = (f32[3,2,56,128]{3,2,1,0:T(8,128)S(1)}, f32[3,2,56,128]{3,2,1,0:T(8,128)S(1)}, u32[]{:S(2)}, u32[]{:S(2)}) collective-permute-start(f32[3,2,56,128]{3,2,1,0:T(8,128)S(1)} %get-tuple-element.32), channel_id=1, source_target_pairs={{0,30},{2,4},{4,2},{6,8},{8,6},{10,12},{12,10},{14,16},{16,14},{18... | collective-permute-start | bytes 516104 | tf_op jit(solution)/shard_map/ppermute | solution.py:51
  37.3 0.0 collective-permute-done.5.got_within
  37.3 5.6 %collective-permute-done.6.got_across = f32[3,2,56,128]{3,2,1,0:T(8,128)S(1)} collective-permute-done((f32[3,2,56,128]{3,2,1,0:T(8,128)S(1)}, f32[3,2,56,128]{3,2,1,0:T(8,128)S(1)}, u32[]{:S(2)}, u32[]{:S(2)}) %collective-permute-start.6) | collective-permute-done | bytes 172064 | tf_op jit(solution)/shard_map/ppermute | solution.py:51
  42.9 1.3 %shard_map.64 = (f32[3,4,48,128]{3,2,1,0:T(8,128)S(1)}, f32[3,2,48,128]{3,2,1,0:T(8,128)S(1)}, f32[3,2,48,128]{3,2,1,0:T(8,128)S(1)}) custom-call(f32[3,6,64,128]{3,2,1,0:T(8,128)S(1)} %get-tuple-element.29.omega, f32[3,4,64,128]{3,2,1,0:T(8,128)S(1)} %get-tuple-element.30.before, f32[3,2,56,128]{3,2,1,0:T(8,128)S(1)} %collective-permute-done.5.got_within, ...), custom_call_target="tpu_custom_call" | custom-call | tf_op jit(solution)/shard_map/pallas_call | solution.py:491
  44.2 0.1 collective-permute-start.7
  44.3 2.0 %collective-permute-start.8 = (f32[3,2,48,128]{3,2,1,0:T(8,128)S(1)}, f32[3,2,48,128]{3,2,1,0:T(8,128)S(1)}, u32[]{:S(2)}, u32[]{:S(2)}) collective-permute-start(f32[3,2,48,128]{3,2,1,0:T(8,128)S(1)} %get-tuple-element.35), channel_id=1, source_target_pairs={{0,30},{2,4},{4,2},{6,8},{8,6},{10,12},{12,10},{14,16},{16,14},{18... | collective-permute-start | bytes 442376 | tf_op jit(solution)/shard_map/ppermute | solution.py:51
  46.3 0.0 collective-permute-done.7.got_within
  46.3 5.4 %collective-permute-done.8.got_across = f32[3,2,48,128]{3,2,1,0:T(8,128)S(1)} collective-permute-done((f32[3,2,48,128]{3,2,1,0:T(8,128)S(1)}, f32[3,2,48,128]{3,2,1,0:T(8,128)S(1)}, u32[]{:S(2)}, u32[]{:S(2)}) %collective-permute-start.8) | collective-permute-done | bytes 147488 | tf_op jit(solution)/shard_map/ppermute | solution.py:51
  51.6 1.2 %shard_map.65 = (f32[3,4,48,128]{3,2,1,0:T(8,128)S(1)}, f32[3,2,48,128]{3,2,1,0:T(8,128)S(1)}, f32[3,2,48,128]{3,2,1,0:T(8,128)S(1)}) custom-call(f32[3,6,64,128]{3,2,1,0:T(8,128)S(1)} %get-tuple-element.29.omega, f32[3,4,48,128]{3,2,1,0:T(8,128)S(1)} %get-tuple-element.33.before, f32[3,2,48,128]{3,2,1,0:T(8,128)S(1)} %collective-permute-done.7.got_within, ...), custom_call_target="tpu_custom_call" | custom-call | tf_op jit(solution)/shard_map/pallas_call | solution.py:491
  52.9 0.1 collective-permute-start.9
  52.9 2.0 %collective-permute-start.10 = (f32[3,2,48,128]{3,2,1,0:T(8,128)S(1)}, f32[3,2,48,128]{3,2,1,0:T(8,128)S(1)}, u32[]{:S(2)}, u32[]{:S(2)}) collective-permute-start(f32[3,2,48,128]{3,2,1,0:T(8,128)S(1)} %get-tuple-element.38), channel_id=1, source_target_pairs={{0,30},{2,4},{4,2},{6,8},{8,6},{10,12},{12,10},{14,16},{16,14},{18... | collective-permute-start | bytes 442376 | tf_op jit(solution)/shard_map/ppermute | solution.py:51
  54.9 0.0 collective-permute-done.9.got_within
  54.9 5.4 %collective-permute-done.10.got_across = f32[3,2,48,128]{3,2,1,0:T(8,128)S(1)} collective-permute-done((f32[3,2,48,128]{3,2,1,0:T(8,128)S(1)}, f32[3,2,48,128]{3,2,1,0:T(8,128)S(1)}, u32[]{:S(2)}, u32[]{:S(2)}) %collective-permute-start.10) | collective-permute-done | bytes 147488 | tf_op jit(solution)/shard_map/ppermute | solution.py:51
  60.3 1.2 %shard_map.66 = (f32[3,4,48,128]{3,2,1,0:T(8,128)S(1)}, f32[3,2,40,128]{3,2,1,0:T(8,128)S(1)}, f32[3,2,40,128]{3,2,1,0:T(8,128)S(1)}) custom-call(f32[3,6,64,128]{3,2,1,0:T(8,128)S(1)} %get-tuple-element.29.omega, f32[3,4,48,128]{3,2,1,0:T(8,128)S(1)} %get-tuple-element.36.before, f32[3,2,48,128]{3,2,1,0:T(8,128)S(1)} %collective-permute-done.9.got_within, ...), custom_call_target="tpu_custom_call" | custom-call | tf_op jit(solution)/shard_map/pallas_call | solution.py:491
  61.5 0.1 collective-permute-start.11
  61.6 2.0 %collective-permute-start.12 = (f32[3,2,40,128]{3,2,1,0:T(8,128)S(1)}, f32[3,2,40,128]{3,2,1,0:T(8,128)S(1)}, u32[]{:S(2)}, u32[]{:S(2)}) collective-permute-start(f32[3,2,40,128]{3,2,1,0:T(8,128)S(1)} %get-tuple-element.41), channel_id=1, source_target_pairs={{0,30},{2,4},{4,2},{6,8},{8,6},{10,12},{12,10},{14,16},{16,14},{18... | collective-permute-start | bytes 368648 | tf_op jit(solution)/shard_map/ppermute | solution.py:51
  63.6 0.0 collective-permute-done.11.got_within
  63.6 5.1 %collective-permute-done.12.got_across = f32[3,2,40,128]{3,2,1,0:T(8,128)S(1)} collective-permute-done((f32[3,2,40,128]{3,2,1,0:T(8,128)S(1)}, f32[3,2,40,128]{3,2,1,0:T(8,128)S(1)}, u32[]{:S(2)}, u32[]{:S(2)}) %collective-permute-start.12) | collective-permute-done | bytes 122912 | tf_op jit(solution)/shard_map/ppermute | solution.py:51
  68.7 1.0 %shard_map.67 = (f32[3,4,32,128]{3,2,1,0:T(8,128)}, f32[3,4,32,128]{3,2,1,0:T(8,128)}) custom-call(f32[3,6,64,128]{3,2,1,0:T(8,128)S(1)} %get-tuple-element.29.omega, f32[3,4,48,128]{3,2,1,0:T(8,128)S(1)} %get-tuple-element.39.potential, f32[3,2,40,128]{3,2,1,0:T(8,128)S(1)} %collective-permute-done.11.got_within, ...), custom_call_target="tpu_custom_call" | custom-call | tf_op jit(solution)/shard_map/pallas_call | solution.py:491
Async XLA Ops:
  0.6 8.5 %copy-start = (f32[3,17408]{1,0:T(4,128)S(1)}, f32[3,17408]{1,0:T(4,128)}, u32[]{:S(2)}) copy-start(f32[3,17408]{1,0:T(4,128)} %offset_hbm.1) | copy-start | bytes 626692
  0.6 8.5 %copy-start.1 = (f32[3,17408]{1,0:T(4,128)S(1)}, f32[3,17408]{1,0:T(4,128)}, u32[]{:S(2)}) copy-start(f32[3,17408]{1,0:T(4,128)} %vort_hbm.1) | copy-start | bytes 626692
  0.6 8.5 %copy-start.2 = (s32[17408]{0:T(1024)S(1)}, s32[17408]{0:T(1024)}, u32[]{:S(2)}) copy-start(s32[17408]{0:T(1024)} %param.4) | copy-start | bytes 208900
  3.0 6.2 %copy-start.3 = (s32[1,3]{1,0:T(1,128)S(1)}, s32[1,3]{1,0:T(1,128)}, u32[]{:S(2)}) copy-start(s32[1,3]{1,0:T(1,128)} %moving.3) | copy-start | bytes 40
  3.0 15.5 %collective-permute-start = (f32[8,1024]{1,0:T(8,128)}, f32[8,1024]{1,0:T(8,128)S(1)}, u32[]{:S(2)}, u32[]{:S(2)}) collective-permute-start(f32[8,1024]{1,0:T(8,128)} %get-tuple-element.22), channel_id=1, source_target_pairs={{0,2},{2,0},{4,6},{6,4},{8,10},{10,8},{12,14},{14,12},{16,18},{18,... | collective-permute-start | bytes 98312 | tf_op jit(solution)/shard_map/ppermute | solution.py:52
  3.5 15.0 %collective-permute-start.1 = (f32[8,1024]{1,0:T(8,128)}, f32[8,1024]{1,0:T(8,128)S(1)}, u32[]{:S(2)}, u32[]{:S(2)}) collective-permute-start(f32[8,1024]{1,0:T(8,128)} %get-tuple-element.23), channel_id=1, source_target_pairs={{0,30},{2,4},{4,2},{6,8},{8,6},{10,12},{12,10},{14,16},{16,14},{18... | collective-permute-start | bytes 98312 | tf_op jit(solution)/shard_map/ppermute | solution.py:51
  19.7 1.5 %collective-permute-start.2 = (f32[3,3,40,128]{3,2,1,0:T(8,128)S(1)}, f32[3,3,40,128]{3,2,1,0:T(8,128)S(1)}, u32[]{:S(2)}, u32[]{:S(2)}) collective-permute-start(f32[3,3,40,128]{3,2,1,0:T(8,128)S(1)} %get-tuple-element.25), channel_id=1, source_target_pairs={{0,2},{2,0},{4,6},{6,4},{8,10},{10,8},{12,14},{14,12},{16,18},{18,... | collective-permute-start | bytes 552968 | tf_op jit(solution)/shard_map/ppermute | solution.py:52
  19.7 7.7 %collective-permute-start.3 = (f32[3,3,40,128]{3,2,1,0:T(8,128)S(1)}, f32[3,3,40,128]{3,2,1,0:T(8,128)S(1)}, u32[]{:S(2)}, u32[]{:S(2)}) collective-permute-start(f32[3,3,40,128]{3,2,1,0:T(8,128)S(1)} %get-tuple-element.26), channel_id=1, source_target_pairs={{0,30},{2,4},{4,2},{6,8},{8,6},{10,12},{12,10},{14,16},{16,14},{18... | collective-permute-start | bytes 552968 | tf_op jit(solution)/shard_map/ppermute | solution.py:51
  27.5 6.8 %collective-permute-start.4 = (f32[3,6,32,128]{3,2,1,0:T(8,128)S(1)}, f32[3,6,32,128]{3,2,1,0:T(8,128)S(1)}, u32[]{:S(2)}, u32[]{:S(2)}) collective-permute-start(f32[3,6,32,128]{3,2,1,0:T(8,128)S(1)} %get-tuple-element.28), channel_id=1, source_target_pairs={{0,1},{1,0},{2,3},{3,2},{4,5},{5,4},{6,7},{7,6},{8,9},{9,8},{10,11... | collective-permute-start | bytes 884744 | tf_op jit(solution)/shard_map/ppermute | solution.py:508
  35.2 2.1 %collective-permute-start.5 = (f32[3,2,56,128]{3,2,1,0:T(8,128)S(1)}, f32[3,2,56,128]{3,2,1,0:T(8,128)S(1)}, u32[]{:S(2)}, u32[]{:S(2)}) collective-permute-start(f32[3,2,56,128]{3,2,1,0:T(8,128)S(1)} %get-tuple-element.31), channel_id=1, source_target_pairs={{0,2},{2,0},{4,6},{6,4},{8,10},{10,8},{12,14},{14,12},{16,18},{18,... | collective-permute-start | bytes 516104 | tf_op jit(solution)/shard_map/ppermute | solution.py:52
  35.3 7.6 %collective-permute-start.6 = (f32[3,2,56,128]{3,2,1,0:T(8,128)S(1)}, f32[3,2,56,128]{3,2,1,0:T(8,128)S(1)}, u32[]{:S(2)}, u32[]{:S(2)}) collective-permute-start(f32[3,2,56,128]{3,2,1,0:T(8,128)S(1)} %get-tuple-element.32), channel_id=1, source_target_pairs={{0,30},{2,4},{4,2},{6,8},{8,6},{10,12},{12,10},{14,16},{16,14},{18... | collective-permute-start | bytes 516104 | tf_op jit(solution)/shard_map/ppermute | solution.py:51
  44.2 2.1 %collective-permute-start.7 = (f32[3,2,48,128]{3,2,1,0:T(8,128)S(1)}, f32[3,2,48,128]{3,2,1,0:T(8,128)S(1)}, u32[]{:S(2)}, u32[]{:S(2)}) collective-permute-start(f32[3,2,48,128]{3,2,1,0:T(8,128)S(1)} %get-tuple-element.34), channel_id=1, source_target_pairs={{0,2},{2,0},{4,6},{6,4},{8,10},{10,8},{12,14},{14,12},{16,18},{18,... | collective-permute-start | bytes 442376 | tf_op jit(solution)/shard_map/ppermute | solution.py:52
  44.3 7.3 %collective-permute-start.8 = (f32[3,2,48,128]{3,2,1,0:T(8,128)S(1)}, f32[3,2,48,128]{3,2,1,0:T(8,128)S(1)}, u32[]{:S(2)}, u32[]{:S(2)}) collective-permute-start(f32[3,2,48,128]{3,2,1,0:T(8,128)S(1)} %get-tuple-element.35), channel_id=1, source_target_pairs={{0,30},{2,4},{4,2},{6,8},{8,6},{10,12},{12,10},{14,16},{16,14},{18... | collective-permute-start | bytes 442376 | tf_op jit(solution)/shard_map/ppermute | solution.py:51
  52.9 2.1 %collective-permute-start.9 = (f32[3,2,48,128]{3,2,1,0:T(8,128)S(1)}, f32[3,2,48,128]{3,2,1,0:T(8,128)S(1)}, u32[]{:S(2)}, u32[]{:S(2)}) collective-permute-start(f32[3,2,48,128]{3,2,1,0:T(8,128)S(1)} %get-tuple-element.37), channel_id=1, source_target_pairs={{0,2},{2,0},{4,6},{6,4},{8,10},{10,8},{12,14},{14,12},{16,18},{18,... | collective-permute-start | bytes 442376 | tf_op jit(solution)/shard_map/ppermute | solution.py:52
  52.9 7.3 %collective-permute-start.10 = (f32[3,2,48,128]{3,2,1,0:T(8,128)S(1)}, f32[3,2,48,128]{3,2,1,0:T(8,128)S(1)}, u32[]{:S(2)}, u32[]{:S(2)}) collective-permute-start(f32[3,2,48,128]{3,2,1,0:T(8,128)S(1)} %get-tuple-element.38), channel_id=1, source_target_pairs={{0,30},{2,4},{4,2},{6,8},{8,6},{10,12},{12,10},{14,16},{16,14},{18... | collective-permute-start | bytes 442376 | tf_op jit(solution)/shard_map/ppermute | solution.py:51
  61.5 2.1 %collective-permute-start.11 = (f32[3,2,40,128]{3,2,1,0:T(8,128)S(1)}, f32[3,2,40,128]{3,2,1,0:T(8,128)S(1)}, u32[]{:S(2)}, u32[]{:S(2)}) collective-permute-start(f32[3,2,40,128]{3,2,1,0:T(8,128)S(1)} %get-tuple-element.40), channel_id=1, source_target_pairs={{0,2},{2,0},{4,6},{6,4},{8,10},{10,8},{12,14},{14,12},{16,18},{18,... | collective-permute-start | bytes 368648 | tf_op jit(solution)/shard_map/ppermute | solution.py:52
  61.6 7.1 %collective-permute-start.12 = (f32[3,2,40,128]{3,2,1,0:T(8,128)S(1)}, f32[3,2,40,128]{3,2,1,0:T(8,128)S(1)}, u32[]{:S(2)}, u32[]{:S(2)}) collective-permute-start(f32[3,2,40,128]{3,2,1,0:T(8,128)S(1)} %get-tuple-element.41), channel_id=1, source_target_pairs={{0,30},{2,4},{4,2},{6,8},{8,6},{10,12},{12,10},{14,16},{16,14},{18... | collective-permute-start | bytes 368648 | tf_op jit(solution)/shard_map/ppermute | solution.py:51

commit v6 on v4

--- a/solution.py
+++ b/solution.py
@@ -310,8 +310,11 @@
     return jnp.where(ids < 4, low, high)
 
 
-def edged_plane(mine, other):
-    return jnp.concatenate([mine, edge_rows(other[:8], other[-8:])], axis=0)
+def edged_plane(mine, other, ends_only=False):
+    edges = edge_rows(other[:8], other[-8:])
+    if ends_only:
+        return jnp.concatenate([mine[-8:], edges, mine[:8]], axis=0)
+    return jnp.concatenate([mine, edges], axis=0)
 
 
 def roll_rows(value, shift):
@@ -323,11 +326,19 @@
 
 
 def relax(fields, sources):
-    ids = lax.broadcasted_iota(jnp.int32, (ROWS, NZ), 0)
-    frozen = (ids > CY) & (ids < ROWS - 1)
-    for sweep in range(SWEEPS):
+    rows = sources[0].shape[0]
+    first_edge = CY if rows == ROWS else 8
+    ids = lax.broadcasted_iota(jnp.int32, (rows, NZ), 0)
+    frozen = (ids > first_edge) & (ids < first_edge + 7)
+    sweeps = SWEEPS
+    if fields is None:
+        none = jnp.zeros((rows, NZ), F32)
+        inner = [jnp.where(frozen, 0.0, source * (1.0 / 6.0)) for source in sources]
+        fields = [none] + inner + [none]
+        sweeps = SWEEPS - 1
+    for sweep in range(sweeps):
         fresh = list(fields)
-        last = sweep == SWEEPS - 1
+        last = sweep == sweeps - 1
         for x in range(2 if last else 1, CX + (2 if last else 3)):
             centre = fields[x]
             summed = fields[x - 1] + fields[x + 1] + roll_rows(centre, 1) + roll_rows(centre, -1)
@@ -337,9 +348,10 @@
     return fields[2 : CX + 2]
 
 
-def pack_rows(a, b, rows):
+def pack_rows(value, rows):
     ids = lax.broadcasted_iota(jnp.int32, (8, NZ), 0)
-    first, last = b[:8], b[CY - 8 :]
+    a, b = value[:CY], value[CY:]
+    first, last = b[:8], b[-8:]
     if rows == CY + 8:
         return jnp.concatenate([a, jnp.where(ids < 4, first, last)], axis=0)
     if rows == CY + 16:
@@ -349,10 +361,10 @@
 
 
 def unpack_rows(packed):
-    a, rest = packed[:CY], packed[CY:]
-    first, last = rest[:8], rest[rest.shape[0] - 8 :]
-    middle = rest[8:16] if rest.shape[0] == 24 else last
-    return a, jnp.concatenate([first, middle, middle, last], axis=0)
+    a, b = packed[:CY], packed[CY:]
+    if b.shape[0] == 24:
+        b = jnp.concatenate([b[:16], b[8:]], axis=0)
+    return a, b
 
 
 def hand_out(potential, to_within, to_across):
@@ -360,10 +372,7 @@
     rows = to_within.shape[2]
     for comp in range(3):
         for x in range(2):
-            low, high = (
-                pack_rows(potential[comp, at, :CY], potential[comp, at, CY:], rows)
-                for at in (x, CX - 2 + x)
-            )
+            low, high = (pack_rows(potential[comp, at], rows) for at in (x, CX - 2 + x))
             to_within[comp, x] = jnp.where(even, high, low)
             to_across[comp, x] = jnp.where(even, low, high)
 
@@ -392,7 +401,7 @@
         high = main[CY - 8 : CY] + jnp.where(ids == 7, edges, 0.0)
         return jnp.concatenate([low, main[8 : CY - 8], high], axis=0)
 
-    def one_component(comp, carry):
+    for comp in range(3):
         sources = ([], [])
         for x in range(CX + 2):
             a = mine[comp, x]
@@ -406,13 +415,9 @@
             sources[0].append(edged_plane(omega_a, omega_b))
             sources[1].append(edged_plane(omega_b, omega_a))
         for block in range(2):
-            fields = [jnp.zeros((ROWS, NZ), F32)] * (CX + 4)
-            fields = relax(fields, sources[block])
+            fields = relax(None, sources[block])
             for x in range(CX):
                 potential[comp, x, block * CY : (block + 1) * CY] = fields[x][:CY]
-        return carry
-
-    lax.fori_loop(0, 3, one_component, 0)
     hand_out(potential, to_within, to_across)
 
 
@@ -424,23 +429,27 @@
 
     below = [chosen(jnp.logical_not(even), x) for x in range(2)]
     above = [chosen(even, x) for x in range(2)]
-    middle = [(potential[comp, x, :CY], potential[comp, x, CY:]) for x in range(CX)]
+    middle = [unpack_rows(potential[comp, x]) for x in range(CX)]
     return below + middle + above
 
 
 def next_kernel(omega, before, got_within, got_across, potential, to_within, to_across):
-    def one_component(comp, carry):
+    ends_only = before.shape[2] == CY + 16
+    for comp in range(3):
         pairs = gathered(before, got_within, got_across, comp)
         charge = [(omega[comp, x, :CY], omega[comp, x, CY:]) for x in range(CX + 2)]
-        for block in range(2):
-            fields = [edged_plane(pair[block], pair[1 - block]) for pair in pairs]
-            sources = [edged_plane(pair[block], pair[1 - block]) for pair in charge]
-            fields = relax(fields, sources)
-            for x in range(CX):
-                potential[comp, x, block * CY : (block + 1) * CY] = fields[x][:CY]
-        return carry
-
-    lax.fori_loop(0, 3, one_component, 0)
+        fields = relax([edged_plane(a, b) for a, b in pairs], [edged_plane(a, b) for a, b in charge])
+        for x in range(CX):
+            potential[comp, x, :CY] = fields[x][:CY]
+        fields = relax(
+            [edged_plane(b, a, ends_only) for a, b in pairs],
+            [edged_plane(b, a, ends_only) for a, b in charge],
+        )
+        first = 16 if ends_only else 0
+        last = 0 if ends_only else CY - 8
+        for x in range(CX):
+            potential[comp, x, CY : CY + 8] = fields[x][first : first + 8]
+            potential[comp, x, CY + 8 :] = fields[x][last : last + 8]
     hand_out(potential, to_within, to_across)
 
 
@@ -498,16 +507,16 @@
         *swap_x(to_within, to_across),
     )
     other = lax.ppermute(message, "gy", [(0, 1), (1, 0)])
-    slab = array(3, CX, 2 * CY, NZ)
+    whole, ends = array(3, CX, 2 * CY, NZ), array(3, CX, CY + 16, NZ)
     depths = [CY + 24, CY + 16, CY + 16, CY + 8]
     edge = array(3, 2, depths[0], NZ)
     omega, potential, to_within, to_across = on_vmem(
-        first_kernel, (array(3, planes, 2 * CY, NZ), slab, edge, edge), mine, other
+        first_kernel, (array(3, planes, 2 * CY, NZ), whole, edge, edge), mine, other
     )
     for depth in depths[1:]:
         edge = array(3, 2, depth, NZ)
         potential, to_within, to_across = on_vmem(
-            next_kernel, (slab, edge, edge), omega, potential, *swap_x(to_within, to_across)
+            next_kernel, (ends, edge, edge), omega, potential, *swap_x(to_within, to_across)
         )
     block = array(3, CX, CY, NZ)
     return on_vmem(

time: 70.3 us -> 69 us (0.982)
  Pallas kernels: 19 us -> 17.7 us
    pallas_call x6, Pallas kernels: 6.95 us -> 5.68 us  [on_vmem(): pl.pallas_call(kernel, in_specs=in_vmem(len(args)), out_specs=tuple(in_vm...]
where the time goes in v6:
time: 69 us; the launch traced here: 68.8 us
  waiting for transfers between devices  33.8 us (49%)
  Pallas kernels  17.7 us (26%)
  starting transfers between devices  16.6 us (24%)
  between operations  0.78 us (1%)
    ppermute x6, waiting for transfers between devices, swap_x(): got_across = lax.ppermute(to_across, 'gx', across(n))  27.8 us
    ppermute x6, starting transfers between devices, swap_x(): got_across = lax.ppermute(to_across, 'gx', across(n))  14.1 us
    pallas_call x1, Pallas kernels, deposit_staying(): pl.pallas_call(functools.partial(staying_kernel, tiles_per_chunk=per_chun...  8.54 us
    pallas_call x6, Pallas kernels, on_vmem(): pl.pallas_call(kernel, in_specs=in_vmem(len(args)), out_specs=tuple(in_vm...  5.68 us
    ppermute x1, waiting for transfers between devices, two_block_solve(): other = lax.ppermute(message, 'gy', [(0, 1), (1, 0)])  5.2 us
    pallas_call x1, Pallas kernels, pack_leaving(): pl.pallas_call(functools.partial(leaving_kernel, capacity=capacity), in_s...  2.33 us
    ppermute x1, starting transfers between devices, two_block_solve(): other = lax.ppermute(message, 'gy', [(0, 1), (1, 0)])  1.58 us
  transfers between devices with their start and end apart: 13, of which 7 were waited for; matrix products, arithmetic and copies ran while one was open for 0% of the time, Pallas kernels for 12%

profile of v6, /device:TPU:0, one launch (start us, length us, event | category | flops | bytes accessed | tf_op | source)
XLA Modules:
  0.0 68.8 jit_solution(11695700501316700007)
XLA Ops:
  0.6 0.0 copy-start
  0.6 0.0 copy-start.1
  0.6 0.0 copy-start.2
  0.7 2.3 %shard_map.60 = (f32[8,1024]{1,0:T(8,128)}, f32[8,1024]{1,0:T(8,128)}) custom-call(s32[1,3]{1,0:T(1,128)} %moving.3, s32[136,128]{1,0:T(8,128)} %bitcast.1, f32[3,17408]{1,0:T(4,128)} %offset_hbm.1, f32[3,17408]{1,0:T(4,128)} %vort_hbm.1), custom_call_target="tpu_custom_call" | custom-call | tf_op jit(solution)/shard_map/pallas_call | solution.py:170
  3.0 0.0 copy-start.3
  3.0 0.5 collective-permute-start
  3.5 5.6 %collective-permute-start.1 = (f32[8,1024]{1,0:T(8,128)}, f32[8,1024]{1,0:T(8,128)S(1)}, u32[]{:S(2)}, u32[]{:S(2)}) collective-permute-start(f32[8,1024]{1,0:T(8,128)} %get-tuple-element.23), channel_id=1, source_target_pairs={{0,30},{2,4},{4,2},{6,8},{8,6},{10,12},{12,10},{14,16},{16,14},{18... | collective-permute-start | bytes 98312 | tf_op jit(solution)/shard_map/ppermute | solution.py:51
  9.2 0.0 copy-done
  9.2 0.0 copy-done.1
  9.2 0.0 copy-done.2
  9.2 0.0 copy-done.3
  9.2 8.5 %shard_map.59.total = f32[288,384]{1,0:T(8,128)S(1)} custom-call(s32[1,3]{1,0:T(1,128)S(1)} %copy-done.3, s32[136,128]{1,0:T(8,128)S(1)} %bitcast.2, f32[3,17408]{1,0:T(4,128)S(1)} %copy-done, f32[3,17408]{1,0:T(4,128)S(1)} %copy-done.1), custom_call_target="tpu_custom_call" | custom-call | flops 3850371072 | bytes 487424 | tf_op jit(solution)/shard_map/pallas_call | solution.py:241
  17.7 0.0 collective-permute-done.got_within
  17.7 0.0 collective-permute-done.1.got_across
  17.7 1.2 %shard_map.61 = (f32[3,7,40,128]{3,2,1,0:T(8,128)S(1)}, f32[3,3,40,128]{3,2,1,0:T(8,128)S(1)}, f32[3,3,40,128]{3,2,1,0:T(8,128)S(1)}) custom-call(f32[288,384]{1,0:T(8,128)S(1)} %shard_map.59.total, f32[8,1024]{1,0:T(8,128)S(1)} %collective-permute-done.got_within, f32[8,1024]{1,0:T(8,128)S(1)} %collective-permute-done.1.got_across), custom_call_target="tpu_custom_call" | custom-call | tf_op jit(solution)/shard_map/pallas_call | solution.py:293
  18.9 0.1 collective-permute-start.2
  19.0 0.6 collective-permute-start.3
  19.6 0.8 %collective-permute-done.2.got_within = f32[3,3,40,128]{3,2,1,0:T(8,128)S(1)} collective-permute-done((f32[3,3,40,128]{3,2,1,0:T(8,128)S(1)}, f32[3,3,40,128]{3,2,1,0:T(8,128)S(1)}, u32[]{:S(2)}, u32[]{:S(2)}) %collective-permute-start.2) | collective-permute-done | bytes 184352 | tf_op jit(solution)/shard_map/ppermute | solution.py:52
  20.4 6.3 %collective-permute-done.3.got_across = f32[3,3,40,128]{3,2,1,0:T(8,128)S(1)} collective-permute-done((f32[3,3,40,128]{3,2,1,0:T(8,128)S(1)}, f32[3,3,40,128]{3,2,1,0:T(8,128)S(1)}, u32[]{:S(2)}, u32[]{:S(2)}) %collective-permute-start.3) | collective-permute-done | bytes 184352 | tf_op jit(solution)/shard_map/ppermute | solution.py:51
  26.7 0.1 shard_map.62
  26.8 1.6 %collective-permute-start.4 = (f32[3,6,32,128]{3,2,1,0:T(8,128)S(1)}, f32[3,6,32,128]{3,2,1,0:T(8,128)S(1)}, u32[]{:S(2)}, u32[]{:S(2)}) collective-permute-start(f32[3,6,32,128]{3,2,1,0:T(8,128)S(1)} %get-tuple-element.28), channel_id=1, source_target_pairs={{0,1},{1,0},{2,3},{3,2},{4,5},{5,4},{6,7},{7,6},{8,9},{9,8},{10,11... | collective-permute-start | bytes 884744 | tf_op jit(solution)/shard_map/ppermute | solution.py:509
  28.4 5.2 %collective-permute-done.4.other = f32[3,6,32,128]{3,2,1,0:T(8,128)S(1)} collective-permute-done((f32[3,6,32,128]{3,2,1,0:T(8,128)S(1)}, f32[3,6,32,128]{3,2,1,0:T(8,128)S(1)}, u32[]{:S(2)}, u32[]{:S(2)}) %collective-permute-start.4) | collective-permute-done | bytes 294944 | tf_op jit(solution)/shard_map/ppermute | solution.py:509
  33.6 0.9 %shard_map.63 = (f32[3,6,64,128]{3,2,1,0:T(8,128)S(1)}, f32[3,4,64,128]{3,2,1,0:T(8,128)S(1)}, f32[3,2,56,128]{3,2,1,0:T(8,128)S(1)}, f32[3,2,56,128]{3,2,1,0:T(8,128)S(1)}) custom-call(f32[3,6,40,128]{3,2,1,0:T(8,128)S(1)} %get-tuple-element.27.mine, f32[3,6,32,128]{3,2,1,0:T(8,128)S(1)} %collective-permute-done.4.other), custom_call_target="tpu_custom_call" | custom-call | tf_op jit(solution)/shard_map/pallas_call | solution.py:492
  34.4 0.1 collective-permute-start.5
  34.5 2.0 %collective-permute-start.6 = (f32[3,2,56,128]{3,2,1,0:T(8,128)S(1)}, f32[3,2,56,128]{3,2,1,0:T(8,128)S(1)}, u32[]{:S(2)}, u32[]{:S(2)}) collective-permute-start(f32[3,2,56,128]{3,2,1,0:T(8,128)S(1)} %get-tuple-element.32), channel_id=1, source_target_pairs={{0,30},{2,4},{4,2},{6,8},{8,6},{10,12},{12,10},{14,16},{16,14},{18... | collective-permute-start | bytes 516104 | tf_op jit(solution)/shard_map/ppermute | solution.py:51
  36.5 0.0 collective-permute-done.5.got_within
  36.5 5.6 %collective-permute-done.6.got_across = f32[3,2,56,128]{3,2,1,0:T(8,128)S(1)} collective-permute-done((f32[3,2,56,128]{3,2,1,0:T(8,128)S(1)}, f32[3,2,56,128]{3,2,1,0:T(8,128)S(1)}, u32[]{:S(2)}, u32[]{:S(2)}) %collective-permute-start.6) | collective-permute-done | bytes 172064 | tf_op jit(solution)/shard_map/ppermute | solution.py:51
  42.1 1.3 %shard_map.64 = (f32[3,4,48,128]{3,2,1,0:T(8,128)S(1)}, f32[3,2,48,128]{3,2,1,0:T(8,128)S(1)}, f32[3,2,48,128]{3,2,1,0:T(8,128)S(1)}) custom-call(f32[3,6,64,128]{3,2,1,0:T(8,128)S(1)} %get-tuple-element.29.omega, f32[3,4,64,128]{3,2,1,0:T(8,128)S(1)} %get-tuple-element.30.before, f32[3,2,56,128]{3,2,1,0:T(8,128)S(1)} %collective-permute-done.5.got_within, ...), custom_call_target="tpu_custom_call" | custom-call | tf_op jit(solution)/shard_map/pallas_call | solution.py:492
  43.4 0.1 collective-permute-start.7
  43.5 2.0 %collective-permute-start.8 = (f32[3,2,48,128]{3,2,1,0:T(8,128)S(1)}, f32[3,2,48,128]{3,2,1,0:T(8,128)S(1)}, u32[]{:S(2)}, u32[]{:S(2)}) collective-permute-start(f32[3,2,48,128]{3,2,1,0:T(8,128)S(1)} %get-tuple-element.35), channel_id=1, source_target_pairs={{0,30},{2,4},{4,2},{6,8},{8,6},{10,12},{12,10},{14,16},{16,14},{18... | collective-permute-start | bytes 442376 | tf_op jit(solution)/shard_map/ppermute | solution.py:51
  45.5 0.0 collective-permute-done.7.got_within
  45.5 5.4 %collective-permute-done.8.got_across = f32[3,2,48,128]{3,2,1,0:T(8,128)S(1)} collective-permute-done((f32[3,2,48,128]{3,2,1,0:T(8,128)S(1)}, f32[3,2,48,128]{3,2,1,0:T(8,128)S(1)}, u32[]{:S(2)}, u32[]{:S(2)}) %collective-permute-start.8) | collective-permute-done | bytes 147488 | tf_op jit(solution)/shard_map/ppermute | solution.py:51
  50.8 1.2 %shard_map.65 = (f32[3,4,48,128]{3,2,1,0:T(8,128)S(1)}, f32[3,2,48,128]{3,2,1,0:T(8,128)S(1)}, f32[3,2,48,128]{3,2,1,0:T(8,128)S(1)}) custom-call(f32[3,6,64,128]{3,2,1,0:T(8,128)S(1)} %get-tuple-element.29.omega, f32[3,4,48,128]{3,2,1,0:T(8,128)S(1)} %get-tuple-element.33.before, f32[3,2,48,128]{3,2,1,0:T(8,128)S(1)} %collective-permute-done.7.got_within, ...), custom_call_target="tpu_custom_call" | custom-call | tf_op jit(solution)/shard_map/pallas_call | solution.py:492
  52.1 0.1 collective-permute-start.9
  52.1 2.0 %collective-permute-start.10 = (f32[3,2,48,128]{3,2,1,0:T(8,128)S(1)}, f32[3,2,48,128]{3,2,1,0:T(8,128)S(1)}, u32[]{:S(2)}, u32[]{:S(2)}) collective-permute-start(f32[3,2,48,128]{3,2,1,0:T(8,128)S(1)} %get-tuple-element.38), channel_id=1, source_target_pairs={{0,30},{2,4},{4,2},{6,8},{8,6},{10,12},{12,10},{14,16},{16,14},{18... | collective-permute-start | bytes 442376 | tf_op jit(solution)/shard_map/ppermute | solution.py:51
  54.1 0.0 collective-permute-done.9.got_within
  54.1 5.4 %collective-permute-done.10.got_across = f32[3,2,48,128]{3,2,1,0:T(8,128)S(1)} collective-permute-done((f32[3,2,48,128]{3,2,1,0:T(8,128)S(1)}, f32[3,2,48,128]{3,2,1,0:T(8,128)S(1)}, u32[]{:S(2)}, u32[]{:S(2)}) %collective-permute-start.10) | collective-permute-done | bytes 147488 | tf_op jit(solution)/shard_map/ppermute | solution.py:51
  59.5 1.2 %shard_map.66 = (f32[3,4,48,128]{3,2,1,0:T(8,128)S(1)}, f32[3,2,40,128]{3,2,1,0:T(8,128)S(1)}, f32[3,2,40,128]{3,2,1,0:T(8,128)S(1)}) custom-call(f32[3,6,64,128]{3,2,1,0:T(8,128)S(1)} %get-tuple-element.29.omega, f32[3,4,48,128]{3,2,1,0:T(8,128)S(1)} %get-tuple-element.36.before, f32[3,2,48,128]{3,2,1,0:T(8,128)S(1)} %collective-permute-done.9.got_within, ...), custom_call_target="tpu_custom_call" | custom-call | tf_op jit(solution)/shard_map/pallas_call | solution.py:492
  60.7 0.1 collective-permute-start.11
  60.8 2.0 %collective-permute-start.12 = (f32[3,2,40,128]{3,2,1,0:T(8,128)S(1)}, f32[3,2,40,128]{3,2,1,0:T(8,128)S(1)}, u32[]{:S(2)}, u32[]{:S(2)}) collective-permute-start(f32[3,2,40,128]{3,2,1,0:T(8,128)S(1)} %get-tuple-element.41), channel_id=1, source_target_pairs={{0,30},{2,4},{4,2},{6,8},{8,6},{10,12},{12,10},{14,16},{16,14},{18... | collective-permute-start | bytes 368648 | tf_op jit(solution)/shard_map/ppermute | solution.py:51
  62.7 0.0 collective-permute-done.11.got_within
  62.7 5.1 %collective-permute-done.12.got_across = f32[3,2,40,128]{3,2,1,0:T(8,128)S(1)} collective-permute-done((f32[3,2,40,128]{3,2,1,0:T(8,128)S(1)}, f32[3,2,40,128]{3,2,1,0:T(8,128)S(1)}, u32[]{:S(2)}, u32[]{:S(2)}) %collective-permute-start.12) | collective-permute-done | bytes 122912 | tf_op jit(solution)/shard_map/ppermute | solution.py:51
  67.8 1.0 %shard_map.67 = (f32[3,4,32,128]{3,2,1,0:T(8,128)}, f32[3,4,32,128]{3,2,1,0:T(8,128)}) custom-call(f32[3,6,64,128]{3,2,1,0:T(8,128)S(1)} %get-tuple-element.29.omega, f32[3,4,48,128]{3,2,1,0:T(8,128)S(1)} %get-tuple-element.39.potential, f32[3,2,40,128]{3,2,1,0:T(8,128)S(1)} %collective-permute-done.11.got_within, ...), custom_call_target="tpu_custom_call" | custom-call | tf_op jit(solution)/shard_map/pallas_call | solution.py:492
Async XLA Ops:
  0.6 8.5 %copy-start = (f32[3,17408]{1,0:T(4,128)S(1)}, f32[3,17408]{1,0:T(4,128)}, u32[]{:S(2)}) copy-start(f32[3,17408]{1,0:T(4,128)} %offset_hbm.1) | copy-start | bytes 626692
  0.6 8.5 %copy-start.1 = (f32[3,17408]{1,0:T(4,128)S(1)}, f32[3,17408]{1,0:T(4,128)}, u32[]{:S(2)}) copy-start(f32[3,17408]{1,0:T(4,128)} %vort_hbm.1) | copy-start | bytes 626692
  0.6 8.5 %copy-start.2 = (s32[17408]{0:T(1024)S(1)}, s32[17408]{0:T(1024)}, u32[]{:S(2)}) copy-start(s32[17408]{0:T(1024)} %param.4) | copy-start | bytes 208900
  3.0 6.2 %copy-start.3 = (s32[1,3]{1,0:T(1,128)S(1)}, s32[1,3]{1,0:T(1,128)}, u32[]{:S(2)}) copy-start(s32[1,3]{1,0:T(1,128)} %moving.3) | copy-start | bytes 40
  3.0 14.7 %collective-permute-start = (f32[8,1024]{1,0:T(8,128)}, f32[8,1024]{1,0:T(8,128)S(1)}, u32[]{:S(2)}, u32[]{:S(2)}) collective-permute-start(f32[8,1024]{1,0:T(8,128)} %get-tuple-element.22), channel_id=1, source_target_pairs={{0,2},{2,0},{4,6},{6,4},{8,10},{10,8},{12,14},{14,12},{16,18},{18,... | collective-permute-start | bytes 98312 | tf_op jit(solution)/shard_map/ppermute | solution.py:52
  3.5 14.2 %collective-permute-start.1 = (f32[8,1024]{1,0:T(8,128)}, f32[8,1024]{1,0:T(8,128)S(1)}, u32[]{:S(2)}, u32[]{:S(2)}) collective-permute-start(f32[8,1024]{1,0:T(8,128)} %get-tuple-element.23), channel_id=1, source_target_pairs={{0,30},{2,4},{4,2},{6,8},{8,6},{10,12},{12,10},{14,16},{16,14},{18... | collective-permute-start | bytes 98312 | tf_op jit(solution)/shard_map/ppermute | solution.py:51
  18.9 1.5 %collective-permute-start.2 = (f32[3,3,40,128]{3,2,1,0:T(8,128)S(1)}, f32[3,3,40,128]{3,2,1,0:T(8,128)S(1)}, u32[]{:S(2)}, u32[]{:S(2)}) collective-permute-start(f32[3,3,40,128]{3,2,1,0:T(8,128)S(1)} %get-tuple-element.25), channel_id=1, source_target_pairs={{0,2},{2,0},{4,6},{6,4},{8,10},{10,8},{12,14},{14,12},{16,18},{18,... | collective-permute-start | bytes 552968 | tf_op jit(solution)/shard_map/ppermute | solution.py:52
  19.0 7.7 %collective-permute-start.3 = (f32[3,3,40,128]{3,2,1,0:T(8,128)S(1)}, f32[3,3,40,128]{3,2,1,0:T(8,128)S(1)}, u32[]{:S(2)}, u32[]{:S(2)}) collective-permute-start(f32[3,3,40,128]{3,2,1,0:T(8,128)S(1)} %get-tuple-element.26), channel_id=1, source_target_pairs={{0,30},{2,4},{4,2},{6,8},{8,6},{10,12},{12,10},{14,16},{16,14},{18... | collective-permute-start | bytes 552968 | tf_op jit(solution)/shard_map/ppermute | solution.py:51
  26.8 6.8 %collective-permute-start.4 = (f32[3,6,32,128]{3,2,1,0:T(8,128)S(1)}, f32[3,6,32,128]{3,2,1,0:T(8,128)S(1)}, u32[]{:S(2)}, u32[]{:S(2)}) collective-permute-start(f32[3,6,32,128]{3,2,1,0:T(8,128)S(1)} %get-tuple-element.28), channel_id=1, source_target_pairs={{0,1},{1,0},{2,3},{3,2},{4,5},{5,4},{6,7},{7,6},{8,9},{9,8},{10,11... | collective-permute-start | bytes 884744 | tf_op jit(solution)/shard_map/ppermute | solution.py:509
  34.4 2.0 %collective-permute-start.5 = (f32[3,2,56,128]{3,2,1,0:T(8,128)S(1)}, f32[3,2,56,128]{3,2,1,0:T(8,128)S(1)}, u32[]{:S(2)}, u32[]{:S(2)}) collective-permute-start(f32[3,2,56,128]{3,2,1,0:T(8,128)S(1)} %get-tuple-element.31), channel_id=1, source_target_pairs={{0,2},{2,0},{4,6},{6,4},{8,10},{10,8},{12,14},{14,12},{16,18},{18,... | collective-permute-start | bytes 516104 | tf_op jit(solution)/shard_map/ppermute | solution.py:52
  34.5 7.6 %collective-permute-start.6 = (f32[3,2,56,128]{3,2,1,0:T(8,128)S(1)}, f32[3,2,56,128]{3,2,1,0:T(8,128)S(1)}, u32[]{:S(2)}, u32[]{:S(2)}) collective-permute-start(f32[3,2,56,128]{3,2,1,0:T(8,128)S(1)} %get-tuple-element.32), channel_id=1, source_target_pairs={{0,30},{2,4},{4,2},{6,8},{8,6},{10,12},{12,10},{14,16},{16,14},{18... | collective-permute-start | bytes 516104 | tf_op jit(solution)/shard_map/ppermute | solution.py:51
  43.4 2.0 %collective-permute-start.7 = (f32[3,2,48,128]{3,2,1,0:T(8,128)S(1)}, f32[3,2,48,128]{3,2,1,0:T(8,128)S(1)}, u32[]{:S(2)}, u32[]{:S(2)}) collective-permute-start(f32[3,2,48,128]{3,2,1,0:T(8,128)S(1)} %get-tuple-element.34), channel_id=1, source_target_pairs={{0,2},{2,0},{4,6},{6,4},{8,10},{10,8},{12,14},{14,12},{16,18},{18,... | collective-permute-start | bytes 442376 | tf_op jit(solution)/shard_map/ppermute | solution.py:52
  43.5 7.3 %collective-permute-start.8 = (f32[3,2,48,128]{3,2,1,0:T(8,128)S(1)}, f32[3,2,48,128]{3,2,1,0:T(8,128)S(1)}, u32[]{:S(2)}, u32[]{:S(2)}) collective-permute-start(f32[3,2,48,128]{3,2,1,0:T(8,128)S(1)} %get-tuple-element.35), channel_id=1, source_target_pairs={{0,30},{2,4},{4,2},{6,8},{8,6},{10,12},{12,10},{14,16},{16,14},{18... | collective-permute-start | bytes 442376 | tf_op jit(solution)/shard_map/ppermute | solution.py:51
  52.1 2.0 %collective-permute-start.9 = (f32[3,2,48,128]{3,2,1,0:T(8,128)S(1)}, f32[3,2,48,128]{3,2,1,0:T(8,128)S(1)}, u32[]{:S(2)}, u32[]{:S(2)}) collective-permute-start(f32[3,2,48,128]{3,2,1,0:T(8,128)S(1)} %get-tuple-element.37), channel_id=1, source_target_pairs={{0,2},{2,0},{4,6},{6,4},{8,10},{10,8},{12,14},{14,12},{16,18},{18,... | collective-permute-start | bytes 442376 | tf_op jit(solution)/shard_map/ppermute | solution.py:52
  52.1 7.3 %collective-permute-start.10 = (f32[3,2,48,128]{3,2,1,0:T(8,128)S(1)}, f32[3,2,48,128]{3,2,1,0:T(8,128)S(1)}, u32[]{:S(2)}, u32[]{:S(2)}) collective-permute-start(f32[3,2,48,128]{3,2,1,0:T(8,128)S(1)} %get-tuple-element.38), channel_id=1, source_target_pairs={{0,30},{2,4},{4,2},{6,8},{8,6},{10,12},{12,10},{14,16},{16,14},{18... | collective-permute-start | bytes 442376 | tf_op jit(solution)/shard_map/ppermute | solution.py:51
  60.7 2.0 %collective-permute-start.11 = (f32[3,2,40,128]{3,2,1,0:T(8,128)S(1)}, f32[3,2,40,128]{3,2,1,0:T(8,128)S(1)}, u32[]{:S(2)}, u32[]{:S(2)}) collective-permute-start(f32[3,2,40,128]{3,2,1,0:T(8,128)S(1)} %get-tuple-element.40), channel_id=1, source_target_pairs={{0,2},{2,0},{4,6},{6,4},{8,10},{10,8},{12,14},{14,12},{16,18},{18,... | collective-permute-start | bytes 368648 | tf_op jit(solution)/shard_map/ppermute | solution.py:52
  60.8 7.1 %collective-permute-start.12 = (f32[3,2,40,128]{3,2,1,0:T(8,128)S(1)}, f32[3,2,40,128]{3,2,1,0:T(8,128)S(1)}, u32[]{:S(2)}, u32[]{:S(2)}) collective-permute-start(f32[3,2,40,128]{3,2,1,0:T(8,128)S(1)} %get-tuple-element.41), channel_id=1, source_target_pairs={{0,30},{2,4},{4,2},{6,8},{8,6},{10,12},{12,10},{14,16},{16,14},{18... | collective-permute-start | bytes 368648 | tf_op jit(solution)/shard_map/ppermute | solution.py:51

commit v7 on v6

--- a/solution.py
+++ b/solution.py
@@ -50,7 +50,7 @@
     n = lax.axis_size("gx")
     got_across = lax.ppermute(to_across, "gx", across(n))
     got_within = lax.ppermute(to_within, "gx", within(n))
-    return got_within, got_across
+    return got_across, got_within
 
 
 def m4_weights(offset):
@@ -255,9 +255,9 @@
     )(moving, cells, part_offset, part_vort)
 
 
-def arrived_kernel(total, got_within, got_across, deposits, to_within, to_across, dense, table, planes, lines):
+def arrived_kernel(total, got_across, got_within, deposits, to_within, to_across, dense, table, planes, lines):
     tiles = got_within.shape[1] // 128
-    for which, got in enumerate((got_within, got_across)):
+    for which, got in enumerate((got_across, got_within)):
         for tile in range(tiles):
             lanes = slice(tile * 128, (tile + 1) * 128)
             place = which * tiles + tile
@@ -286,7 +286,7 @@
     to_across[...] = deposits[:, pl.ds(first_across, 3)]
 
 
-def deposit_arrived(total, got_within, got_across):
+def deposit_arrived(total, got_across, got_within):
     received = got_within.shape[1]
     edge = jax.ShapeDtypeStruct((3, 3, ROWS, NZ), F32)
     tiles = 2 * received // 128
@@ -302,7 +302,7 @@
             pltpu.VMEM((3 * NZ, 2 * received), BF16),
         ],
         compiler_params=params(),
-    )(total, got_within, got_across)
+    )(total, got_across, got_within)
 
 
 def edge_rows(low, high):
@@ -377,7 +377,7 @@
             to_across[comp, x] = jnp.where(even, low, high)
 
 
-def fold_kernel(deposits, got_within, got_across, mine, message):
+def fold_kernel(deposits, got_across, got_within, mine, message):
     even = is_even()
     ids = lax.broadcasted_iota(jnp.int32, (8, NZ), 0)
     for comp in range(3):
@@ -421,7 +421,7 @@
     hand_out(potential, to_within, to_across)
 
 
-def gathered(potential, got_within, got_across, comp):
+def gathered(potential, got_across, got_within, comp):
     even = is_even()
 
     def chosen(pick, x):
@@ -433,10 +433,10 @@
     return below + middle + above
 
 
-def next_kernel(omega, before, got_within, got_across, potential, to_within, to_across):
+def next_kernel(omega, before, got_across, got_within, potential, to_within, to_across):
     ends_only = before.shape[2] == CY + 16
     for comp in range(3):
-        pairs = gathered(before, got_within, got_across, comp)
+        pairs = gathered(before, got_across, got_within, comp)
         charge = [(omega[comp, x, :CY], omega[comp, x, CY:]) for x in range(CX + 2)]
         fields = relax([edged_plane(a, b) for a, b in pairs], [edged_plane(a, b) for a, b in charge])
         for x in range(CX):
@@ -453,10 +453,10 @@
     hand_out(potential, to_within, to_across)
 
 
-def last_kernel(omega, potential, got_within, got_across, velocity, stretching):
+def last_kernel(omega, potential, got_across, got_within, velocity, stretching):
     psi = []
     for comp in range(3):
-        pairs = gathered(potential, got_within, got_across, comp)
+        pairs = gathered(potential, got_across, got_within, comp)
         psi.append([edged_plane(a, b) for a, b in pairs])
 
     def slope_x(planes, x):
@@ -609,9 +609,9 @@
 
 def per_device(part_cell, part_offset, part_vort, moving):
     particles = (moving, part_cell.reshape(-1, 128), part_offset, part_vort)
-    got_within, got_across = swap_x(*pack_leaving(*particles))
+    got_across, got_within = swap_x(*pack_leaving(*particles))
     total = deposit_staying(*particles)
-    deposits, to_within, to_across = deposit_arrived(total, got_within, got_across)
+    deposits, to_within, to_across = deposit_arrived(total, got_across, got_within)
     if lax.axis_size("gy") == 2:
         return two_block_solve(deposits, to_within, to_across)
     return general_solve(deposits)

time: 69 us -> 68 us (0.986)
  waiting for transfers between devices: 33.8 us -> 32.2 us
    ppermute x6, starting transfers between devices: 14.1 us -> 15.5 us  [swap_x(): got_across = lax.ppermute(to_across, 'gx', across(n))]
    ppermute x6, starting transfers between devices: 0.87 us -> 0.02 us  [swap_x(): got_within = lax.ppermute(to_within, 'gx', within(n))]
    ppermute x6, waiting for transfers between devices: 27.8 us -> 27 us  [swap_x(): got_across = lax.ppermute(to_across, 'gx', across(n))]
    ppermute x6, waiting for transfers between devices: 0.79 us -> 0.02 us  [swap_x(): got_within = lax.ppermute(to_within, 'gx', within(n))]
  transfers between devices with their start and end apart: 13 -> 13, of which waited for: 7 -> 6; matrix products, arithmetic and copies ran while one was open for 0% -> 0% of each run, Pallas kernels for 12% -> 13%
where the time goes in v7:
time: 68 us; the launch traced here: 67.8 us
  waiting for transfers between devices  32.2 us (47%)
  Pallas kernels  17.7 us (26%)
  starting transfers between devices  17.1 us (25%)
  between operations  0.76 us (1%)
    ppermute x6, waiting for transfers between devices, swap_x(): got_across = lax.ppermute(to_across, 'gx', across(n))  27 us
    ppermute x6, starting transfers between devices, swap_x(): got_across = lax.ppermute(to_across, 'gx', across(n))  15.5 us
    pallas_call x1, Pallas kernels, deposit_staying(): pl.pallas_call(functools.partial(staying_kernel, tiles_per_chunk=per_chun...  8.54 us
    pallas_call x6, Pallas kernels, on_vmem(): pl.pallas_call(kernel, in_specs=in_vmem(len(args)), out_specs=tuple(in_vm...  5.68 us
    ppermute x1, waiting for transfers between devices, two_block_solve(): other = lax.ppermute(message, 'gy', [(0, 1), (1, 0)])  5.2 us
    pallas_call x1, Pallas kernels, pack_leaving(): pl.pallas_call(functools.partial(leaving_kernel, capacity=capacity), in_s...  2.33 us
    ppermute x1, starting transfers between devices, two_block_solve(): other = lax.ppermute(message, 'gy', [(0, 1), (1, 0)])  1.58 us
  transfers between devices with their start and end apart: 13, of which 6 were waited for; matrix products, arithmetic and copies ran while one was open for 0% of the time, Pallas kernels for 13%

profile of v7, /device:TPU:0, one launch (start us, length us, event | category | flops | bytes accessed | tf_op | source)
XLA Modules:
  0.0 67.8 jit_solution(6860595457698324916)
XLA Ops:
  0.6 0.0 copy-start
  0.6 0.0 copy-start.1
  0.6 0.0 copy-start.2
  0.7 2.3 %shard_map.60 = (f32[8,1024]{1,0:T(8,128)}, f32[8,1024]{1,0:T(8,128)}) custom-call(s32[1,3]{1,0:T(1,128)} %moving.3, s32[136,128]{1,0:T(8,128)} %bitcast.1, f32[3,17408]{1,0:T(4,128)} %offset_hbm.1, f32[3,17408]{1,0:T(4,128)} %vort_hbm.1), custom_call_target="tpu_custom_call" | custom-call | tf_op jit(solution)/shard_map/pallas_call | solution.py:170
  3.0 0.0 copy-start.3
  3.0 5.5 %collective-permute-start = (f32[8,1024]{1,0:T(8,128)}, f32[8,1024]{1,0:T(8,128)S(1)}, u32[]{:S(2)}, u32[]{:S(2)}) collective-permute-start(f32[8,1024]{1,0:T(8,128)} %get-tuple-element.22), channel_id=1, source_target_pairs={{0,30},{2,4},{4,2},{6,8},{8,6},{10,12},{12,10},{14,16},{16,14},{18... | collective-permute-start | bytes 98312 | tf_op jit(solution)/shard_map/ppermute | solution.py:51
  8.5 0.0 collective-permute-start.1
  8.5 0.0 copy-done
  8.5 0.0 copy-done.1
  8.5 0.0 copy-done.2
  8.5 0.0 copy-done.3
  8.5 8.5 %shard_map.59.total = f32[288,384]{1,0:T(8,128)S(1)} custom-call(s32[1,3]{1,0:T(1,128)S(1)} %copy-done.3, s32[136,128]{1,0:T(8,128)S(1)} %bitcast.2, f32[3,17408]{1,0:T(4,128)S(1)} %copy-done, f32[3,17408]{1,0:T(4,128)S(1)} %copy-done.1), custom_call_target="tpu_custom_call" | custom-call | flops 3850371072 | bytes 487424 | tf_op jit(solution)/shard_map/pallas_call | solution.py:241
  17.1 0.0 collective-permute-done.got_across
  17.1 0.0 collective-permute-done.1.got_within
  17.1 1.2 %shard_map.61 = (f32[3,7,40,128]{3,2,1,0:T(8,128)S(1)}, f32[3,3,40,128]{3,2,1,0:T(8,128)S(1)}, f32[3,3,40,128]{3,2,1,0:T(8,128)S(1)}) custom-call(f32[288,384]{1,0:T(8,128)S(1)} %shard_map.59.total, f32[8,1024]{1,0:T(8,128)S(1)} %collective-permute-done.got_across, f32[8,1024]{1,0:T(8,128)S(1)} %collective-permute-done.1.got_within), custom_call_target="tpu_custom_call" | custom-call | tf_op jit(solution)/shard_map/pallas_call | solution.py:293
  18.2 0.8 %collective-permute-start.2 = (f32[3,3,40,128]{3,2,1,0:T(8,128)S(1)}, f32[3,3,40,128]{3,2,1,0:T(8,128)S(1)}, u32[]{:S(2)}, u32[]{:S(2)}) collective-permute-start(f32[3,3,40,128]{3,2,1,0:T(8,128)S(1)} %get-tuple-element.25), channel_id=1, source_target_pairs={{0,30},{2,4},{4,2},{6,8},{8,6},{10,12},{12,10},{14,16},{16,14},{18... | collective-permute-start | bytes 552968 | tf_op jit(solution)/shard_map/ppermute | solution.py:51
  19.0 0.0 collective-permute-start.3
  19.0 6.9 %collective-permute-done.2.got_across = f32[3,3,40,128]{3,2,1,0:T(8,128)S(1)} collective-permute-done((f32[3,3,40,128]{3,2,1,0:T(8,128)S(1)}, f32[3,3,40,128]{3,2,1,0:T(8,128)S(1)}, u32[]{:S(2)}, u32[]{:S(2)}) %collective-permute-start.2) | collective-permute-done | bytes 184352 | tf_op jit(solution)/shard_map/ppermute | solution.py:51
  26.0 0.0 collective-permute-done.3.got_within
  26.0 0.1 shard_map.62
  26.0 1.6 %collective-permute-start.4 = (f32[3,6,32,128]{3,2,1,0:T(8,128)S(1)}, f32[3,6,32,128]{3,2,1,0:T(8,128)S(1)}, u32[]{:S(2)}, u32[]{:S(2)}) collective-permute-start(f32[3,6,32,128]{3,2,1,0:T(8,128)S(1)} %get-tuple-element.28), channel_id=1, source_target_pairs={{0,1},{1,0},{2,3},{3,2},{4,5},{5,4},{6,7},{7,6},{8,9},{9,8},{10,11... | collective-permute-start | bytes 884744 | tf_op jit(solution)/shard_map/ppermute | solution.py:509
  27.6 5.2 %collective-permute-done.4.other = f32[3,6,32,128]{3,2,1,0:T(8,128)S(1)} collective-permute-done((f32[3,6,32,128]{3,2,1,0:T(8,128)S(1)}, f32[3,6,32,128]{3,2,1,0:T(8,128)S(1)}, u32[]{:S(2)}, u32[]{:S(2)}) %collective-permute-start.4) | collective-permute-done | bytes 294944 | tf_op jit(solution)/shard_map/ppermute | solution.py:509
  32.8 0.9 %shard_map.63 = (f32[3,6,64,128]{3,2,1,0:T(8,128)S(1)}, f32[3,4,64,128]{3,2,1,0:T(8,128)S(1)}, f32[3,2,56,128]{3,2,1,0:T(8,128)S(1)}, f32[3,2,56,128]{3,2,1,0:T(8,128)S(1)}) custom-call(f32[3,6,40,128]{3,2,1,0:T(8,128)S(1)} %get-tuple-element.27.mine, f32[3,6,32,128]{3,2,1,0:T(8,128)S(1)} %collective-permute-done.4.other), custom_call_target="tpu_custom_call" | custom-call | tf_op jit(solution)/shard_map/pallas_call | solution.py:492
  33.7 2.3 %collective-permute-start.5 = (f32[3,2,56,128]{3,2,1,0:T(8,128)S(1)}, f32[3,2,56,128]{3,2,1,0:T(8,128)S(1)}, u32[]{:S(2)}, u32[]{:S(2)}) collective-permute-start(f32[3,2,56,128]{3,2,1,0:T(8,128)S(1)} %get-tuple-element.31), channel_id=1, source_target_pairs={{0,30},{2,4},{4,2},{6,8},{8,6},{10,12},{12,10},{14,16},{16,14},{18... | collective-permute-start | bytes 516104 | tf_op jit(solution)/shard_map/ppermute | solution.py:51
  36.0 0.0 collective-permute-start.6
  36.0 5.3 %collective-permute-done.5.got_across = f32[3,2,56,128]{3,2,1,0:T(8,128)S(1)} collective-permute-done((f32[3,2,56,128]{3,2,1,0:T(8,128)S(1)}, f32[3,2,56,128]{3,2,1,0:T(8,128)S(1)}, u32[]{:S(2)}, u32[]{:S(2)}) %collective-permute-start.5) | collective-permute-done | bytes 172064 | tf_op jit(solution)/shard_map/ppermute | solution.py:51
  41.3 0.0 collective-permute-done.6.got_within
  41.3 1.3 %shard_map.64 = (f32[3,4,48,128]{3,2,1,0:T(8,128)S(1)}, f32[3,2,48,128]{3,2,1,0:T(8,128)S(1)}, f32[3,2,48,128]{3,2,1,0:T(8,128)S(1)}) custom-call(f32[3,6,64,128]{3,2,1,0:T(8,128)S(1)} %get-tuple-element.29.omega, f32[3,4,64,128]{3,2,1,0:T(8,128)S(1)} %get-tuple-element.30.before, f32[3,2,56,128]{3,2,1,0:T(8,128)S(1)} %collective-permute-done.5.got_across, ...), custom_call_target="tpu_custom_call" | custom-call | tf_op jit(solution)/shard_map/pallas_call | solution.py:492
  42.6 2.3 %collective-permute-start.7 = (f32[3,2,48,128]{3,2,1,0:T(8,128)S(1)}, f32[3,2,48,128]{3,2,1,0:T(8,128)S(1)}, u32[]{:S(2)}, u32[]{:S(2)}) collective-permute-start(f32[3,2,48,128]{3,2,1,0:T(8,128)S(1)} %get-tuple-element.34), channel_id=1, source_target_pairs={{0,30},{2,4},{4,2},{6,8},{8,6},{10,12},{12,10},{14,16},{16,14},{18... | collective-permute-start | bytes 442376 | tf_op jit(solution)/shard_map/ppermute | solution.py:51
  44.9 0.0 collective-permute-start.8
  44.9 5.0 %collective-permute-done.7.got_across = f32[3,2,48,128]{3,2,1,0:T(8,128)S(1)} collective-permute-done((f32[3,2,48,128]{3,2,1,0:T(8,128)S(1)}, f32[3,2,48,128]{3,2,1,0:T(8,128)S(1)}, u32[]{:S(2)}, u32[]{:S(2)}) %collective-permute-start.7) | collective-permute-done | bytes 147488 | tf_op jit(solution)/shard_map/ppermute | solution.py:51
  49.9 0.0 collective-permute-done.8.got_within
  49.9 1.2 %shard_map.65 = (f32[3,4,48,128]{3,2,1,0:T(8,128)S(1)}, f32[3,2,48,128]{3,2,1,0:T(8,128)S(1)}, f32[3,2,48,128]{3,2,1,0:T(8,128)S(1)}) custom-call(f32[3,6,64,128]{3,2,1,0:T(8,128)S(1)} %get-tuple-element.29.omega, f32[3,4,48,128]{3,2,1,0:T(8,128)S(1)} %get-tuple-element.33.before, f32[3,2,48,128]{3,2,1,0:T(8,128)S(1)} %collective-permute-done.7.got_across, ...), custom_call_target="tpu_custom_call" | custom-call | tf_op jit(solution)/shard_map/pallas_call | solution.py:492
  51.2 2.3 %collective-permute-start.9 = (f32[3,2,48,128]{3,2,1,0:T(8,128)S(1)}, f32[3,2,48,128]{3,2,1,0:T(8,128)S(1)}, u32[]{:S(2)}, u32[]{:S(2)}) collective-permute-start(f32[3,2,48,128]{3,2,1,0:T(8,128)S(1)} %get-tuple-element.37), channel_id=1, source_target_pairs={{0,30},{2,4},{4,2},{6,8},{8,6},{10,12},{12,10},{14,16},{16,14},{18... | collective-permute-start | bytes 442376 | tf_op jit(solution)/shard_map/ppermute | solution.py:51
  53.5 0.0 collective-permute-start.10
  53.5 5.0 %collective-permute-done.9.got_across = f32[3,2,48,128]{3,2,1,0:T(8,128)S(1)} collective-permute-done((f32[3,2,48,128]{3,2,1,0:T(8,128)S(1)}, f32[3,2,48,128]{3,2,1,0:T(8,128)S(1)}, u32[]{:S(2)}, u32[]{:S(2)}) %collective-permute-start.9) | collective-permute-done | bytes 147488 | tf_op jit(solution)/shard_map/ppermute | solution.py:51
  58.5 0.0 collective-permute-done.10.got_within
  58.5 1.2 %shard_map.66 = (f32[3,4,48,128]{3,2,1,0:T(8,128)S(1)}, f32[3,2,40,128]{3,2,1,0:T(8,128)S(1)}, f32[3,2,40,128]{3,2,1,0:T(8,128)S(1)}) custom-call(f32[3,6,64,128]{3,2,1,0:T(8,128)S(1)} %get-tuple-element.29.omega, f32[3,4,48,128]{3,2,1,0:T(8,128)S(1)} %get-tuple-element.36.before, f32[3,2,48,128]{3,2,1,0:T(8,128)S(1)} %collective-permute-done.9.got_across, ...), custom_call_target="tpu_custom_call" | custom-call | tf_op jit(solution)/shard_map/pallas_call | solution.py:492
  59.7 2.3 %collective-permute-start.11 = (f32[3,2,40,128]{3,2,1,0:T(8,128)S(1)}, f32[3,2,40,128]{3,2,1,0:T(8,128)S(1)}, u32[]{:S(2)}, u32[]{:S(2)}) collective-permute-start(f32[3,2,40,128]{3,2,1,0:T(8,128)S(1)} %get-tuple-element.40), channel_id=1, source_target_pairs={{0,30},{2,4},{4,2},{6,8},{8,6},{10,12},{12,10},{14,16},{16,14},{18... | collective-permute-start | bytes 368648 | tf_op jit(solution)/shard_map/ppermute | solution.py:51
  62.1 0.0 collective-permute-start.12
  62.1 4.7 %collective-permute-done.11.got_across = f32[3,2,40,128]{3,2,1,0:T(8,128)S(1)} collective-permute-done((f32[3,2,40,128]{3,2,1,0:T(8,128)S(1)}, f32[3,2,40,128]{3,2,1,0:T(8,128)S(1)}, u32[]{:S(2)}, u32[]{:S(2)}) %collective-permute-start.11) | collective-permute-done | bytes 122912 | tf_op jit(solution)/shard_map/ppermute | solution.py:51
  66.8 0.0 collective-permute-done.12.got_within
  66.8 1.0 %shard_map.67 = (f32[3,4,32,128]{3,2,1,0:T(8,128)}, f32[3,4,32,128]{3,2,1,0:T(8,128)}) custom-call(f32[3,6,64,128]{3,2,1,0:T(8,128)S(1)} %get-tuple-element.29.omega, f32[3,4,48,128]{3,2,1,0:T(8,128)S(1)} %get-tuple-element.39.potential, f32[3,2,40,128]{3,2,1,0:T(8,128)S(1)} %collective-permute-done.11.got_across, ...), custom_call_target="tpu_custom_call" | custom-call | tf_op jit(solution)/shard_map/pallas_call | solution.py:492
Async XLA Ops:
  0.6 7.9 %copy-start = (f32[3,17408]{1,0:T(4,128)S(1)}, f32[3,17408]{1,0:T(4,128)}, u32[]{:S(2)}) copy-start(f32[3,17408]{1,0:T(4,128)} %offset_hbm.1) | copy-start | bytes 626692
  0.6 7.9 %copy-start.1 = (f32[3,17408]{1,0:T(4,128)S(1)}, f32[3,17408]{1,0:T(4,128)}, u32[]{:S(2)}) copy-start(f32[3,17408]{1,0:T(4,128)} %vort_hbm.1) | copy-start | bytes 626692
  0.6 7.9 %copy-start.2 = (s32[17408]{0:T(1024)S(1)}, s32[17408]{0:T(1024)}, u32[]{:S(2)}) copy-start(s32[17408]{0:T(1024)} %param.4) | copy-start | bytes 208900
  3.0 5.5 %copy-start.3 = (s32[1,3]{1,0:T(1,128)S(1)}, s32[1,3]{1,0:T(1,128)}, u32[]{:S(2)}) copy-start(s32[1,3]{1,0:T(1,128)} %moving.3) | copy-start | bytes 40
  3.0 14.1 %collective-permute-start = (f32[8,1024]{1,0:T(8,128)}, f32[8,1024]{1,0:T(8,128)S(1)}, u32[]{:S(2)}, u32[]{:S(2)}) collective-permute-start(f32[8,1024]{1,0:T(8,128)} %get-tuple-element.22), channel_id=1, source_target_pairs={{0,30},{2,4},{4,2},{6,8},{8,6},{10,12},{12,10},{14,16},{16,14},{18... | collective-permute-start | bytes 98312 | tf_op jit(solution)/shard_map/ppermute | solution.py:51
  8.5 8.6 %collective-permute-start.1 = (f32[8,1024]{1,0:T(8,128)}, f32[8,1024]{1,0:T(8,128)S(1)}, u32[]{:S(2)}, u32[]{:S(2)}) collective-permute-start(f32[8,1024]{1,0:T(8,128)} %get-tuple-element.23), channel_id=1, source_target_pairs={{0,2},{2,0},{4,6},{6,4},{8,10},{10,8},{12,14},{14,12},{16,18},{18,... | collective-permute-start | bytes 98312 | tf_op jit(solution)/shard_map/ppermute | solution.py:52
  18.2 7.7 %collective-permute-start.2 = (f32[3,3,40,128]{3,2,1,0:T(8,128)S(1)}, f32[3,3,40,128]{3,2,1,0:T(8,128)S(1)}, u32[]{:S(2)}, u32[]{:S(2)}) collective-permute-start(f32[3,3,40,128]{3,2,1,0:T(8,128)S(1)} %get-tuple-element.25), channel_id=1, source_target_pairs={{0,30},{2,4},{4,2},{6,8},{8,6},{10,12},{12,10},{14,16},{16,14},{18... | collective-permute-start | bytes 552968 | tf_op jit(solution)/shard_map/ppermute | solution.py:51
  19.0 6.9 %collective-permute-start.3 = (f32[3,3,40,128]{3,2,1,0:T(8,128)S(1)}, f32[3,3,40,128]{3,2,1,0:T(8,128)S(1)}, u32[]{:S(2)}, u32[]{:S(2)}) collective-permute-start(f32[3,3,40,128]{3,2,1,0:T(8,128)S(1)} %get-tuple-element.26), channel_id=1, source_target_pairs={{0,2},{2,0},{4,6},{6,4},{8,10},{10,8},{12,14},{14,12},{16,18},{18,... | collective-permute-start | bytes 552968 | tf_op jit(solution)/shard_map/ppermute | solution.py:52
  26.0 6.8 %collective-permute-start.4 = (f32[3,6,32,128]{3,2,1,0:T(8,128)S(1)}, f32[3,6,32,128]{3,2,1,0:T(8,128)S(1)}, u32[]{:S(2)}, u32[]{:S(2)}) collective-permute-start(f32[3,6,32,128]{3,2,1,0:T(8,128)S(1)} %get-tuple-element.28), channel_id=1, source_target_pairs={{0,1},{1,0},{2,3},{3,2},{4,5},{5,4},{6,7},{7,6},{8,9},{9,8},{10,11... | collective-permute-start | bytes 884744 | tf_op jit(solution)/shard_map/ppermute | solution.py:509
  33.7 7.6 %collective-permute-start.5 = (f32[3,2,56,128]{3,2,1,0:T(8,128)S(1)}, f32[3,2,56,128]{3,2,1,0:T(8,128)S(1)}, u32[]{:S(2)}, u32[]{:S(2)}) collective-permute-start(f32[3,2,56,128]{3,2,1,0:T(8,128)S(1)} %get-tuple-element.31), channel_id=1, source_target_pairs={{0,30},{2,4},{4,2},{6,8},{8,6},{10,12},{12,10},{14,16},{16,14},{18... | collective-permute-start | bytes 516104 | tf_op jit(solution)/shard_map/ppermute | solution.py:51
  36.0 5.3 %collective-permute-start.6 = (f32[3,2,56,128]{3,2,1,0:T(8,128)S(1)}, f32[3,2,56,128]{3,2,1,0:T(8,128)S(1)}, u32[]{:S(2)}, u32[]{:S(2)}) collective-permute-start(f32[3,2,56,128]{3,2,1,0:T(8,128)S(1)} %get-tuple-element.32), channel_id=1, source_target_pairs={{0,2},{2,0},{4,6},{6,4},{8,10},{10,8},{12,14},{14,12},{16,18},{18,... | collective-permute-start | bytes 516104 | tf_op jit(solution)/shard_map/ppermute | solution.py:52
  42.6 7.3 %collective-permute-start.7 = (f32[3,2,48,128]{3,2,1,0:T(8,128)S(1)}, f32[3,2,48,128]{3,2,1,0:T(8,128)S(1)}, u32[]{:S(2)}, u32[]{:S(2)}) collective-permute-start(f32[3,2,48,128]{3,2,1,0:T(8,128)S(1)} %get-tuple-element.34), channel_id=1, source_target_pairs={{0,30},{2,4},{4,2},{6,8},{8,6},{10,12},{12,10},{14,16},{16,14},{18... | collective-permute-start | bytes 442376 | tf_op jit(solution)/shard_map/ppermute | solution.py:51
  44.9 5.0 %collective-permute-start.8 = (f32[3,2,48,128]{3,2,1,0:T(8,128)S(1)}, f32[3,2,48,128]{3,2,1,0:T(8,128)S(1)}, u32[]{:S(2)}, u32[]{:S(2)}) collective-permute-start(f32[3,2,48,128]{3,2,1,0:T(8,128)S(1)} %get-tuple-element.35), channel_id=1, source_target_pairs={{0,2},{2,0},{4,6},{6,4},{8,10},{10,8},{12,14},{14,12},{16,18},{18,... | collective-permute-start | bytes 442376 | tf_op jit(solution)/shard_map/ppermute | solution.py:52
  51.2 7.3 %collective-permute-start.9 = (f32[3,2,48,128]{3,2,1,0:T(8,128)S(1)}, f32[3,2,48,128]{3,2,1,0:T(8,128)S(1)}, u32[]{:S(2)}, u32[]{:S(2)}) collective-permute-start(f32[3,2,48,128]{3,2,1,0:T(8,128)S(1)} %get-tuple-element.37), channel_id=1, source_target_pairs={{0,30},{2,4},{4,2},{6,8},{8,6},{10,12},{12,10},{14,16},{16,14},{18... | collective-permute-start | bytes 442376 | tf_op jit(solution)/shard_map/ppermute | solution.py:51
  53.5 5.0 %collective-permute-start.10 = (f32[3,2,48,128]{3,2,1,0:T(8,128)S(1)}, f32[3,2,48,128]{3,2,1,0:T(8,128)S(1)}, u32[]{:S(2)}, u32[]{:S(2)}) collective-permute-start(f32[3,2,48,128]{3,2,1,0:T(8,128)S(1)} %get-tuple-element.38), channel_id=1, source_target_pairs={{0,2},{2,0},{4,6},{6,4},{8,10},{10,8},{12,14},{14,12},{16,18},{18,... | collective-permute-start | bytes 442376 | tf_op jit(solution)/shard_map/ppermute | solution.py:52
  59.7 7.1 %collective-permute-start.11 = (f32[3,2,40,128]{3,2,1,0:T(8,128)S(1)}, f32[3,2,40,128]{3,2,1,0:T(8,128)S(1)}, u32[]{:S(2)}, u32[]{:S(2)}) collective-permute-start(f32[3,2,40,128]{3,2,1,0:T(8,128)S(1)} %get-tuple-element.40), channel_id=1, source_target_pairs={{0,30},{2,4},{4,2},{6,8},{8,6},{10,12},{12,10},{14,16},{16,14},{18... | collective-permute-start | bytes 368648 | tf_op jit(solution)/shard_map/ppermute | solution.py:51
  62.1 4.8 %collective-permute-start.12 = (f32[3,2,40,128]{3,2,1,0:T(8,128)S(1)}, f32[3,2,40,128]{3,2,1,0:T(8,128)S(1)}, u32[]{:S(2)}, u32[]{:S(2)}) collective-permute-start(f32[3,2,40,128]{3,2,1,0:T(8,128)S(1)} %get-tuple-element.41), channel_id=1, source_target_pairs={{0,2},{2,0},{4,6},{6,4},{8,10},{10,8},{12,14},{14,12},{16,18},{18,... | collective-permute-start | bytes 368648 | tf_op jit(solution)/shard_map/ppermute | solution.py:52
